TPU v7x, 32 devices: a whole 2x2x4 slice. The times are simulated.
32 devices in a mesh: strike: 16 (over z, y, x), normal: 2 (over core).
Axes of the slice: x: 2, y: 2, z: 4, core: 2. Of those that a mesh axis runs over, the one named last changes fastest.
Arguments:
- displacement: float32 [3, 512, 16, 128], P(None, 'strike', 'normal'), may hold values from -6 to 6
- velocity: float32 [3, 512, 16, 128], P(None, 'strike', 'normal'), may hold values from -6 to 6
- stiffness: float32 [512, 16, 128], P('strike', 'normal'), may hold values from 0.4 to 1.3
- yield_flags: int32 [128, 16, 32], P('strike', 'normal'), may hold values from 0 to 1
- contact: int32 [2, 512, 128], P(None, 'strike'), may hold values 0 or 1
- history: bfloat16 [2, 8, 2, 3, 128, 512], P(None, None, None, None, 'strike'), may hold values from -6 to 6
- kernel: float32 [2, 8, 3, 512], replicated, may hold values from -1.8 to 1.8
Outputs:
- final_displacement: float32 [3, 512, 16, 128], P(None, 'strike', 'normal')
- final_velocity: float32 [3, 512, 16, 128], P(None, 'strike', 'normal')
All inputs are finite; a program needn't handle non-finite values. No bound on the sum of `contact` on one device may be relied on, other than what follows from the above.
Results may differ from a plain program's by a relative error of at most 0.001.
Values may be sent and summed in bfloat16 or wider, within the bound.
No kernel may reach another device: no remote copies, remote signals or barrier semaphores. Data moves between devices by JAX's collectives and lax.ppermute only.
A program may use at most 64 MiB of HBM per device.

v0:
```python
import math

import jax
import jax.numpy as jnp
from jax import lax
from jax.sharding import PartitionSpec as P

SUB = 3
BLK = 4


time_step = 0.5


def padded(cells, sides, width, closed):
    for axis, dim in sides:
        count = lax.axis_size(axis)
        ends = count if closed else count - 1
        head = lax.slice_in_dim(cells, 0, width, axis=dim)
        tail = lax.slice_in_dim(cells, cells.shape[dim] - width, cells.shape[dim], axis=dim)
        cells = jnp.concatenate(
            [
                lax.ppermute(tail, axis, [(i, (i + 1) % count) for i in range(ends)]),
                cells,
                lax.ppermute(head, axis, [((i + 1) % count, i) for i in range(ends)]),
            ],
            axis=dim,
        )
    return cells


def phase_tables(mode_count, first_mode, block_modes):
    node_ids = jnp.arange(mode_count, dtype=jnp.int32)[:, None]
    mode_ids = (first_mode + jnp.arange(block_modes, dtype=jnp.int32))[None, :]
    phases = (node_ids * mode_ids % mode_count).astype(jnp.float32) * (2.0 * math.pi / mode_count)
    return (jnp.cos(phases).astype(jnp.bfloat16), jnp.sin(phases).astype(jnp.bfloat16))


def blocks_expand(yield_map, block_size):
    strike_blocks, normal_layers, dip_blocks = yield_map.shape
    widened = jnp.broadcast_to(
        yield_map.astype(jnp.float32)[:, None, :, :, None],
        (strike_blocks, block_size, normal_layers, dip_blocks, block_size),
    )
    return widened.reshape(strike_blocks * block_size, normal_layers, dip_blocks * block_size)


def strike_pad(values):
    return padded(values, (("strike", 1),), 1, True)


def normal_pad(values):
    return padded(values, (("normal", 2),), 1, False)


def laplace(values, strike_side, normal_side):
    dip_padded = jnp.pad(values, ((0, 0), (0, 0), (0, 0), (1, 1)))
    return (
        strike_side[:, 2:]
        + strike_side[:, :-2]
        + (normal_side[:, :, 2:] + normal_side[:, :, :-2])
        + (dip_padded[..., 2:] + dip_padded[..., :-2])
        - 6.0 * values
    )


def body(displacement, velocity, stiffness, yield_flags, contact, history, kernel):
    layer_index = lax.axis_index("normal")
    layer_count = lax.axis_size("normal")
    is_lowest = layer_index == 0
    is_highest = layer_index == layer_count - 1
    face_index = is_highest.astype(jnp.int32)
    own_layers = displacement.shape[2]
    modulus = stiffness * (1.0 - 0.5 * blocks_expand(yield_flags, BLK))
    own_history = lax.dynamic_index_in_dim(history, face_index, 0, keepdims=False)
    own_kernel = lax.dynamic_index_in_dim(kernel, face_index, 0, keepdims=False)
    touching = lax.dynamic_index_in_dim(contact, face_index, 0, keepdims=False).astype(jnp.float32)
    layer_rows = jnp.arange(own_layers)
    plane_rows = (
        (layer_rows == 0) & is_lowest | (layer_rows == own_layers - 1) & is_highest
    ).astype(jnp.float32)
    plane = jnp.where(is_highest, displacement[:, :, -1, :], displacement[:, :, 0, :])
    outgoing = jnp.swapaxes(plane, 1, 2).astype(jnp.bfloat16)
    modal = lax.all_to_all(outgoing, "strike", split_axis=1, concat_axis=2, tiled=True)
    components, dip_rows, mode_count = modal.shape
    row_count = components * dip_rows
    flat = modal.reshape(row_count, mode_count)
    block_modes = min(mode_count, 1024)
    normalizer = 1.0 / math.sqrt(mode_count)

    def one_block(summed, block_index):
        first_mode = block_index * block_modes
        cosines, sines = phase_tables(mode_count, first_mode, block_modes)
        real_part = normalizer * jnp.dot(flat, cosines, preferred_element_type=jnp.float32)
        imag_part = -(normalizer * jnp.dot(flat, sines, preferred_element_type=jnp.float32))
        current = jnp.stack([real_part, imag_part]).reshape(2, components, dip_rows, block_modes)
        older = lax.dynamic_slice_in_dim(own_history, first_mode, block_modes, 4).astype(
            jnp.float32
        )
        lagged = jnp.concatenate([current[None], older[:-1]], axis=0)
        weights = lax.dynamic_slice_in_dim(own_kernel, first_mode, block_modes, 2)[
            :, None, :, None, :
        ]
        modal_force = jnp.sum(weights * lagged, axis=0).astype(jnp.bfloat16)
        upper = modal_force[0].reshape(row_count, block_modes)
        lower = modal_force[1].reshape(row_count, block_modes)
        partial_sum = jnp.dot(upper, cosines.T, preferred_element_type=jnp.float32) - jnp.dot(
            lower, sines.T, preferred_element_type=jnp.float32
        )
        return (summed + partial_sum, None)

    summed, unused = lax.scan(
        one_block,
        jnp.zeros((row_count, mode_count), jnp.float32),
        jnp.arange(mode_count // block_modes),
    )
    traction = (normalizer * summed).reshape(components, dip_rows, mode_count)
    returned = lax.all_to_all(
        traction.astype(jnp.bfloat16), "strike", split_axis=2, concat_axis=1, tiled=True
    ).astype(traction.dtype)
    pushed = touching[None] * jnp.swapaxes(returned, 1, 2)
    force = pushed[:, :, None, :] * plane_rows[None, None, :, None]
    prepared = (strike_pad(displacement), normal_pad(displacement))
    moved = displacement
    speed = velocity
    strike_side, normal_side = prepared
    for substep in range(SUB):
        if substep > 0:
            strike_side = strike_pad(moved)
            normal_side = normal_pad(moved)
        acceleration = modulus * laplace(moved, strike_side, normal_side) + force
        speed = speed + time_step * acceleration
        moved = moved + time_step * speed
    return (moved, speed)


def solution(mesh):
    return jax.shard_map(
        body,
        mesh=mesh,
        in_specs=(
            P(None, "strike", "normal", None),
            P(None, "strike", "normal", None),
            P("strike", "normal", None),
            P("strike", "normal", None),
            P(None, "strike", None),
            P(None, None, None, None, "strike", None),
            P(),
        ),
        out_specs=(P(None, "strike", "normal", None), P(None, "strike", "normal", None)),
        check_vma=False,
    )
```

profile of v0, /device:TPU:0, one launch (start us, length us, event | category | flops | bytes accessed | tf_op | source)
XLA Modules:
  0.0 85.9 jit_solution(10015494832772093365)
XLA Ops:
  0.6 0.0 copy-start
  0.6 1.2 %fusion.67 = (f32[3,32,1,128]{3,2,1,0:T(1,128)S(1)}, f32[3,32,1,128]{3,2,1,0:T(1,128)S(1)}) fusion(f32[3,32,8,128]{3,2,1,0:T(8,128)} %param.7), kind=kLoop, calls=%fused_computation.107 | loop fusion | bytes 196608 | tf_op jit(solution)/shard_map/slice | solution.py:19
  1.9 1.3 %collective-permute-start.2 = (f32[3,32,1,128]{3,1,0,2:T(8,128)S(1)}, f32[3,32,1,128]{3,1,0,2:T(8,128)S(1)}, u32[]{:S(2)}, u32[]{:S(2)}) collective-permute-start(f32[3,32,1,128]{3,1,0,2:T(8,128)S(1)} %bitcast.57), channel_id=1, source_target_pairs={{1,0},{3,2},{5,4},{7,6},{9,8},{11,10},{13,12},{15,14},{17,16},{19,... | collective-permute-start | bytes 147464 | tf_op jit(solution)/shard_map/ppermute | solution.py:25
  3.2 3.0 %collective-permute-start.3 = (f32[3,32,1,128]{3,1,0,2:T(8,128)S(1)}, f32[3,32,1,128]{3,1,0,2:T(8,128)S(1)}, u32[]{:S(2)}, u32[]{:S(2)}) collective-permute-start(f32[3,32,1,128]{3,1,0,2:T(8,128)S(1)} %bitcast.55), channel_id=1, source_target_pairs={{0,1},{2,3},{4,5},{6,7},{8,9},{10,11},{12,13},{14,15},{16,17},{18,... | collective-permute-start | bytes 147464 | tf_op jit(solution)/shard_map/ppermute | solution.py:23
  6.2 0.1 copy.59
  6.4 0.7 reshape.51
  7.1 8.3 %all-to-all-start = ((bf16[16,2,384]{2,1,0:T(2,128)(2,1)}), bf16[16,2,384]{2,1,0:T(2,128)(2,1)S(1)}, u32[]{:S(2)}, u32[]{:S(2)}) async-start(bf16[16,2,384]{2,1,0:T(2,128)(2,1)} %reshape.51), calls=%async_computation | async-start | bytes 49152 | tf_op jit(solution)/shard_map/all_to_all | solution.py:84
  15.4 1.3 %fusion.66 = (f32[3,1,8,128]{3,2,1,0:T(8,128)}, f32[3,1,8,128]{3,2,1,0:T(8,128)}) fusion(f32[3,32,8,128]{3,2,1,0:T(8,128)} %param.7), kind=kLoop, calls=%fused_computation.106 | loop fusion | bytes 49152 | tf_op jit(solution)/shard_map/slice | solution.py:19
  16.8 5.5 %collective-permute-start = (f32[3,1,8,128]{3,2,1,0:T(8,128)}, f32[3,1,8,128]{3,2,1,0:T(8,128)S(1)}, u32[]{:S(2)}, u32[]{:S(2)}) collective-permute-start(f32[3,1,8,128]{3,2,1,0:T(8,128)} %get-tuple-element.31), channel_id=1, source_target_pairs={{2,0},{4,2},{6,4},{8,6},{10,8},{12,10},{14,12},{16,14},{18,16},{20... | collective-permute-start | bytes 36872 | tf_op jit(solution)/shard_map/ppermute | solution.py:25
  22.3 0.0 collective-permute-start.1
  22.3 1.0 %fusion.41 = f32[7,2,3,8,512]{4,3,2,1,0:T(8,128)S(1)} fusion(bf16[2,8,2,3,8,512]{5,4,3,2,1,0:T(8,128)(2,1)} %param.12, s32[]{:T(128)S(6)} %select_n.35), kind=kLoop, calls=%fused_computation.75 | loop fusion | flops 172032 | bytes 1032196 | tf_op jit(solution)/shard_map/while/body/eval_jaxpr/slice | solution.py:100
  23.3 0.0 copy-done
  23.4 0.8 multiply_subtract_fusion
  24.1 0.7 convert_bitcast_fusion
  24.9 0.0 all-to-all-done
  24.9 0.1 reshape.52
  25.1 0.1 reshape.47
  25.2 4.4 %fusion.1 = f32[1,1,3,8,512]{4,3,2,1,0:T(8,128)S(1)} fusion(bf16[24,512]{1,0:T(8,128)(2,1)S(1)} %reshape.47), kind=kOutput, calls=%fused_computation.6 | convolution fusion | flops 16539648 | bytes 73728 | tf_op jit(solution)/shard_map/while/body/eval_jaxpr/dot_general | solution.py:95
  29.7 4.4 %fusion.2 = f32[1,1,3,8,512]{4,3,2,1,0:T(8,128)S(1)} fusion(bf16[24,512]{1,0:T(8,128)(2,1)S(1)} %reshape.47), kind=kOutput, calls=%fused_computation.8 | convolution fusion | flops 16527360 | bytes 73728 | tf_op jit(solution)/shard_map/while/body/eval_jaxpr/dot_general | solution.py:94
  34.1 0.1 fusion.12
  34.2 4.1 %fusion.13 = f32[24,512]{1,0:T(8,128)S(1)} fusion(bf16[2,3,8,512]{3,2,1,0:T(8,128)(2,1)S(1)} %fusion.12), kind=kOutput, calls=%fused_computation.31 | convolution fusion | flops 16515072 | bytes 73728 | tf_op jit(solution)/shard_map/while/body/eval_jaxpr/dot_general | solution.py:107
  38.3 4.4 %fusion.5 = bf16[3,8,512]{2,1,0:T(8,128)(2,1)S(1)} fusion(f32[24,512]{1,0:T(8,128)S(1)} %fusion.13, bf16[2,3,8,512]{3,2,1,0:T(8,128)(2,1)S(1)} %fusion.12), kind=kOutput, calls=%fused_computation.11 | convolution fusion | flops 16551936 | bytes 98304 | tf_op jit(solution)/shard_map/while/body/eval_jaxpr/dot_general | solution.py:107
  42.7 0.3 copy.62
  43.0 1.1 %reshape.53 = bf16[16,2,384]{2,1,0:T(2,128)(2,1)} reshape(bf16[512,3,8]{2,1,0:T(4,128)(2,1)S(1)} %bitcast.49) | data formatting | bytes 49152
  44.1 7.0 %all-to-all-start.1 = ((bf16[16,2,384]{2,1,0:T(2,128)(2,1)}), bf16[16,2,384]{2,1,0:T(2,128)(2,1)S(1)}, u32[]{:S(2)}, u32[]{:S(2)}) async-start(bf16[16,2,384]{2,1,0:T(2,128)(2,1)} %reshape.53), calls=%async_computation.1 | async-start | bytes 49152 | tf_op jit(solution)/shard_map/all_to_all | solution.py:118
  51.1 0.6 or_convert_fusion
  51.7 0.1 copy.57
  51.8 0.1 copy.51
  51.9 0.0 copy-start.3
  51.9 0.5 broadcast_in_dim.5
  52.4 0.0 copy-start.1
  52.4 0.0 copy-start.2
  52.4 0.6 copy.52
  53.0 5.5 %all-to-all-done.1 = bf16[16,2,384]{2,1,0:T(2,128)(2,1)S(1)} async-done(((bf16[16,2,384]{2,1,0:T(2,128)(2,1)}), bf16[16,2,384]{2,1,0:T(2,128)(2,1)S(1)}, u32[]{:S(2)}, u32[]{:S(2)}) %all-to-all-start.1) | async-done | bytes 24608 | tf_op jit(solution)/shard_map/all_to_all | solution.py:118
  58.5 0.5 reshape.54
  58.9 0.2 copy.63
  59.2 0.1 reshape.50
  59.3 0.1 bitcast_multiply_fusion
  59.4 0.1 copy.65
  59.5 0.0 collective-permute-done
  59.5 0.0 collective-permute-done.1
  59.5 0.0 collective-permute-done.2
  59.5 0.0 collective-permute-done.3
  59.5 0.4 multiply_add_fusion.5
  59.9 0.1 fusion.65
  60.0 1.3 %collective-permute-start.6 = (f32[3,32,1,128]{3,2,1,0:T(1,128)S(1)}, f32[3,32,1,128]{3,2,1,0:T(1,128)S(1)}, u32[]{:S(2)}, u32[]{:S(2)}) collective-permute-start(f32[3,32,1,128]{3,2,1,0:T(1,128)S(1)} %get-tuple-element.29), channel_id=1, source_target_pairs={{1,0},{3,2},{5,4},{7,6},{9,8},{11,10},{13,12},{15,14},{17,16},{19,... | collective-permute-start | bytes 147464 | tf_op jit(solution)/shard_map/ppermute | solution.py:25
  61.3 3.0 %collective-permute-start.7 = (f32[3,32,1,128]{3,2,1,0:T(1,128)S(1)}, f32[3,32,1,128]{3,2,1,0:T(1,128)S(1)}, u32[]{:S(2)}, u32[]{:S(2)}) collective-permute-start(f32[3,32,1,128]{3,2,1,0:T(1,128)S(1)} %get-tuple-element.30), channel_id=1, source_target_pairs={{0,1},{2,3},{4,5},{6,7},{8,9},{10,11},{12,13},{14,15},{16,17},{18,... | collective-permute-start | bytes 147464 | tf_op jit(solution)/shard_map/ppermute | solution.py:23
  64.3 0.8 collective-permute-start.4
  65.1 1.3 %collective-permute-start.5 = (f32[3,1,8,128]{3,2,1,0:T(8,128)S(1)}, f32[3,1,8,128]{3,2,1,0:T(8,128)S(1)}, u32[]{:S(2)}, u32[]{:S(2)}) collective-permute-start(f32[3,1,8,128]{3,2,1,0:T(8,128)S(1)} %get-tuple-element.28), channel_id=1, source_target_pairs={{0,2},{2,4},{4,6},{6,8},{8,10},{10,12},{12,14},{14,16},{16,18},{18... | collective-permute-start | bytes 36872 | tf_op jit(solution)/shard_map/ppermute | solution.py:23
  66.4 1.7 %collective-permute-done.4 = f32[3,1,8,128]{3,2,1,0:T(8,128)S(1)} collective-permute-done((f32[3,1,8,128]{3,2,1,0:T(8,128)S(1)}, f32[3,1,8,128]{3,2,1,0:T(8,128)S(1)}, u32[]{:S(2)}, u32[]{:S(2)}) %collective-permute-start.4) | collective-permute-done | bytes 12320 | tf_op jit(solution)/shard_map/ppermute | solution.py:25
  68.1 4.3 %collective-permute-done.5 = f32[3,1,8,128]{3,2,1,0:T(8,128)S(1)} collective-permute-done((f32[3,1,8,128]{3,2,1,0:T(8,128)S(1)}, f32[3,1,8,128]{3,2,1,0:T(8,128)S(1)}, u32[]{:S(2)}, u32[]{:S(2)}) %collective-permute-start.5) | collective-permute-done | bytes 12320 | tf_op jit(solution)/shard_map/ppermute | solution.py:23
  72.4 0.0 collective-permute-done.6
  72.4 0.0 collective-permute-done.7
  72.4 0.4 multiply_add_fusion.4
  72.8 0.1 fusion.63
  72.9 1.3 %collective-permute-start.10 = (f32[3,32,1,128]{3,2,1,0:T(1,128)S(1)}, f32[3,32,1,128]{3,2,1,0:T(1,128)S(1)}, u32[]{:S(2)}, u32[]{:S(2)}) collective-permute-start(f32[3,32,1,128]{3,2,1,0:T(1,128)S(1)} %get-tuple-element.25), channel_id=1, source_target_pairs={{1,0},{3,2},{5,4},{7,6},{9,8},{11,10},{13,12},{15,14},{17,16},{19,... | collective-permute-start | bytes 147464 | tf_op jit(solution)/shard_map/ppermute | solution.py:25
  74.2 3.0 %collective-permute-start.11 = (f32[3,32,1,128]{3,2,1,0:T(1,128)S(1)}, f32[3,32,1,128]{3,2,1,0:T(1,128)S(1)}, u32[]{:S(2)}, u32[]{:S(2)}) collective-permute-start(f32[3,32,1,128]{3,2,1,0:T(1,128)S(1)} %get-tuple-element.26), channel_id=1, source_target_pairs={{0,1},{2,3},{4,5},{6,7},{8,9},{10,11},{12,13},{14,15},{16,17},{18,... | collective-permute-start | bytes 147464 | tf_op jit(solution)/shard_map/ppermute | solution.py:23
  77.2 0.1 collective-permute-start.8
  77.3 2.0 %collective-permute-start.9 = (f32[3,1,8,128]{3,2,1,0:T(8,128)S(1)}, f32[3,1,8,128]{3,2,1,0:T(8,128)S(1)}, u32[]{:S(2)}, u32[]{:S(2)}) collective-permute-start(f32[3,1,8,128]{3,2,1,0:T(8,128)S(1)} %get-tuple-element.24), channel_id=1, source_target_pairs={{0,2},{2,4},{4,6},{6,8},{8,10},{10,12},{12,14},{14,16},{16,18},{18... | collective-permute-start | bytes 36872 | tf_op jit(solution)/shard_map/ppermute | solution.py:23
  79.3 1.7 %collective-permute-done.8 = f32[3,1,8,128]{3,2,1,0:T(8,128)S(1)} collective-permute-done((f32[3,1,8,128]{3,2,1,0:T(8,128)S(1)}, f32[3,1,8,128]{3,2,1,0:T(8,128)S(1)}, u32[]{:S(2)}, u32[]{:S(2)}) %collective-permute-start.8) | collective-permute-done | bytes 12320 | tf_op jit(solution)/shard_map/ppermute | solution.py:25
  81.0 3.7 %collective-permute-done.9 = f32[3,1,8,128]{3,2,1,0:T(8,128)S(1)} collective-permute-done((f32[3,1,8,128]{3,2,1,0:T(8,128)S(1)}, f32[3,1,8,128]{3,2,1,0:T(8,128)S(1)}, u32[]{:S(2)}, u32[]{:S(2)}) %collective-permute-start.9) | collective-permute-done | bytes 12320 | tf_op jit(solution)/shard_map/ppermute | solution.py:23
  84.6 0.0 collective-permute-done.10
  84.6 0.0 collective-permute-done.11
  84.6 1.3 %multiply_add_fusion.3 = (f32[3,32,8,128]{3,2,1,0:T(8,128)}, f32[3,32,8,128]{3,2,1,0:T(8,128)}) fusion(f32[3,32,8,128]{3,2,1,0:T(8,128)S(1)} %get-tuple-element.14, f32[3,32,8,128]{3,2,1,0:T(8,128)S(1)} %get-tuple-element.20, f32[8]{0:T(128)S(1)} %copy-done.4, f32[3,32,128]{2,1,0:T(8,128)S(1)} %copy.65, f32[3,32,1,128]{3,2,1,0:T(1,128)S(1)} %collective-permute-done.11, ...), kind=kLoop, calls=%fused_computation.71 | loop fusion | flops 1769472 | bytes 1876000 | tf_op jit(solution)/shard_map/add | solution.py:133
  (13 shorter events, 0.1 us)
Async XLA Ops:
  0.6 22.7 %copy-start = (f32[2,8,3,512]{3,1,2,0:T(8,128)S(1)}, f32[2,8,3,512]{3,1,2,0:T(8,128)}, u32[]{:S(2)}) copy-start(f32[2,8,3,512]{3,1,2,0:T(8,128)} %param.13) | copy-start | bytes 294916
  1.9 57.6 %collective-permute-start.2 = (f32[3,32,1,128]{3,1,0,2:T(8,128)S(1)}, f32[3,32,1,128]{3,1,0,2:T(8,128)S(1)}, u32[]{:S(2)}, u32[]{:S(2)}) collective-permute-start(f32[3,32,1,128]{3,1,0,2:T(8,128)S(1)} %bitcast.57), channel_id=1, source_target_pairs={{1,0},{3,2},{5,4},{7,6},{9,8},{11,10},{13,12},{15,14},{17,16},{19,... | collective-permute-start | bytes 147464 | tf_op jit(solution)/shard_map/ppermute | solution.py:25
  3.2 56.3 %collective-permute-start.3 = (f32[3,32,1,128]{3,1,0,2:T(8,128)S(1)}, f32[3,32,1,128]{3,1,0,2:T(8,128)S(1)}, u32[]{:S(2)}, u32[]{:S(2)}) collective-permute-start(f32[3,32,1,128]{3,1,0,2:T(8,128)S(1)} %bitcast.55), channel_id=1, source_target_pairs={{0,1},{2,3},{4,5},{6,7},{8,9},{10,11},{12,13},{14,15},{16,17},{18,... | collective-permute-start | bytes 147464 | tf_op jit(solution)/shard_map/ppermute | solution.py:23
  7.1 17.8 %all-to-all-start = ((bf16[16,2,384]{2,1,0:T(2,128)(2,1)}), bf16[16,2,384]{2,1,0:T(2,128)(2,1)S(1)}, u32[]{:S(2)}, u32[]{:S(2)}) async-start(bf16[16,2,384]{2,1,0:T(2,128)(2,1)} %reshape.51), calls=%async_computation | async-start | bytes 49152 | tf_op jit(solution)/shard_map/all_to_all | solution.py:84
  16.8 42.7 %collective-permute-start = (f32[3,1,8,128]{3,2,1,0:T(8,128)}, f32[3,1,8,128]{3,2,1,0:T(8,128)S(1)}, u32[]{:S(2)}, u32[]{:S(2)}) collective-permute-start(f32[3,1,8,128]{3,2,1,0:T(8,128)} %get-tuple-element.31), channel_id=1, source_target_pairs={{2,0},{4,2},{6,4},{8,6},{10,8},{12,10},{14,12},{16,14},{18,16},{20... | collective-permute-start | bytes 36872 | tf_op jit(solution)/shard_map/ppermute | solution.py:25
  22.3 37.2 %collective-permute-start.1 = (f32[3,1,8,128]{3,2,1,0:T(8,128)}, f32[3,1,8,128]{3,2,1,0:T(8,128)S(1)}, u32[]{:S(2)}, u32[]{:S(2)}) collective-permute-start(f32[3,1,8,128]{3,2,1,0:T(8,128)} %get-tuple-element.32), channel_id=1, source_target_pairs={{0,2},{2,4},{4,6},{6,8},{8,10},{10,12},{12,14},{14,16},{16,18},{18... | collective-permute-start | bytes 36872 | tf_op jit(solution)/shard_map/ppermute | solution.py:23
  44.1 14.4 %all-to-all-start.1 = ((bf16[16,2,384]{2,1,0:T(2,128)(2,1)}), bf16[16,2,384]{2,1,0:T(2,128)(2,1)S(1)}, u32[]{:S(2)}, u32[]{:S(2)}) async-start(bf16[16,2,384]{2,1,0:T(2,128)(2,1)} %reshape.53), calls=%async_computation.1 | async-start | bytes 49152 | tf_op jit(solution)/shard_map/all_to_all | solution.py:118
  51.9 1.1 %copy-start.3 = (f32[32,8,128]{2,1,0:T(8,128)S(1)}, f32[32,8,128]{2,1,0:T(8,128)}, u32[]{:S(2)}) copy-start(f32[32,8,128]{2,1,0:T(8,128)} %param.9) | copy-start | bytes 393220
  52.4 7.2 %copy-start.1 = (f32[3,32,8,128]{3,2,1,0:T(8,128)S(1)}, f32[3,32,8,128]{3,2,1,0:T(8,128)}, u32[]{:S(2)}) copy-start(f32[3,32,8,128]{3,2,1,0:T(8,128)} %param.7) | copy-start | bytes 1179652
  52.4 7.2 %copy-start.2 = (f32[3,32,8,128]{3,2,1,0:T(8,128)S(1)}, f32[3,32,8,128]{3,2,1,0:T(8,128)}, u32[]{:S(2)}) copy-start(f32[3,32,8,128]{3,2,1,0:T(8,128)} %param.8) | copy-start | bytes 1179652
  52.9 6.6 %copy-start.4 = (f32[8]{0:T(128)S(1)}, f32[8]{0:T(128)}, u32[]{:S(2)}) copy-start(f32[8]{0:T(128)} %or_convert_fusion) | copy-start | bytes 100
  60.0 12.4 %collective-permute-start.6 = (f32[3,32,1,128]{3,2,1,0:T(1,128)S(1)}, f32[3,32,1,128]{3,2,1,0:T(1,128)S(1)}, u32[]{:S(2)}, u32[]{:S(2)}) collective-permute-start(f32[3,32,1,128]{3,2,1,0:T(1,128)S(1)} %get-tuple-element.29), channel_id=1, source_target_pairs={{1,0},{3,2},{5,4},{7,6},{9,8},{11,10},{13,12},{15,14},{17,16},{19,... | collective-permute-start | bytes 147464 | tf_op jit(solution)/shard_map/ppermute | solution.py:25
  61.3 11.1 %collective-permute-start.7 = (f32[3,32,1,128]{3,2,1,0:T(1,128)S(1)}, f32[3,32,1,128]{3,2,1,0:T(1,128)S(1)}, u32[]{:S(2)}, u32[]{:S(2)}) collective-permute-start(f32[3,32,1,128]{3,2,1,0:T(1,128)S(1)} %get-tuple-element.30), channel_id=1, source_target_pairs={{0,1},{2,3},{4,5},{6,7},{8,9},{10,11},{12,13},{14,15},{16,17},{18,... | collective-permute-start | bytes 147464 | tf_op jit(solution)/shard_map/ppermute | solution.py:23
  64.3 3.7 %collective-permute-start.4 = (f32[3,1,8,128]{3,2,1,0:T(8,128)S(1)}, f32[3,1,8,128]{3,2,1,0:T(8,128)S(1)}, u32[]{:S(2)}, u32[]{:S(2)}) collective-permute-start(f32[3,1,8,128]{3,2,1,0:T(8,128)S(1)} %get-tuple-element.27), channel_id=1, source_target_pairs={{2,0},{4,2},{6,4},{8,6},{10,8},{12,10},{14,12},{16,14},{18,16},{20... | collective-permute-start | bytes 36872 | tf_op jit(solution)/shard_map/ppermute | solution.py:25
  65.1 7.3 %collective-permute-start.5 = (f32[3,1,8,128]{3,2,1,0:T(8,128)S(1)}, f32[3,1,8,128]{3,2,1,0:T(8,128)S(1)}, u32[]{:S(2)}, u32[]{:S(2)}) collective-permute-start(f32[3,1,8,128]{3,2,1,0:T(8,128)S(1)} %get-tuple-element.28), channel_id=1, source_target_pairs={{0,2},{2,4},{4,6},{6,8},{8,10},{10,12},{12,14},{14,16},{16,18},{18... | collective-permute-start | bytes 36872 | tf_op jit(solution)/shard_map/ppermute | solution.py:23
  72.9 11.8 %collective-permute-start.10 = (f32[3,32,1,128]{3,2,1,0:T(1,128)S(1)}, f32[3,32,1,128]{3,2,1,0:T(1,128)S(1)}, u32[]{:S(2)}, u32[]{:S(2)}) collective-permute-start(f32[3,32,1,128]{3,2,1,0:T(1,128)S(1)} %get-tuple-element.25), channel_id=1, source_target_pairs={{1,0},{3,2},{5,4},{7,6},{9,8},{11,10},{13,12},{15,14},{17,16},{19,... | collective-permute-start | bytes 147464 | tf_op jit(solution)/shard_map/ppermute | solution.py:25
  74.2 10.5 %collective-permute-start.11 = (f32[3,32,1,128]{3,2,1,0:T(1,128)S(1)}, f32[3,32,1,128]{3,2,1,0:T(1,128)S(1)}, u32[]{:S(2)}, u32[]{:S(2)}) collective-permute-start(f32[3,32,1,128]{3,2,1,0:T(1,128)S(1)} %get-tuple-element.26), channel_id=1, source_target_pairs={{0,1},{2,3},{4,5},{6,7},{8,9},{10,11},{12,13},{14,15},{16,17},{18,... | collective-permute-start | bytes 147464 | tf_op jit(solution)/shard_map/ppermute | solution.py:23
  77.2 3.7 %collective-permute-start.8 = (f32[3,1,8,128]{3,2,1,0:T(8,128)S(1)}, f32[3,1,8,128]{3,2,1,0:T(8,128)S(1)}, u32[]{:S(2)}, u32[]{:S(2)}) collective-permute-start(f32[3,1,8,128]{3,2,1,0:T(8,128)S(1)} %get-tuple-element.23), channel_id=1, source_target_pairs={{2,0},{4,2},{6,4},{8,6},{10,8},{12,10},{14,12},{16,14},{18,16},{20... | collective-permute-start | bytes 36872 | tf_op jit(solution)/shard_map/ppermute | solution.py:25
  77.3 7.3 %collective-permute-start.9 = (f32[3,1,8,128]{3,2,1,0:T(8,128)S(1)}, f32[3,1,8,128]{3,2,1,0:T(8,128)S(1)}, u32[]{:S(2)}, u32[]{:S(2)}) collective-permute-start(f32[3,1,8,128]{3,2,1,0:T(8,128)S(1)} %get-tuple-element.24), channel_id=1, source_target_pairs={{0,2},{2,4},{4,6},{6,8},{8,10},{10,12},{12,14},{14,16},{16,18},{18... | collective-permute-start | bytes 36872 | tf_op jit(solution)/shard_map/ppermute | solution.py:23
where the time goes:
time: 86.4 us; the launch traced here: 85.9 us
  starting transfers between devices  38 us (44%)
  matrix products  17.3 us (20%)
  waiting for transfers between devices  16.8 us (19%)
  local copies, waits for them, and re-layouts  7.48 us (9%)
  other arithmetic  5.33 us (6%)
  between operations  0.97 us (1%)
    ppermute x6, starting transfers between devices, padded(): lax.ppermute(tail, axis, [(i, (i + 1) % count) for i in range(ends)])  12.4 us
    ppermute x6, starting transfers between devices, padded(): lax.ppermute(head, axis, [((i + 1) % count, i) for i in range(ends)])  10.2 us
    all_to_all x1, starting transfers between devices, body(): lax.all_to_all(outgoing, 'strike', split_axis=1, concat_axis=2, tiled=True)  8.31 us
    ppermute x6, waiting for transfers between devices, padded(): lax.ppermute(tail, axis, [(i, (i + 1) % count) for i in range(ends)])  7.98 us
    all_to_all x1, starting transfers between devices, body(): lax.all_to_all(traction.astype(jnp.bfloat16), 'strike', split_axis=2, con...  7 us
    all_to_all x1, waiting for transfers between devices, body(): lax.all_to_all(traction.astype(jnp.bfloat16), 'strike', split_axis=2, con...  5.48 us
    dot_general x1, matrix products, one_block(): jnp.dot(flat, sines, preferred_element_type=jnp.float32)  4.43 us
    dot_general x1, matrix products, one_block(): jnp.dot(flat, cosines, preferred_element_type=jnp.float32)  4.4 us
  transfers between devices with their start and end apart: 14, of which 5 were waited for; matrix products, arithmetic and copies ran while one was open for 31% of the time, Pallas kernels for 0%

commit v1 on v0

v1 whole, which is shorter than its diff:
```python
import functools
import math

import jax
import jax.numpy as jnp
import numpy as np
from jax import lax
from jax.experimental import pallas as pl
from jax.experimental.pallas import tpu as pltpu
from jax.sharding import PartitionSpec as P

SUB = 3
BLK = 4
WIN = 4
EDGE = 8
PAD = 4
LANES = 128

time_step = 0.5

f32 = jnp.float32
bf16 = jnp.bfloat16
ANY = pl.BlockSpec(memory_space=pl.ANY)
VMEM = pl.BlockSpec(memory_space=pltpu.VMEM)


def round_up(value, step):
    return -(-value // step) * step


def phase_quarter(mode_count):
    phase = np.outer(np.arange(mode_count), np.arange(mode_count // 4)) % mode_count
    phase = phase * (2.0 * np.pi / mode_count)
    return np.concatenate([np.cos(phase), -np.sin(phase)]).astype(np.float32).astype(bf16)


class Sizes:
    def __init__(self, mesh, displacement, history):
        self.strike = mesh.shape["strike"]
        self.normal = mesh.shape["normal"]
        self.parts, self.nodes, self.layers, self.dips = displacement.shape
        self.lags = history.shape[1]
        self.rows = history.shape[4]
        self.modes = history.shape[5]
        self.chunks = self.modes // LANES
        self.spectral = round_up(self.parts * self.rows, 8)
        self.chunk_rows = round_up(self.spectral + 2 * self.parts, 16)
        self.plane_rows = self.parts * self.nodes
        self.common = self.plane_rows + self.chunks * self.chunk_rows
        self.halo_u = self.common
        self.halo_v = self.halo_u + self.parts * 3 * 2 * self.layers
        self.halo_m = self.halo_v + self.parts * 2 * self.layers
        self.halo_c = self.halo_m + 2 * self.layers
        self.whole = self.halo_c + 16
        self.block = self.nodes + 2 * EDGE
        self.targets = self.strike // WIN
        self.span = self.nodes + 2 * PAD
        self.stride = self.nodes * self.layers
        self.two_sided = self.normal > 2


def widen_flags(flags, dips):
    blocks = flags.shape[1]
    block_id = lax.broadcasted_iota(jnp.int32, (blocks, dips), 0)
    dip_id = lax.broadcasted_iota(jnp.int32, (blocks, dips), 1)
    spread = (dip_id // BLK == block_id).astype(bf16)
    wide = jnp.dot(flags.astype(f32).astype(bf16), spread, preferred_element_type=f32)
    return 1.0 - 0.5 * wide


def prep_kernel(z, u_hbm, v_hbm, s_hbm, y_hbm, c_hbm, h_hbm, k_hbm, t_hbm,
                right_ref, left_ref, far_ref, g_ref,
                u_ref, v_ref, s_ref, y_ref, c_ref, h_ref, k_ref, t_ref, re_ref, im_ref, sems):
    is_high = lax.axis_index("normal") == z.normal - 1
    face = is_high.astype(jnp.int32)
    last = z.nodes - 2
    pairs = [
        (h_hbm.at[face, pl.ds(0, z.lags - 1)], h_ref),
        (k_hbm.at[face], k_ref),
        (t_hbm, t_ref),
        (u_hbm, u_ref),
        (v_hbm.at[:, pl.ds(0, 2)], v_ref.at[0]),
        (v_hbm.at[:, pl.ds(last, 2)], v_ref.at[1]),
        (s_hbm.at[pl.ds(0, 2)], s_ref.at[0]),
        (s_hbm.at[pl.ds(last, 2)], s_ref.at[1]),
        (y_hbm, y_ref),
        (c_hbm.at[face], c_ref),
    ]
    copies = [pltpu.make_async_copy(a, b, sems.at[i]) for i, (a, b) in enumerate(pairs)]
    for copy in copies:
        copy.start()
    re_ref[...] = jnp.zeros_like(re_ref)
    im_ref[...] = jnp.zeros_like(im_ref)
    copies[0].wait()
    copies[1].wait()
    for c in range(z.parts):
        for q, dst in ((0, re_ref), (1, im_ref)):
            total = None
            for lag in range(1, z.lags):
                term = k_ref[lag, pl.ds(c, 1), :] * h_ref[lag - 1, q, c].astype(f32)
                total = term if total is None else total + term
            dst[pl.ds(c * z.rows, z.rows), :] = total
        newest = k_ref[0, pl.ds(c, 1), :]
        high = newest.astype(bf16).astype(f32)
        re_ref[pl.ds(z.spectral + c, 1), :] = high
        re_ref[pl.ds(z.spectral + z.parts + c, 1), :] = newest - high
    re, im = re_ref[...], im_ref[...]
    quarter = lax.broadcasted_iota(jnp.int32, (1, z.modes), 1) % 4
    one = (quarter == 0).astype(f32) - (quarter == 2).astype(f32)
    two = (quarter == 1).astype(f32) - (quarter == 3).astype(f32)
    flip = 1.0 - 2.0 * (quarter % 2).astype(f32)
    turned = jnp.concatenate(
        [
            jnp.concatenate([re, im], axis=1),
            jnp.concatenate([re * one - im * two, re * two + im * one], axis=1),
            jnp.concatenate([re * flip, im * flip], axis=1),
            jnp.concatenate([re * one + im * two, im * one - re * two], axis=1),
        ],
        axis=0,
    ).astype(bf16)
    copies[2].wait()
    lines = jnp.dot(turned, t_ref[...], preferred_element_type=f32) * (1.0 / math.sqrt(z.modes))
    per_quarter = z.chunks // 4
    for m in range(4):
        for q in range(per_quarter):
            piece = lines[m * z.chunk_rows:(m + 1) * z.chunk_rows, q * LANES:(q + 1) * LANES]
            chunk = m * per_quarter + q
            at = pl.ds(z.plane_rows + chunk * z.chunk_rows, z.chunk_rows)
            for ref in (right_ref, left_ref, far_ref):
                ref[at, :] = piece.astype(bf16)
            g_ref[chunk] = piece[z.spectral:z.spectral + 8]
    for copy in copies[3:]:
        copy.wait()
    layer = face * (z.layers - 1)
    for c in range(z.parts):
        plane = u_ref[pl.ds(c * z.stride + layer, z.nodes, stride=z.layers), :].astype(bf16)
        for ref in (right_ref, left_ref, far_ref):
            ref[pl.ds(c * z.nodes, z.nodes), :] = plane
    soft = widen_flags(y_ref[...], z.dips)
    for ref, side, first in ((left_ref, 0, 0), (right_ref, 1, z.nodes - 3)):
        for c in range(z.parts):
            for j in range(3):
                tile = u_ref[pl.ds(c * z.stride + (first + j) * z.layers, z.layers), :]
                high = tile.astype(bf16).astype(f32)
                both = jnp.concatenate([high, tile - high], axis=0).astype(bf16)
                ref[pl.ds(z.halo_u + (c * 3 + j) * 2 * z.layers, 2 * z.layers), :] = both
            both = jnp.concatenate([v_ref[side, c, 0], v_ref[side, c, 1]], axis=0).astype(bf16)
            ref[pl.ds(z.halo_v + c * 2 * z.layers, 2 * z.layers), :] = both
        start = 0 if side == 0 else soft.shape[0] - z.layers
        part = soft[start:start + z.layers]
        both = jnp.concatenate([s_ref[side, 0] * part, s_ref[side, 1] * part], axis=0)
        ref[pl.ds(z.halo_m, 2 * z.layers), :] = both.astype(bf16)
        start = 0 if side == 0 else z.nodes - 16
        ref[pl.ds(z.halo_c, 16), :] = c_ref[pl.ds(start, 16), :].astype(f32).astype(bf16)


def toeplitz_kernel(z, g_ref, out_ref):
    for c in range(z.parts):
        line = jnp.concatenate(
            [
                g_ref[j, pl.ds(c, 1), :] + g_ref[j, pl.ds(z.parts + c, 1), :]
                for j in range(z.chunks)
            ],
            axis=1,
        ) * (1.0 / math.sqrt(z.modes))
        shift = 2 * z.nodes - EDGE
        wide = pltpu.roll(
            jnp.broadcast_to(line, (z.block, z.modes)), shift, 1, stride=1, stride_axis=0
        )
        for s in range(z.targets):
            j = (-s * WIN * z.nodes // LANES) % z.chunks
            out_ref[c, pl.ds(s * z.block, z.block), :] = wide[:, j * LANES:(j + 1) * LANES].astype(bf16)


def middle_kernel(z, toeplitz_ref, far_ref, left_ref, own_ref, right_ref, mine_ref, *out_refs):
    me = lax.axis_index("strike")
    window = (far_ref, left_ref, own_ref, right_ref)
    total = z.targets * z.block
    lines = jnp.concatenate(
        [
            jnp.concatenate(
                [ref[pl.ds(z.plane_rows + j * z.chunk_rows, z.chunk_rows), :] for ref in window],
                axis=0,
            )
            for j in range(z.chunks)
        ],
        axis=1,
    )
    row = lax.broadcasted_iota(jnp.int32, (z.block, z.modes), 0)
    node = lax.broadcasted_iota(jnp.int32, (z.block, z.modes), 1)
    wanted = []
    for s in range(z.targets):
        start = (me + WIN * s) * z.nodes - EDGE + z.modes
        wanted.append((node == (row + start) % z.modes).astype(f32).astype(bf16))
    picked = lax.dot_general(
        jnp.concatenate(wanted, axis=0), lines, (((1,), (1,)), ((), ())), preferred_element_type=f32
    ).astype(bf16)
    row = lax.broadcasted_iota(jnp.int32, (z.chunk_rows, z.dips), 0)
    dip = lax.broadcasted_iota(jnp.int32, (z.chunk_rows, z.dips), 1)
    for c in range(z.parts):
        inside = (row >= c * z.rows) & (row < (c + 1) * z.rows)
        stack = [ref[pl.ds(c * z.nodes, z.nodes), :] for ref in window]
        for w in range(WIN):
            first = z.rows * ((me + w - 2 + z.strike) % z.strike)
            place = inside & (dip - first == row - c * z.rows)
            stack.append(place.astype(f32).astype(bf16))
        factors = jnp.concatenate([toeplitz_ref[c], picked], axis=1)
        part = jnp.dot(factors, jnp.concatenate(stack, axis=0), preferred_element_type=f32)
        at = pl.ds(c * z.block, z.block)
        mine_ref[at, :] = part[:z.block]
        for s, ref in enumerate(out_refs, 1):
            ref[at, :] = part[s * z.block:(s + 1) * z.block].astype(bf16)


def assemble(z, u_hbm, v_hbm, s_hbm, y_hbm, left_ref, right_ref,
             u_ref, v_ref, m_ref, s_ref, y_ref, sems):
    top = PAD * z.layers
    copies = []
    for c in range(z.parts):
        for k, (src, dst) in enumerate(((u_hbm, u_ref), (v_hbm, v_ref))):
            copies.append(
                pltpu.make_async_copy(
                    src.at[pl.ds(c * z.stride, z.stride)],
                    dst.at[c, pl.ds(top, z.stride)],
                    sems.at[2 * c + k],
                )
            )
    copies.append(pltpu.make_async_copy(s_hbm, s_ref, sems.at[2 * z.parts]))
    copies.append(pltpu.make_async_copy(y_hbm, y_ref, sems.at[2 * z.parts + 1]))
    for copy in copies:
        copy.start()
    size = z.layers
    end = (PAD + z.nodes) * size
    blank = jnp.zeros((size, z.dips), f32)
    for ref, at_u, at_v in ((left_ref, PAD - 3, PAD - 2), (right_ref, PAD + z.nodes, PAD + z.nodes)):
        for c in range(z.parts):
            for j in range(3):
                both = ref[pl.ds(z.halo_u + (c * 3 + j) * 2 * size, 2 * size), :].astype(f32)
                u_ref[c, pl.ds((at_u + j) * size, size), :] = both[:size] + both[size:]
            both = ref[pl.ds(z.halo_v + c * 2 * size, 2 * size), :].astype(f32)
            v_ref[c, pl.ds(at_v * size, 2 * size), :] = both
        m_ref[pl.ds(at_v * size, 2 * size), :] = ref[pl.ds(z.halo_m, 2 * size), :].astype(f32)
    for c in range(z.parts):
        u_ref[c, pl.ds(0, size), :] = blank
        u_ref[c, pl.ds(end + 3 * size, size), :] = blank
        for at in (0, size, end + 2 * size, end + 3 * size):
            v_ref[c, pl.ds(at, size), :] = blank
    for at in (0, size, end + 2 * size, end + 3 * size):
        m_ref[pl.ds(at, size), :] = blank
    for copy in copies:
        copy.wait()
    soft = widen_flags(y_ref[...], z.dips)
    for n in range(z.nodes):
        at = n // BLK * size
        m_ref[pl.ds(top + n * size, size), :] = s_ref[pl.ds(n * size, size), :] * soft[at:at + size]


def layer_of(z, level):
    is_high = lax.axis_index("normal") == z.normal - 1
    return jnp.where(is_high, z.layers - 1 - level, level)


def edge_kernel(z, u_hbm, v_hbm, s_hbm, y_hbm, c_hbm, left_ref, right_ref, *rest):
    outs = rest[:-7]
    (u_ref, v_ref, m_ref, s_ref, y_ref, c_ref, sems) = rest[-7:]
    modulus_ref, contact_ref = outs[:2]
    place = lax.axis_index("normal")
    is_high = place == z.normal - 1
    face = is_high.astype(jnp.int32)
    touch = pltpu.make_async_copy(c_hbm.at[face], c_ref, sems.at[2 * z.parts + 2])
    touch.start()
    assemble(z, u_hbm, v_hbm, s_hbm, y_hbm, left_ref, right_ref, u_ref, v_ref, m_ref, s_ref, y_ref, sems)
    for out, levels in zip(outs[2:], ((7, 6, 5), (0, 1, 2))):
        levels = tuple(z.layers - 8 + f if f > 2 else f for f in levels)
        for j, level in enumerate(levels):
            at = pl.ds(layer_of(z, level), z.span, stride=z.layers)
            for c in range(z.parts):
                out[3 * c + j] = u_ref[c, at, :]
                if j < 2:
                    out[3 * z.parts + 2 * c + j] = v_ref[c, at, :]
            if j < 2:
                out[5 * z.parts + j] = m_ref[at, :]
    modulus_ref[...] = jnp.zeros_like(modulus_ref)
    for j in range(3):
        at = pl.ds(layer_of(z, j), z.span, stride=z.layers)
        modulus_ref[j, pl.ds(EDGE - PAD, z.span), :] = m_ref[at, :]
    touch.wait()
    is_face = (is_high | (place == 0)).astype(f32)
    contact_ref[...] = jnp.zeros_like(contact_ref)
    contact_ref[pl.ds(EDGE, z.nodes), :] = c_ref[...].astype(f32) * is_face
    before = left_ref[pl.ds(z.halo_c, 16), :].astype(f32) * is_face
    after = right_ref[pl.ds(z.halo_c, 16), :].astype(f32) * is_face
    contact_ref[pl.ds(0, EDGE), :] = before[16 - EDGE:]
    contact_ref[pl.ds(EDGE + z.nodes, EDGE), :] = after[:EDGE]


def in_plane(values, first_dip, last_dip):
    count, dips = values.shape
    around = pltpu.roll(values, 1, 0) + pltpu.roll(values, count - 1, 0)
    around += jnp.where(first_dip, 0.0, pltpu.roll(values, 1, 1))
    around += jnp.where(last_dip, 0.0, pltpu.roll(values, dips - 1, 1))
    return around - 6.0 * values


def base_kernel(z, u_hbm, v_hbm, s_hbm, y_hbm, left_ref, right_ref, *rest):
    (out_u, out_v, u_ref, v_ref, m_ref, s_ref, y_ref, sems) = rest[-8:]
    sides = rest[:-8]
    assemble(z, u_hbm, v_hbm, s_hbm, y_hbm, left_ref, right_ref, u_ref, v_ref, m_ref, s_ref, y_ref, sems)
    dip = lax.broadcasted_iota(jnp.int32, (z.span, z.dips), 1)
    first_dip, last_dip = dip == 0, dip == z.dips - 1
    low = -2 if z.two_sided else 0
    top = z.layers

    def fetch(kind, c, level):
        if 0 <= level < top:
            at = pl.ds(layer_of(z, level), z.span, stride=z.layers)
            return m_ref[at, :] if kind == "m" else (u_ref if kind == "u" else v_ref)[c, at, :]
        side, j = (sides[0], level - top) if level >= top else (sides[1], -1 - level)
        base = {"u": 3 * c, "v": 3 * z.parts + 2 * c, "m": 5 * z.parts}[kind]
        return side[base + j]

    def one_part(c, unused):
        u = {f: fetch("u", c, f) for f in range(low - 1 if z.two_sided else 0, top + 3)}
        v = {f: fetch("v", c, f) for f in range(low, top + 2)}
        for step in range(SUB):
            levels = range(low + step if z.two_sided else 0, top + 2 - step)
            for f in levels:
                lap = in_plane(u[f], first_dip, last_dip) + u[f + 1]
                if f - 1 in u:
                    lap += u[f - 1]
                v[f] = v[f] + time_step * (fetch("m", c, f) * lap)
            u = {f: u[f] + time_step * v[f] for f in levels}
        for f in range(top):
            at = pl.ds(c * z.stride + layer_of(z, f), z.nodes, stride=z.layers)
            out_u[at, :] = u[f][PAD:PAD + z.nodes]
            out_v[at, :] = v[f][PAD:PAD + z.nodes]
        return unused

    lax.fori_loop(0, z.parts, one_part, 0)


def final_kernel(z, mine_ref, contact_ref, modulus_ref, base_u, base_v, *rest):
    out_u, out_v = rest[-2:]
    dip = lax.broadcasted_iota(jnp.int32, (z.block, z.dips), 1)
    first_dip, last_dip = dip == 0, dip == z.dips - 1
    out_u[...] = base_u[...]
    out_v[...] = base_v[...]
    contact = contact_ref[...]
    m0, m1, m2 = modulus_ref[0], modulus_ref[1], modulus_ref[2]
    h = time_step
    for c in range(z.parts):
        at = pl.ds(c * z.block, z.block)
        force = mine_ref[at, :]
        for ref in rest[:-2]:
            force = force + ref[at, :].astype(f32)
        force = force * contact
        v0 = h * force
        u0 = h * v0
        v1 = h * (m1 * u0)
        v0 = v0 + h * (m0 * in_plane(u0, first_dip, last_dip) + force)
        u0 = u0 + h * v0
        u1 = h * v1
        v2 = h * (m2 * u1)
        w0 = v0 + h * (m0 * (in_plane(u0, first_dip, last_dip) + u1) + force)
        v1 = v1 + h * (m1 * (in_plane(u1, first_dip, last_dip) + u0))
        pairs = ((u0 + h * w0, w0), (u1 + h * v1, v1), (h * v2, v2))
        for f, (du, dv) in enumerate(pairs):
            at = pl.ds(c * z.stride + layer_of(z, f), z.nodes, stride=z.layers)
            out_u[at, :] = out_u[at, :] + du[EDGE:EDGE + z.nodes]
            out_v[at, :] = out_v[at, :] + dv[EDGE:EDGE + z.nodes]


PARAMS = pltpu.CompilerParams(vmem_limit_bytes=32 * 2**20)


def shape(dims, kind):
    return jax.ShapeDtypeStruct(dims, kind)


def body(mesh, displacement, velocity, stiffness, yield_flags, contact, history, kernel):
    z = Sizes(mesh, displacement, history)
    u = displacement.reshape(-1, z.dips)
    v = velocity.reshape(-1, z.dips)
    s = stiffness.reshape(-1, z.dips)
    y = yield_flags.reshape(-1, yield_flags.shape[2])
    dma = pltpu.SemaphoreType.DMA
    ring = lambda step: [(i, (i + step) % z.strike) for i in range(z.strike)]

    to_right, to_left, to_far, response = pl.pallas_call(
        functools.partial(prep_kernel, z),
        out_shape=(
            shape((z.whole, LANES), bf16),
            shape((z.whole, LANES), bf16),
            shape((z.common, LANES), bf16),
            shape((z.chunks, 8, LANES), f32),
        ),
        in_specs=[ANY] * 8,
        out_specs=(VMEM,) * 4,
        scratch_shapes=[
            pltpu.VMEM(u.shape, f32),
            pltpu.VMEM((2, z.parts, 2, z.layers, z.dips), f32),
            pltpu.VMEM((2, 2, z.layers, z.dips), f32),
            pltpu.VMEM(y.shape, jnp.int32),
            pltpu.VMEM(contact.shape[1:], jnp.int32),
            pltpu.VMEM((z.lags - 1, 2, z.parts, z.rows, z.modes), bf16),
            pltpu.VMEM((z.lags, z.parts, z.modes), f32),
            pltpu.VMEM((2 * z.modes, z.modes // 4), bf16),
            pltpu.VMEM((z.chunk_rows, z.modes), f32),
            pltpu.VMEM((z.chunk_rows, z.modes), f32),
            dma((10,)),
        ],
        compiler_params=PARAMS,
        name="prepare",
    )(u, velocity, stiffness, y, contact, history, kernel, phase_quarter(z.modes))

    from_left = lax.ppermute(to_right, "strike", ring(1))
    from_right = lax.ppermute(to_left, "strike", ring(-1))
    from_far = lax.ppermute(to_far, "strike", ring(2))

    toeplitz = pl.pallas_call(
        functools.partial(toeplitz_kernel, z),
        out_shape=shape((z.parts, z.targets * z.block, LANES), bf16),
        in_specs=[VMEM],
        out_specs=VMEM,
        compiler_params=PARAMS,
        name="toeplitz",
    )(response)

    block = (z.parts * z.block, z.dips)
    mine, *parcels = pl.pallas_call(
        functools.partial(middle_kernel, z),
        out_shape=(shape(block, f32),) + (shape(block, bf16),) * (z.targets - 1),
        in_specs=[VMEM] * 5,
        out_specs=(VMEM,) * z.targets,
        compiler_params=PARAMS,
        name="partial_tractions",
    )(toeplitz, from_far, from_left, to_far, from_right)

    arrived = [lax.ppermute(p, "strike", ring(WIN * (k + 1))) for k, p in enumerate(parcels)]

    tiles = [
        pltpu.VMEM((z.parts, z.span * z.layers, z.dips), f32),
        pltpu.VMEM((z.parts, z.span * z.layers, z.dips), f32),
        pltpu.VMEM((z.span * z.layers, z.dips), f32),
        pltpu.VMEM(s.shape, f32),
        pltpu.VMEM(y.shape, jnp.int32),
    ]
    edge = (5 * z.parts + 2, z.span, z.dips)
    sides = 2 if z.two_sided else 1
    modulus, touching, *edges = pl.pallas_call(
        functools.partial(edge_kernel, z),
        out_shape=(shape((3, z.block, z.dips), f32), shape((z.block, z.dips), f32))
        + (shape(edge, f32),) * sides,
        in_specs=[ANY] * 5 + [VMEM] * 2,
        out_specs=(VMEM,) * (2 + sides),
        scratch_shapes=tiles + [pltpu.VMEM(contact.shape[1:], jnp.int32), dma((2 * z.parts + 3,))],
        compiler_params=PARAMS,
        name="normal_edges",
    )(u, v, s, y, contact, from_left, from_right)

    if z.two_sided:
        is_high = lax.axis_index("normal") == z.normal - 1
        above, below = edges
        steps = [(i, i + 1) for i in range(z.normal - 1)]
        from_below = lax.ppermute(above, "normal", steps)
        from_above = lax.ppermute(
            jnp.where(is_high, above, below), "normal", [(j, i) for i, j in steps]
        )
        sided = [
            jnp.where(is_high, from_below, from_above),
            jnp.where(is_high, from_above, from_below),
        ]
    else:
        sided = [lax.ppermute(edges[0], "normal", [(0, 1), (1, 0)])]

    base = pl.pallas_call(
        functools.partial(base_kernel, z),
        out_shape=(shape(u.shape, f32),) * 2,
        in_specs=[ANY] * 4 + [VMEM] * (2 + sides),
        out_specs=(VMEM,) * 2,
        scratch_shapes=tiles + [dma((2 * z.parts + 2,))],
        compiler_params=PARAMS,
        name="unloaded_substeps",
    )(u, v, s, y, from_left, from_right, *sided)

    moved, speed = pl.pallas_call(
        functools.partial(final_kernel, z),
        out_shape=(shape(u.shape, f32),) * 2,
        in_specs=[VMEM] * (5 + len(arrived)),
        out_specs=(VMEM,) * 2,
        compiler_params=PARAMS,
        name="add_force_response",
    )(mine, touching, modulus, *base, *arrived)
    return (moved.reshape(displacement.shape), speed.reshape(displacement.shape))


def solution(mesh):
    return jax.shard_map(
        functools.partial(body, mesh),
        mesh=mesh,
        in_specs=(
            P(None, "strike", "normal", None),
            P(None, "strike", "normal", None),
            P("strike", "normal", None),
            P("strike", "normal", None),
            P(None, "strike", None),
            P(None, None, None, None, "strike", None),
            P(),
        ),
        out_specs=(P(None, "strike", "normal", None), P(None, "strike", "normal", None)),
        check_vma=False,
    )
```

time: 86.4 us -> 34.5 us (0.40)
  starting transfers between devices: 38 us -> 12.6 us
  matrix products: 17.3 us -> 0 us
  waiting for transfers between devices: 16.8 us -> 8.54 us
  Pallas kernels: 0 us -> 7.28 us
  other arithmetic: 5.33 us -> 0 us
  local copies, waits for them, and re-layouts: 7.48 us -> 5.1 us
    dot_general x4 -> x0, matrix products: 17.3 us -> none  [the longest x1 4.43 us: one_block(): jnp.dot(flat, sines, preferred_element_type=jnp.float32)]
    all_to_all x2 -> x0, starting transfers between devices: 15.3 us -> none  [the longest x1 8.31 us: body(): lax.all_to_all(outgoing, 'strike', split_axis=1, concat_axis=2, tiled=True)]
    ppermute x12 -> x7, starting transfers between devices: 22.6 us -> 12.6 us  [the longest x1 4.06 us: body(): from_right = lax.ppermute(to_left, 'strike', ring(-1))]
    pallas_call x0 -> x6, Pallas kernels: none -> 7.28 us  [the longest x1 2.9 us: body(): pl.pallas_call(functools.partial(base_kernel, z), out_shape=(shape(u.shap...]
    all_to_all x2 -> x0, waiting for transfers between devices: 5.48 us -> none  [the longest x1 5.48 us: body(): lax.all_to_all(traction.astype(jnp.bfloat16), 'strike', split_axis=2, con...]
    ppermute x12 -> x7, waiting for transfers between devices: 11.3 us -> 8.54 us  [the longest x1 5.33 us: body(): from_far = lax.ppermute(to_far, 'strike', ring(2))]
    slice x6 -> x0, local copies, waits for them, and re-layouts: 2.68 us -> none  [padded(): head = lax.slice_in_dim(cells, 0, width, axis=dim)]
    unnamed x14 -> x19, local copies, waits for them, and re-layouts: 2.45 us -> 5.1 us
  transfers between devices with their start and end apart: 14 -> 7, of which waited for: 5 -> 2; matrix products, arithmetic and copies ran while one was open for 31% -> 0% of each run, Pallas kernels for 0% -> 10%
where the time goes in v1:
time: 34.5 us; the launch traced here: 34.3 us
  starting transfers between devices  12.6 us (37%)
  waiting for transfers between devices  8.54 us (25%)
  Pallas kernels  7.28 us (21%)
  local copies, waits for them, and re-layouts  5.1 us (15%)
  between operations  0.79 us (2%)
    ppermute x1, waiting for transfers between devices, body(): from_far = lax.ppermute(to_far, 'strike', ring(2))  5.33 us
    unnamed x19, local copies, waits for them, and re-layouts  5.1 us
    ppermute x1, starting transfers between devices, body(): from_right = lax.ppermute(to_left, 'strike', ring(-1))  4.06 us
    ppermute x3, starting transfers between devices, body(): lax.ppermute(p, 'strike', ring(WIN * (k + 1)))  3.87 us
    ppermute x1, waiting for transfers between devices, body(): from_left = lax.ppermute(to_right, 'strike', ring(1))  3.19 us
    ppermute x1, starting transfers between devices, body(): from_left = lax.ppermute(to_right, 'strike', ring(1))  2.99 us
    pallas_call x1, Pallas kernels, body(): pl.pallas_call(functools.partial(base_kernel, z), out_shape=(shape(u.shap...  2.9 us
    ppermute x1, starting transfers between devices, body(): from_far = lax.ppermute(to_far, 'strike', ring(2))  1.57 us
  transfers between devices with their start and end apart: 7, of which 2 were waited for; matrix products, arithmetic and copies ran while one was open for 0% of the time, Pallas kernels for 10%

profile of v1, /device:TPU:0, one launch (start us, length us, event | category | flops | bytes accessed | tf_op | source)
XLA Modules:
  0.0 34.3 jit_solution(13095560902509678823)
XLA Ops:
  0.6 0.0 copy-start.8
  0.6 0.0 copy-start.4
  0.7 0.0 copy-start.6
  0.7 1.0 %copy.10.k_hbm = f32[2,8,3,512]{3,2,1,0:T(4,128)S(1)} copy(f32[2,8,3,512]{3,1,2,0:T(8,128)} %param.14) | data formatting | bytes 196608 | tf_op args[6]
  1.7 0.0 copy-done.8
  1.7 0.0 copy-done.4
  1.7 0.0 copy-done.6
  1.7 0.0 copy-start
  1.7 1.0 %copy-done = f32[3,32,8,128]{3,2,1,0:T(8,128)S(1)} copy-done((f32[3,32,8,128]{3,2,1,0:T(8,128)S(1)}, f32[3,32,8,128]{3,2,1,0:T(8,128)}, u32[]{:S(2)}) %copy-start) | copy-done | bytes 393240
  2.7 0.0 copy-start.2
  2.7 1.0 %copy-done.2 = f32[3,32,8,128]{3,2,1,0:T(8,128)S(1)} copy-done((f32[3,32,8,128]{3,2,1,0:T(8,128)S(1)}, f32[3,32,8,128]{3,2,1,0:T(8,128)}, u32[]{:S(2)}) %copy-start.2) | copy-done | bytes 393240
  3.7 0.0 copy-start.5
  3.7 1.1 %copy-done.5 = bf16[2,8,2,3,8,512]{5,4,3,2,1,0:T(8,128)(2,1)S(1)} copy-done((bf16[2,8,2,3,8,512]{5,4,3,2,1,0:T(8,128)(2,1)S(1)}, bf16[2,8,2,3,8,512]{5,4,3,2,1,0:T(8,128)(2,1)}, u32[]{:S(2)}) %copy-start.5) | copy-done | bytes 786456
  4.8 0.0 copy-start.7
  4.8 0.9 %copy-done.7 = bf16[1024,128]{1,0:T(8,128)(2,1)S(1)} copy-done((bf16[1024,128]{1,0:T(8,128)(2,1)S(1)}, bf16[1024,128]{1,0:T(8,128)(2,1)}, u32[]{:S(2)}) %copy-start.7) | copy-done | bytes 262168
  5.8 1.1 %prepare.1 = (bf16[448,128]{1,0:T(8,128)(2,1)S(1)}, bf16[448,128]{1,0:T(8,128)(2,1)S(1)}, bf16[224,128]{1,0:T(8,128)(2,1)S(1)}, f32[4,8,128]{2,1,0:T(8,128)S(1)}) custom-call(f32[768,128]{1,0:T(8,128)S(1)} %bitcast.6, f32[3,32,8,128]{3,2,1,0:T(8,128)S(1)} %copy-done.2, f32[32,8,128]{2,1,0:T(8,128)S(1)} %copy-done.4, s32[64,32]{1,0:T(8,128)S(1)} %bitcast.13, ...), custom_call_target="tpu_custom_call" | custom-call | tf_op jit(solution)/shard_map/prepare/pallas_call | solution.py:389
  6.9 3.0 %collective-permute-start.1 = (bf16[448,128]{1,0:T(8,128)(2,1)S(1)}, bf16[448,128]{1,0:T(8,128)(2,1)S(1)}, u32[]{:S(2)}, u32[]{:S(2)}) collective-permute-start(bf16[448,128]{1,0:T(8,128)(2,1)S(1)} %get-tuple-element.19), channel_id=1, source_target_pairs={{0,2},{2,4},{4,6},{6,8},{8,10},{10,12},{12,14},{14,16},{16,18},{18... | collective-permute-start | bytes 344072 | tf_op jit(solution)/shard_map/ppermute | solution.py:416
  9.9 4.1 %collective-permute-start.2 = (bf16[448,128]{1,0:T(8,128)(2,1)S(1)}, bf16[448,128]{1,0:T(8,128)(2,1)S(1)}, u32[]{:S(2)}, u32[]{:S(2)}) collective-permute-start(bf16[448,128]{1,0:T(8,128)(2,1)S(1)} %get-tuple-element.20), channel_id=1, source_target_pairs={{0,30},{2,0},{4,2},{6,4},{8,6},{10,8},{12,10},{14,12},{16,14},{18,... | collective-permute-start | bytes 344072 | tf_op jit(solution)/shard_map/ppermute | solution.py:417
  13.9 3.2 %collective-permute-done.1.left_ref = bf16[448,128]{1,0:T(8,128)(2,1)S(1)} collective-permute-done((bf16[448,128]{1,0:T(8,128)(2,1)S(1)}, bf16[448,128]{1,0:T(8,128)(2,1)S(1)}, u32[]{:S(2)}, u32[]{:S(2)}) %collective-permute-start.1) | collective-permute-done | bytes 114720 | tf_op jit(solution)/shard_map/ppermute | solution.py:416
  17.1 0.0 collective-permute-done.2.right_ref
  17.1 0.0 copy-start.3
  17.1 1.5 %normal_edges.1 = (f32[3,48,128]{2,1,0:T(8,128)S(1)}, f32[48,128]{1,0:T(8,128)S(1)}, f32[17,40,128]{2,1,0:T(8,128)S(1)}) custom-call(f32[768,128]{1,0:T(8,128)S(1)} %bitcast.7, f32[768,128]{1,0:T(8,128)S(1)} %bitcast.9, f32[256,128]{1,0:T(8,128)S(1)} %bitcast.11, s32[64,32]{1,0:T(8,128)S(1)} %bitcast.14, s32[2,32,128]{2,1,0:T(8,128)S(1)} %copy-done.8, ...), custom_call_target="tpu_custom_call" | custom-call | tf_op jit(solution)/shard_map/normal_edges/pallas_call | solution.py:450
  18.7 0.0 copy-start.1
  18.7 0.1 collective-permute-start.3
  18.8 1.6 %collective-permute-start = (bf16[224,128]{1,0:T(8,128)(2,1)S(1)}, bf16[224,128]{1,0:T(8,128)(2,1)S(1)}, u32[]{:S(2)}, u32[]{:S(2)}) collective-permute-start(bf16[224,128]{1,0:T(8,128)(2,1)S(1)} %get-tuple-element.18.own_ref), channel_id=1, source_target_pairs={{0,4},{2,6},{4,8},{6,10},{8,12},{10,14},{12,16},{14,18},{16,20},{1... | collective-permute-start | bytes 172040 | tf_op jit(solution)/shard_map/ppermute | solution.py:418
  20.3 0.1 toeplitz.1.toeplitz_ref
  20.4 5.3 %collective-permute-done.far_ref = bf16[224,128]{1,0:T(8,128)(2,1)S(1)} collective-permute-done((bf16[224,128]{1,0:T(8,128)(2,1)S(1)}, bf16[224,128]{1,0:T(8,128)(2,1)S(1)}, u32[]{:S(2)}, u32[]{:S(2)}) %collective-permute-start) | collective-permute-done | bytes 57376 | tf_op jit(solution)/shard_map/ppermute | solution.py:418
  25.8 0.5 %partial_tractions.1 = (f32[144,128]{1,0:T(8,128)S(1)}, bf16[144,128]{1,0:T(8,128)(2,1)S(1)}, bf16[144,128]{1,0:T(8,128)(2,1)S(1)}, bf16[144,128]{1,0:T(8,128)(2,1)S(1)}) custom-call(bf16[3,192,128]{2,1,0:T(8,128)(2,1)S(1)} %toeplitz.1.toeplitz_ref, bf16[224,128]{1,0:T(8,128)(2,1)S(1)} %collective-permute-done.far_ref, ...), custom_call_target="tpu_custom_call" | custom-call | tf_op jit(solution)/shard_map/partial_tractions/pallas_call | solution.py:430
  26.3 0.1 collective-permute-start.4
  26.3 1.9 %collective-permute-start.5 = (bf16[144,128]{1,0:T(8,128)(2,1)S(1)}, bf16[144,128]{1,0:T(8,128)(2,1)S(1)}, u32[]{:S(2)}, u32[]{:S(2)}) collective-permute-start(bf16[144,128]{1,0:T(8,128)(2,1)S(1)} %get-tuple-element.28), channel_id=1, source_target_pairs={{0,16},{2,18},{4,20},{6,22},{8,24},{10,26},{12,28},{14,30},{16,0},... | collective-permute-start | bytes 110600 | tf_op jit(solution)/shard_map/ppermute | solution.py:439
  28.2 1.9 %collective-permute-start.6 = (bf16[144,128]{1,0:T(8,128)(2,1)S(1)}, bf16[144,128]{1,0:T(8,128)(2,1)S(1)}, u32[]{:S(2)}, u32[]{:S(2)}) collective-permute-start(bf16[144,128]{1,0:T(8,128)(2,1)S(1)} %get-tuple-element.29), channel_id=1, source_target_pairs={{0,24},{2,26},{4,28},{6,30},{8,0},{10,2},{12,4},{14,6},{16,8},{18,... | collective-permute-start | bytes 110600 | tf_op jit(solution)/shard_map/ppermute | solution.py:439
  30.1 0.0 collective-permute-done.3.rest_0_
  30.1 0.0 copy-done.3
  30.1 0.0 copy-done.1
  30.1 2.9 %unloaded_substeps.1 = (f32[768,128]{1,0:T(8,128)S(1)}, f32[768,128]{1,0:T(8,128)S(1)}) custom-call(f32[768,128]{1,0:T(8,128)S(1)} %bitcast.8, f32[768,128]{1,0:T(8,128)S(1)} %bitcast.10, f32[256,128]{1,0:T(8,128)S(1)} %bitcast.12, s32[64,32]{1,0:T(8,128)S(1)} %bitcast.15, bf16[448,128]{1,0:T(8,128)(2,1)S(1)} %collective-permute-done.1.left_ref, ...), custom_call_target="tpu_custom_call" | custom-call | tf_op jit(solution)/shard_map/unloaded_substeps/pallas_call | solution.py:476
  33.1 0.0 collective-permute-done.4.rest_0_
  33.1 0.0 collective-permute-done.5.rest_1_
  33.1 0.0 collective-permute-done.6.rest_2_
  33.1 1.2 %add_force_response.1 = (f32[768,128]{1,0:T(8,128)}, f32[768,128]{1,0:T(8,128)}) custom-call(f32[144,128]{1,0:T(8,128)S(1)} %get-tuple-element.21.mine_ref, f32[48,128]{1,0:T(8,128)S(1)} %get-tuple-element.22.contact_ref, f32[3,48,128]{2,1,0:T(8,128)S(1)} %get-tuple-element.23.modulus_ref, f32[768,128]{1,0:T(8,128)S(1)} %get-tuple-element.25.base_u, ...), custom_call_target="tpu_custom_call" | custom-call | tf_op jit(solution)/shard_map/add_force_response/pallas_call | solution.py:486
Async XLA Ops:
  0.6 1.0 %copy-start.8 = (s32[2,32,128]{2,1,0:T(8,128)S(1)}, s32[2,32,128]{2,1,0:T(8,128)}, u32[]{:S(2)}) copy-start(s32[2,32,128]{2,1,0:T(8,128)} %c_hbm.3) | copy-start | bytes 98308
  0.6 1.0 %copy-start.4 = (f32[32,8,128]{2,1,0:T(8,128)S(1)}, f32[32,8,128]{2,1,0:T(8,128)}, u32[]{:S(2)}) copy-start(f32[32,8,128]{2,1,0:T(8,128)} %s_hbm.1) | copy-start | bytes 393220
  0.7 1.0 %copy-start.6 = (s32[8,8,32]{2,1,0:T(8,128)S(1)}, s32[8,8,32]{2,1,0:T(8,128)}, u32[]{:S(2)}) copy-start(s32[8,8,32]{2,1,0:T(8,128)} %param.11) | copy-start | bytes 24580
  1.7 1.0 %copy-start = (f32[3,32,8,128]{3,2,1,0:T(8,128)S(1)}, f32[3,32,8,128]{3,2,1,0:T(8,128)}, u32[]{:S(2)}) copy-start(f32[3,32,8,128]{3,2,1,0:T(8,128)} %param.8) | copy-start | bytes 1179652
  2.7 1.0 %copy-start.2 = (f32[3,32,8,128]{3,2,1,0:T(8,128)S(1)}, f32[3,32,8,128]{3,2,1,0:T(8,128)}, u32[]{:S(2)}) copy-start(f32[3,32,8,128]{3,2,1,0:T(8,128)} %v_hbm.1) | copy-start | bytes 1179652
  3.7 1.1 %copy-start.5 = (bf16[2,8,2,3,8,512]{5,4,3,2,1,0:T(8,128)(2,1)S(1)}, bf16[2,8,2,3,8,512]{5,4,3,2,1,0:T(8,128)(2,1)}, u32[]{:S(2)}) copy-start(bf16[2,8,2,3,8,512]{5,4,3,2,1,0:T(8,128)(2,1)} %h_hbm.1) | copy-start | bytes 2359300
  4.8 0.9 %copy-start.7 = (bf16[1024,128]{1,0:T(8,128)(2,1)S(1)}, bf16[1024,128]{1,0:T(8,128)(2,1)}, u32[]{:S(2)}) copy-start(bf16[1024,128]{1,0:T(8,128)(2,1)} %constant.2.clone.t_hbm) | copy-start | bytes 786436
  6.9 10.2 %collective-permute-start.1 = (bf16[448,128]{1,0:T(8,128)(2,1)S(1)}, bf16[448,128]{1,0:T(8,128)(2,1)S(1)}, u32[]{:S(2)}, u32[]{:S(2)}) collective-permute-start(bf16[448,128]{1,0:T(8,128)(2,1)S(1)} %get-tuple-element.19), channel_id=1, source_target_pairs={{0,2},{2,4},{4,6},{6,8},{8,10},{10,12},{12,14},{14,16},{16,18},{18... | collective-permute-start | bytes 344072 | tf_op jit(solution)/shard_map/ppermute | solution.py:416
  9.9 7.2 %collective-permute-start.2 = (bf16[448,128]{1,0:T(8,128)(2,1)S(1)}, bf16[448,128]{1,0:T(8,128)(2,1)S(1)}, u32[]{:S(2)}, u32[]{:S(2)}) collective-permute-start(bf16[448,128]{1,0:T(8,128)(2,1)S(1)} %get-tuple-element.20), channel_id=1, source_target_pairs={{0,30},{2,0},{4,2},{6,4},{8,6},{10,8},{12,10},{14,12},{16,14},{18,... | collective-permute-start | bytes 344072 | tf_op jit(solution)/shard_map/ppermute | solution.py:417
  17.1 13.0 %copy-start.3 = (f32[3,32,8,128]{3,2,1,0:T(8,128)S(1)}, f32[3,32,8,128]{3,2,1,0:T(8,128)}, u32[]{:S(2)}) copy-start(f32[3,32,8,128]{3,2,1,0:T(8,128)} %v_hbm.1) | copy-start | bytes 1179652
  18.7 11.5 %copy-start.1 = (f32[3,32,8,128]{3,2,1,0:T(8,128)S(1)}, f32[3,32,8,128]{3,2,1,0:T(8,128)}, u32[]{:S(2)}) copy-start(f32[3,32,8,128]{3,2,1,0:T(8,128)} %param.8) | copy-start | bytes 1179652
  18.7 11.5 %collective-permute-start.3 = (f32[17,40,128]{2,1,0:T(8,128)S(1)}, f32[17,40,128]{2,1,0:T(8,128)S(1)}, u32[]{:S(2)}, u32[]{:S(2)}) collective-permute-start(f32[17,40,128]{2,1,0:T(8,128)S(1)} %get-tuple-element.24), channel_id=1, source_target_pairs={{0,1},{1,0},{2,3},{3,2},{4,5},{5,4},{6,7},{7,6},{8,9},{9,8},{10,11... | collective-permute-start | bytes 1044488 | tf_op jit(solution)/shard_map/ppermute | solution.py:474
  18.8 7.0 %collective-permute-start = (bf16[224,128]{1,0:T(8,128)(2,1)S(1)}, bf16[224,128]{1,0:T(8,128)(2,1)S(1)}, u32[]{:S(2)}, u32[]{:S(2)}) collective-permute-start(bf16[224,128]{1,0:T(8,128)(2,1)S(1)} %get-tuple-element.18.own_ref), channel_id=1, source_target_pairs={{0,4},{2,6},{4,8},{6,10},{8,12},{10,14},{12,16},{14,18},{16,20},{1... | collective-permute-start | bytes 172040 | tf_op jit(solution)/shard_map/ppermute | solution.py:418
  26.3 6.8 %collective-permute-start.4 = (bf16[144,128]{1,0:T(8,128)(2,1)S(1)}, bf16[144,128]{1,0:T(8,128)(2,1)S(1)}, u32[]{:S(2)}, u32[]{:S(2)}) collective-permute-start(bf16[144,128]{1,0:T(8,128)(2,1)S(1)} %get-tuple-element.27), channel_id=1, source_target_pairs={{0,8},{2,10},{4,12},{6,14},{8,16},{10,18},{12,20},{14,22},{16,24},... | collective-permute-start | bytes 110600 | tf_op jit(solution)/shard_map/ppermute | solution.py:439
  26.3 6.7 %collective-permute-start.5 = (bf16[144,128]{1,0:T(8,128)(2,1)S(1)}, bf16[144,128]{1,0:T(8,128)(2,1)S(1)}, u32[]{:S(2)}, u32[]{:S(2)}) collective-permute-start(bf16[144,128]{1,0:T(8,128)(2,1)S(1)} %get-tuple-element.28), channel_id=1, source_target_pairs={{0,16},{2,18},{4,20},{6,22},{8,24},{10,26},{12,28},{14,30},{16,0},... | collective-permute-start | bytes 110600 | tf_op jit(solution)/shard_map/ppermute | solution.py:439
  28.2 4.9 %collective-permute-start.6 = (bf16[144,128]{1,0:T(8,128)(2,1)S(1)}, bf16[144,128]{1,0:T(8,128)(2,1)S(1)}, u32[]{:S(2)}, u32[]{:S(2)}) collective-permute-start(bf16[144,128]{1,0:T(8,128)(2,1)S(1)} %get-tuple-element.29), channel_id=1, source_target_pairs={{0,24},{2,26},{4,28},{6,30},{8,0},{10,2},{12,4},{14,6},{16,8},{18,... | collective-permute-start | bytes 110600 | tf_op jit(solution)/shard_map/ppermute | solution.py:439

commit v2 on v1

v2 whole, which is shorter than its diff:
```python
import functools
import math

import jax
import jax.numpy as jnp
import numpy as np
from jax import lax
from jax.experimental import pallas as pl
from jax.experimental.pallas import tpu as pltpu
from jax.sharding import PartitionSpec as P

SUB = 3
BLK = 4
WIN = 4
TAIL = 8
LANES = 128

time_step = 0.5

f32 = jnp.float32
bf16 = jnp.bfloat16
VMEM = pl.BlockSpec(memory_space=pltpu.VMEM)


def round_up(value, step):
    return -(-value // step) * step


def phase_quarter(mode_count):
    phase = np.outer(np.arange(mode_count), np.arange(mode_count // 4)) % mode_count
    phase = phase * (2.0 * np.pi / mode_count)
    return np.concatenate([np.cos(phase), -np.sin(phase)]).astype(np.float32).astype(bf16)


class Sizes:
    def __init__(self, mesh, displacement, history):
        self.strike = mesh.shape["strike"]
        self.normal = mesh.shape["normal"]
        self.parts, self.nodes, self.layers, self.dips = displacement.shape
        self.lags = history.shape[1]
        self.rows = history.shape[4]
        self.modes = history.shape[5]
        self.chunks = self.modes // LANES
        self.spectral = round_up(self.parts * self.rows, 8)
        self.chunk_rows = round_up(self.spectral + 2 * self.parts, 16)
        self.plane_rows = self.parts * self.nodes
        self.common = self.plane_rows + self.chunks * self.chunk_rows
        self.halo_v = self.parts * 3 * 2 * self.layers
        self.halo_m = self.halo_v + self.parts * 2 * self.layers
        self.halo_c = self.halo_m + 2 * self.layers
        self.corner = self.halo_c + 16
        self.span = self.nodes + TAIL
        self.targets = self.strike // WIN
        self.stride = self.nodes * self.layers
        self.sides = 1 if self.normal == 2 else 2
        self.halo = self.corner + round_up(self.sides * self.parts * 8, 16)


def widen_flags(flags, dips):
    blocks = flags.shape[1]
    block_id = lax.broadcasted_iota(jnp.int32, (blocks, dips), 0)
    dip_id = lax.broadcasted_iota(jnp.int32, (blocks, dips), 1)
    spread = (dip_id // BLK == block_id).astype(bf16)
    wide = jnp.dot(flags.astype(f32).astype(bf16), spread, preferred_element_type=f32)
    return 1.0 - 0.5 * wide


def node_offset(rows):
    return jnp.where(rows < rows.shape[0] - TAIL // 2, rows, rows - rows.shape[0])


def layer_of(z, level):
    is_high = lax.axis_index("normal") == z.normal - 1
    return jnp.where(is_high, z.layers - 1 - level, level)


def start_all(pairs, sems):
    copies = [pltpu.make_async_copy(a, b, sems.at[i]) for i, (a, b) in enumerate(pairs)]
    for copy in copies:
        copy.start()
    return copies


def set_modulus(z, s_ref, y_ref, out_ref):
    soft = widen_flags(y_ref[...], z.dips)
    for n in range(z.nodes):
        at = n // BLK * z.layers
        rows = pl.ds(n * z.layers, z.layers)
        out_ref[rows, :] = s_ref[rows, :] * soft[at:at + z.layers]


def common_kernel(z, u_hbm, h_hbm, k_hbm, t_hbm, v_hbm, s_hbm, y_hbm, out_ref, g_ref, *rest):
    edges = rest[:z.sides]
    u_ref, h_ref, k_ref, t_ref, v_ref, s_ref, y_ref, re_ref, im_ref, sems = rest[z.sides:]
    is_high = lax.axis_index("normal") == z.normal - 1
    face = is_high.astype(jnp.int32)
    copies = start_all(
        [
            (h_hbm.at[face, pl.ds(0, z.lags - 1)], h_ref),
            (k_hbm.at[face], k_ref),
            (t_hbm, t_ref),
            (u_hbm, u_ref),
            (v_hbm, v_ref),
            (s_hbm, s_ref),
            (y_hbm, y_ref),
        ],
        sems,
    )
    re_ref[...] = jnp.zeros_like(re_ref)
    im_ref[...] = jnp.zeros_like(im_ref)
    copies[1].wait()
    copies[0].wait()
    for c in range(z.parts):
        for q, dst in ((0, re_ref), (1, im_ref)):
            total = None
            for lag in range(1, z.lags):
                term = k_ref[c, pl.ds(lag, 1), :] * h_ref[lag - 1, q, c].astype(f32)
                total = term if total is None else total + term
            dst[pl.ds(c * z.rows, z.rows), :] = total
        newest = k_ref[c, pl.ds(0, 1), :]
        high = newest.astype(bf16).astype(f32)
        re_ref[pl.ds(z.spectral + c, 1), :] = high
        re_ref[pl.ds(z.spectral + z.parts + c, 1), :] = newest - high
    re, im = re_ref[...], im_ref[...]
    quarter = lax.broadcasted_iota(jnp.int32, (1, z.modes), 1) % 4
    one = (quarter == 0).astype(f32) - (quarter == 2).astype(f32)
    two = (quarter == 1).astype(f32) - (quarter == 3).astype(f32)
    flip = 1.0 - 2.0 * (quarter % 2).astype(f32)
    turned = jnp.concatenate(
        [
            jnp.concatenate([re, im], axis=1),
            jnp.concatenate([re * one - im * two, re * two + im * one], axis=1),
            jnp.concatenate([re * flip, im * flip], axis=1),
            jnp.concatenate([re * one + im * two, im * one - re * two], axis=1),
        ],
        axis=0,
    ).astype(bf16)
    copies[2].wait()
    lines = jnp.dot(turned, t_ref[...], preferred_element_type=f32) * (1.0 / math.sqrt(z.modes))
    per_quarter = z.chunks // 4
    for m in range(4):
        for q in range(per_quarter):
            piece = lines[m * z.chunk_rows:(m + 1) * z.chunk_rows, q * LANES:(q + 1) * LANES]
            chunk = m * per_quarter + q
            out_ref[pl.ds(z.plane_rows + chunk * z.chunk_rows, z.chunk_rows), :] = piece.astype(bf16)
            g_ref[chunk] = piece[z.spectral:z.spectral + 8]
    copies[3].wait()
    layer = face * (z.layers - 1)
    for c in range(z.parts):
        plane = u_ref[pl.ds(c * z.stride + layer, z.nodes, stride=z.layers), :]
        out_ref[pl.ds(c * z.nodes, z.nodes), :] = plane.astype(bf16)
    for copy in copies[4:]:
        copy.wait()
    set_modulus(z, s_ref, y_ref, s_ref)
    size = z.layers
    for out, levels in zip(edges, ((size - 1, size - 2, size - 3), (0, 1, 2))):
        for j, f in enumerate(levels):
            layer = layer_of(z, f)
            for c in range(z.parts):
                at = pl.ds(c * z.stride + layer, z.nodes, stride=size)
                out[3 * c + j] = u_ref[at, :]
                if j < 2:
                    out[3 * z.parts + 2 * c + j] = v_ref[at, :]
            if j < 2:
                out[5 * z.parts + j] = s_ref[pl.ds(layer, z.nodes, stride=size), :]


def halo_kernel(z, u_hbm, v_hbm, s_hbm, y_hbm, c_hbm, *rest):
    beside = rest[:z.sides]
    right_ref, left_ref, u_ref, v_ref, s_ref, y_ref, c_ref, sems = rest[z.sides:]
    is_high = lax.axis_index("normal") == z.normal - 1
    face = is_high.astype(jnp.int32)
    copies = start_all(
        [
            (u_hbm.at[:, pl.ds(0, 3)], u_ref.at[0]),
            (u_hbm.at[:, pl.ds(z.nodes - 3, 3)], u_ref.at[1]),
            (v_hbm.at[:, pl.ds(0, 2)], v_ref.at[0]),
            (v_hbm.at[:, pl.ds(z.nodes - 2, 2)], v_ref.at[1]),
            (s_hbm.at[pl.ds(0, 2)], s_ref.at[0]),
            (s_hbm.at[pl.ds(z.nodes - 2, 2)], s_ref.at[1]),
            (y_hbm, y_ref),
            (c_hbm.at[face], c_ref),
        ],
        sems,
    )
    for copy in copies:
        copy.wait()
    soft = widen_flags(y_ref[...], z.dips)
    for ref, side in ((left_ref, 0), (right_ref, 1)):
        for c in range(z.parts):
            for j in range(3):
                tile = u_ref[side, c, j]
                high = tile.astype(bf16).astype(f32)
                both = jnp.concatenate([high, tile - high], axis=0).astype(bf16)
                ref[pl.ds((c * 3 + j) * 2 * z.layers, 2 * z.layers), :] = both
            both = jnp.concatenate([v_ref[side, c, 0], v_ref[side, c, 1]], axis=0).astype(bf16)
            ref[pl.ds(z.halo_v + c * 2 * z.layers, 2 * z.layers), :] = both
        start = 0 if side == 0 else soft.shape[0] - z.layers
        part = soft[start:start + z.layers]
        both = jnp.concatenate([s_ref[side, 0] * part, s_ref[side, 1] * part], axis=0)
        ref[pl.ds(z.halo_m, 2 * z.layers), :] = both.astype(bf16)
        start = 0 if side == 0 else z.nodes - 16
        ref[pl.ds(z.halo_c, 16), :] = c_ref[pl.ds(start, 16), :].astype(f32).astype(bf16)
        pieces = []
        near = 0 if side == 0 else z.nodes - 1
        pair = 0 if side == 0 else z.nodes - 2
        for edge in beside:
            for c in range(z.parts):
                some = jnp.concatenate(
                    [edge[3 * c, pl.ds(pair, 2), :], edge[3 * c + 1, pl.ds(near, 1), :]], axis=0
                )
                high = some.astype(bf16).astype(f32)
                speed = edge[3 * z.parts + 2 * c, pl.ds(near, 1), :]
                pieces += [high, some - high, speed, edge[5 * z.parts, pl.ds(near, 1), :]]
        spare = z.halo - z.corner - 8 * z.sides * z.parts
        if spare:
            pieces.append(jnp.zeros((spare, z.dips), f32))
        ref[pl.ds(z.corner, z.halo - z.corner), :] = jnp.concatenate(pieces, axis=0).astype(bf16)


def tables_kernel(z, g_ref, s_ref, y_ref, out_ref, m_ref, wide_ref):
    me = lax.axis_index("strike")
    place, group = me % WIN, me // WIN
    for c in range(z.parts):
        line = jnp.concatenate(
            [
                g_ref[j, pl.ds(c, 1), :] + g_ref[j, pl.ds(z.parts + c, 1), :]
                for j in range(z.chunks)
            ],
            axis=1,
        ) * (1.0 / math.sqrt(z.modes))
        wide = jnp.broadcast_to(line, (z.span, z.modes))
        wide = pltpu.roll(wide, 0, 1, stride=1, stride_axis=0)
        last = jnp.broadcast_to(line, (TAIL, z.modes))
        last = pltpu.roll(last, z.modes - TAIL, 1, stride=1, stride_axis=0)
        row = lax.broadcasted_iota(jnp.int32, (TAIL, z.modes), 0)
        last = jnp.where(row < TAIL // 2, wide[z.nodes:], last)
        wide = jnp.concatenate([wide[:z.nodes], last], axis=0)
        wide = pltpu.roll(wide, place * z.nodes, 1)
        for j in range(z.chunks):
            wide_ref[j] = wide[:, j * LANES:(j + 1) * LANES]
        for s in range(z.targets):
            j = (group - (group ^ s) + z.chunks) % z.chunks
            out_ref[c, pl.ds(s * z.span, z.span), :] = wide_ref[j]
    set_modulus(z, s_ref, y_ref, m_ref)


def middle_kernel(z, toeplitz_ref, *rest):
    window, mine_ref, out_refs, stack_ref = rest[:WIN], rest[WIN], rest[WIN + 1:-1], rest[-1]
    me = lax.axis_index("strike")
    place, group = me % WIN, me // WIN
    lines = jnp.concatenate(
        [
            jnp.concatenate(
                [ref[pl.ds(z.plane_rows + j * z.chunk_rows, z.chunk_rows), :] for ref in window],
                axis=0,
            )
            for j in range(z.chunks)
        ],
        axis=1,
    )
    offset = node_offset(lax.broadcasted_iota(jnp.int32, (z.span, z.modes), 0))
    away = lax.broadcasted_iota(jnp.int32, (z.span, z.modes), 1) - offset
    away = jnp.where(away < 0, away + z.modes, away)
    away = jnp.where(away >= z.modes, away - z.modes, away)
    wanted = [
        (away == ((group ^ s) * WIN + place) * z.nodes).astype(f32) for s in range(z.targets)
    ]
    picked = lax.dot_general(
        jnp.concatenate(wanted, axis=0).astype(bf16),
        lines,
        (((1,), (1,)), ((), ())),
        preferred_element_type=f32,
    )
    row = lax.broadcasted_iota(jnp.int32, (z.chunk_rows, z.dips), 0)
    ahead = lax.broadcasted_iota(jnp.int32, (z.chunk_rows, z.dips), 1) - row
    own_rows = WIN * z.nodes
    parts = []
    for c in range(z.parts):
        inside = (row >= c * z.rows) & (row < (c + 1) * z.rows)
        for w, ref in enumerate(window):
            at = pl.multiple_of((place ^ w) * z.nodes, z.nodes)
            stack_ref[c, pl.ds(at, z.nodes), :] = ref[pl.ds(c * z.nodes, z.nodes), :]
            spot = inside & (ahead == z.rows * (me ^ w) - c * z.rows)
            at = pl.ds(own_rows + w * z.chunk_rows, z.chunk_rows)
            stack_ref[c, at, :] = spot.astype(f32).astype(bf16)
        factors = jnp.concatenate([toeplitz_ref[c], picked], axis=1).astype(bf16)
        parts.append(jnp.dot(factors, stack_ref[c], preferred_element_type=f32))
        mine_ref[pl.ds(c * z.span, z.span), :] = parts[c][:z.span]
    for s, ref in enumerate(out_refs, 1):
        ref[...] = jnp.concatenate(
            [part[s * z.span:(s + 1) * z.span] for part in parts], axis=0
        ).astype(bf16)


def unpack(z, left_ref, right_ref, uh_ref, vh_ref, mh_ref):
    size = z.layers
    for ref, at_u, at_v in ((right_ref, 0, 0), (left_ref, TAIL - 3, TAIL - 2)):
        for c in range(z.parts):
            for j in range(3):
                both = ref[pl.ds((c * 3 + j) * 2 * size, 2 * size), :].astype(f32)
                uh_ref[c, pl.ds((at_u + j) * size, size), :] = both[:size] + both[size:]
            both = ref[pl.ds(z.halo_v + c * 2 * size, 2 * size), :].astype(f32)
            vh_ref[c, pl.ds(at_v * size, 2 * size), :] = both
        mh_ref[pl.ds(at_v * size, 2 * size), :] = ref[pl.ds(z.halo_m, 2 * size), :].astype(f32)
    for c in range(z.parts):
        uh_ref[c, pl.ds(3 * size, 2 * size), :] = jnp.zeros((2 * size, z.dips), f32)
        vh_ref[c, pl.ds(2 * size, 4 * size), :] = jnp.zeros((4 * size, z.dips), f32)
    mh_ref[pl.ds(2 * size, 4 * size), :] = jnp.zeros((4 * size, z.dips), f32)


def corner_tiles(z, left_ref, right_ref, tile_ref):
    rows = pl.ds(z.corner, z.halo - z.corner)
    after, before = right_ref[rows, :].astype(f32), left_ref[rows, :].astype(f32)
    blank = jnp.zeros((TAIL, z.dips), f32)

    def tile(head, tail):
        return jnp.concatenate([head, blank[:TAIL - head.shape[0] - tail.shape[0]], tail], axis=0)

    for side in range(z.sides):
        for c in range(z.parts):
            at = 8 * (side * z.parts + c)
            a, b = after[at:at + 8], before[at:at + 8]
            head, tail = a[0:3] + a[3:6], b[0:3] + b[3:6]
            tile_ref[side, 3 * c] = tile(head[:2], tail[:2])
            tile_ref[side, 3 * c + 1] = tile(head[2:], tail[2:])
            tile_ref[side, 3 * c + 2] = blank
            tile_ref[side, 3 * z.parts + 2 * c] = tile(a[6:7], b[6:7])
            tile_ref[side, 3 * z.parts + 2 * c + 1] = blank
            if c == 0:
                tile_ref[side, 5 * z.parts] = tile(a[7:8], b[7:8])
                tile_ref[side, 5 * z.parts + 1] = blank


def in_plane(values, first_dip, last_dip):
    count, dips = values.shape
    around = pltpu.roll(values, 1, 0) + pltpu.roll(values, count - 1, 0)
    around += jnp.where(first_dip, 0.0, pltpu.roll(values, 1, 1))
    around += jnp.where(last_dip, 0.0, pltpu.roll(values, dips - 1, 1))
    return around - 6.0 * values


def base_kernel(z, u_ref, v_ref, m_ref, c_ref, left_ref, right_ref, *rest):
    sides = rest[:z.sides]
    out_u, out_v, mh_ref, ch_ref, uh_ref, vh_ref, tile_ref = rest[z.sides:]
    unpack(z, left_ref, right_ref, uh_ref, vh_ref, mh_ref)
    corner_tiles(z, left_ref, right_ref, tile_ref)
    place = lax.axis_index("normal")
    is_high = place == z.normal - 1
    is_face = (is_high | (place == 0)).astype(f32)
    row = lax.broadcasted_iota(jnp.int32, (TAIL, z.dips), 0)
    before = left_ref[pl.ds(z.halo_c, 16), :].astype(f32)[16 - TAIL:]
    after = right_ref[pl.ds(z.halo_c, 16), :].astype(f32)[:TAIL]
    own = jnp.where(is_high, c_ref[1], c_ref[0]).astype(f32)
    tail = jnp.where(row < TAIL // 2, after, before)
    ch_ref[...] = jnp.concatenate([own, tail], axis=0) * is_face
    dip = lax.broadcasted_iota(jnp.int32, (z.span, z.dips), 1)
    first_dip, last_dip = dip == 0, dip == z.dips - 1
    low = -2 if z.sides == 2 else 0
    top = z.layers

    def fetch(kind, c, f):
        if 0 <= f < top:
            layer = layer_of(z, f)
            own = {"u": u_ref, "v": v_ref, "m": m_ref}[kind]
            first = 0 if kind == "m" else c * z.stride
            tail = mh_ref if kind == "m" else (uh_ref if kind == "u" else vh_ref).at[c]
            return jnp.concatenate(
                [
                    own[pl.ds(first + layer, z.nodes, stride=top), :],
                    tail[pl.ds(layer, TAIL, stride=top), :],
                ],
                axis=0,
            )
        side, j = (0, f - top) if f >= top else (1, -1 - f)
        at = {"u": 3 * c, "v": 3 * z.parts + 2 * c, "m": 5 * z.parts}[kind] + j
        return jnp.concatenate([sides[side][at], tile_ref[side, at]], axis=0)

    def one_part(c, unused):
        u = {f: fetch("u", c, f) for f in range(low - 1 if z.sides == 2 else 0, top + 3)}
        v = {f: fetch("v", c, f) for f in range(low, top + 2)}
        for step in range(SUB):
            levels = range(low + step if z.sides == 2 else 0, top + 2 - step)
            for f in levels:
                lap = in_plane(u[f], first_dip, last_dip) + u[f + 1]
                if f - 1 in u:
                    lap += u[f - 1]
                v[f] = v[f] + time_step * (fetch("m", c, f) * lap)
            u = {f: u[f] + time_step * v[f] for f in levels}
        for f in range(top):
            at = pl.ds(c * z.stride + layer_of(z, f), z.nodes, stride=z.layers)
            out_u[at, :] = u[f][:z.nodes]
            out_v[at, :] = v[f][:z.nodes]
        return unused

    lax.fori_loop(0, z.parts, one_part, 0)


def final_kernel(z, mine_ref, contact_ref, m_ref, mh_ref, base_u, base_v, *rest):
    out_u, out_v = rest[-2:]
    dip = lax.broadcasted_iota(jnp.int32, (z.span, z.dips), 1)
    first_dip, last_dip = dip == 0, dip == z.dips - 1
    out_u[...] = base_u[...]
    out_v[...] = base_v[...]
    contact = contact_ref[...]
    m0, m1, m2 = (
        jnp.concatenate(
            [
                m_ref[pl.ds(layer_of(z, f), z.nodes, stride=z.layers), :],
                mh_ref[pl.ds(layer_of(z, f), TAIL, stride=z.layers), :],
            ],
            axis=0,
        )
        for f in range(3)
    )
    h = time_step
    arrived = [ref[...].astype(f32) for ref in rest[:-2]]
    for c in range(z.parts):
        force = mine_ref[pl.ds(c * z.span, z.span), :]
        for other in arrived:
            force = force + other[c * z.span:(c + 1) * z.span]
        force = force * contact
        v0 = h * force
        u0 = h * v0
        v1 = h * (m1 * u0)
        v0 = v0 + h * (m0 * in_plane(u0, first_dip, last_dip) + force)
        u0 = u0 + h * v0
        u1 = h * v1
        v2 = h * (m2 * u1)
        w0 = v0 + h * (m0 * (in_plane(u0, first_dip, last_dip) + u1) + force)
        v1 = v1 + h * (m1 * (in_plane(u1, first_dip, last_dip) + u0))
        pairs = ((u0 + h * w0, w0), (u1 + h * v1, v1), (h * v2, v2))
        for f, (du, dv) in enumerate(pairs):
            at = pl.ds(c * z.stride + layer_of(z, f), z.nodes, stride=z.layers)
            out_u[at, :] = out_u[at, :] + du[:z.nodes]
            out_v[at, :] = out_v[at, :] + dv[:z.nodes]


PARAMS = pltpu.CompilerParams(vmem_limit_bytes=32 * 2**20)
FIRST = pltpu.CompilerParams(vmem_limit_bytes=63 * 2**20)
HBM = pl.BlockSpec(memory_space=pltpu.HBM)


def shape(dims, kind):
    return jax.ShapeDtypeStruct(dims, kind)


def body(mesh, displacement, velocity, stiffness, yield_flags, contact, history, kernel):
    z = Sizes(mesh, displacement, history)
    u = displacement.reshape(-1, z.dips)
    v = velocity.reshape(-1, z.dips)
    s = stiffness.reshape(-1, z.dips)
    y = yield_flags.reshape(-1, yield_flags.shape[2])
    dma = pltpu.SemaphoreType.DMA
    ring = lambda step: [(i, (i + step) % z.strike) for i in range(z.strike)]
    swap = lambda mask: [(i, i ^ mask) for i in range(z.strike)]

    edge = (5 * z.parts + 2, z.nodes, z.dips)
    common, response, *edges = pl.pallas_call(
        functools.partial(common_kernel, z),
        out_shape=(shape((z.common, LANES), bf16), shape((z.chunks, 8, LANES), f32))
        + (shape(edge, f32),) * z.sides,
        in_specs=[HBM] * 7,
        out_specs=(VMEM,) * (2 + z.sides),
        scratch_shapes=[
            pltpu.VMEM(u.shape, f32),
            pltpu.VMEM((z.lags - 1, 2, z.parts, z.rows, z.modes), bf16),
            pltpu.VMEM((z.parts, z.lags, z.modes), f32),
            pltpu.VMEM((2 * z.modes, z.modes // 4), bf16),
            pltpu.VMEM(v.shape, f32),
            pltpu.VMEM(s.shape, f32),
            pltpu.VMEM(y.shape, jnp.int32),
            pltpu.VMEM((z.chunk_rows, z.modes), f32),
            pltpu.VMEM((z.chunk_rows, z.modes), f32),
            dma((7,)),
        ],
        compiler_params=FIRST,
        name="plane_and_history",
    )(u, history, kernel.transpose(0, 2, 1, 3), phase_quarter(z.modes), v, s, y)

    window = [common] + [lax.ppermute(common, "strike", swap(w)) for w in range(1, WIN)]

    if z.sides == 2:
        is_high = lax.axis_index("normal") == z.normal - 1
        above, below = edges
        steps = [(i, i + 1) for i in range(z.normal - 1)]
        from_below = lax.ppermute(above, "normal", steps)
        from_above = lax.ppermute(
            jnp.where(is_high, above, below), "normal", [(j, i) for i, j in steps]
        )
        beside = [
            jnp.where(is_high, from_below, from_above),
            jnp.where(is_high, from_above, from_below),
        ]
    else:
        beside = [lax.ppermute(edges[0], "normal", [(0, 1), (1, 0)])]

    to_right, to_left = pl.pallas_call(
        functools.partial(halo_kernel, z),
        out_shape=(shape((z.halo, LANES), bf16),) * 2,
        in_specs=[HBM] * 5 + [VMEM] * z.sides,
        out_specs=(VMEM,) * 2,
        scratch_shapes=[
            pltpu.VMEM((2, z.parts, 3, z.layers, z.dips), f32),
            pltpu.VMEM((2, z.parts, 2, z.layers, z.dips), f32),
            pltpu.VMEM((2, 2, z.layers, z.dips), f32),
            pltpu.VMEM(y.shape, jnp.int32),
            pltpu.VMEM(contact.shape[1:], jnp.int32),
            dma((8,)),
        ],
        compiler_params=PARAMS,
        name="strike_edges",
    )(displacement, velocity, stiffness, y, contact, *beside)
    from_left = lax.ppermute(to_right, "strike", ring(1))
    from_right = lax.ppermute(to_left, "strike", ring(-1))

    toeplitz, modulus = pl.pallas_call(
        functools.partial(tables_kernel, z),
        out_shape=(shape((z.parts, z.targets * z.span, LANES), f32), shape(s.shape, f32)),
        in_specs=[VMEM] * 3,
        out_specs=(VMEM,) * 2,
        scratch_shapes=[pltpu.VMEM((z.chunks, z.span, LANES), f32)],
        compiler_params=PARAMS,
        name="toeplitz_and_modulus",
    )(response, s, y)

    block = (z.parts * z.span, z.dips)
    mine, *parcels = pl.pallas_call(
        functools.partial(middle_kernel, z),
        out_shape=(shape(block, f32),) + (shape(block, bf16),) * (z.targets - 1),
        in_specs=[VMEM] * (1 + WIN),
        out_specs=(VMEM,) * z.targets,
        scratch_shapes=[pltpu.VMEM((z.parts, WIN * (z.nodes + z.chunk_rows), z.dips), bf16)],
        compiler_params=PARAMS,
        name="partial_tractions",
    )(toeplitz, *window)

    arrived = [lax.ppermute(p, "strike", swap(WIN * (k + 1))) for k, p in enumerate(parcels)]
    tail = (z.parts, TAIL * z.layers, z.dips)
    base_u, base_v, tail_modulus, touching = pl.pallas_call(
        functools.partial(base_kernel, z),
        out_shape=(
            shape(u.shape, f32),
            shape(u.shape, f32),
            shape(tail[1:], f32),
            shape((z.span, z.dips), f32),
        ),
        in_specs=[VMEM] * (6 + z.sides),
        out_specs=(VMEM,) * 4,
        scratch_shapes=[
            pltpu.VMEM(tail, f32),
            pltpu.VMEM(tail, f32),
            pltpu.VMEM((z.sides, edge[0], TAIL, z.dips), f32),
        ],
        compiler_params=PARAMS,
        name="unloaded_substeps",
    )(u, v, modulus, contact, from_left, from_right, *beside)

    moved, speed = pl.pallas_call(
        functools.partial(final_kernel, z),
        out_shape=(shape(u.shape, f32),) * 2,
        in_specs=[VMEM] * (6 + len(arrived)),
        out_specs=(VMEM,) * 2,
        compiler_params=PARAMS,
        name="add_force_response",
    )(mine, touching, modulus, tail_modulus, base_u, base_v, *arrived)
    return (moved.reshape(displacement.shape), speed.reshape(displacement.shape))


def solution(mesh):
    return jax.shard_map(
        functools.partial(body, mesh),
        mesh=mesh,
        in_specs=(
            P(None, "strike", "normal", None),
            P(None, "strike", "normal", None),
            P("strike", "normal", None),
            P("strike", "normal", None),
            P(None, "strike", None),
            P(None, None, None, None, "strike", None),
            P(),
        ),
        out_specs=(P(None, "strike", "normal", None), P(None, "strike", "normal", None)),
        check_vma=False,
    )
```

time: 34.5 us -> 25 us (0.72)
  waiting for transfers between devices: 8.54 us -> 2.41 us
  local copies, waits for them, and re-layouts: 5.1 us -> 0.52 us
  starting transfers between devices: 12.6 us -> 15.1 us
  Pallas kernels: 7.28 us -> 5.92 us
    unnamed x19 -> x14, local copies, waits for them, and re-layouts: 5.1 us -> 0.52 us
    ppermute x5 -> x7, starting transfers between devices: 5.51 us -> 9.14 us  [the longest x3 4.44 us: body(): lax.ppermute(p, 'strike', swap(WIN * (k + 1)))]
    ppermute x1, waiting for transfers between devices: 3.19 us -> 0.01 us  [body(): from_left = lax.ppermute(to_right, 'strike', ring(1))]
    ppermute x5 -> x7, waiting for transfers between devices: 5.35 us -> 2.4 us  [the longest x3 2.39 us: body(): lax.ppermute(p, 'strike', swap(WIN * (k + 1)))]
    pallas_call x1, Pallas kernels: 2.9 us -> 1.32 us  [body(): pl.pallas_call(functools.partial(base_kernel, z), out_shape=(shape(u.shap...]
    ppermute x1, starting transfers between devices: 2.99 us -> 1.93 us  [body(): from_left = lax.ppermute(to_right, 'strike', ring(1))]
  transfers between devices with their start and end apart: 7 -> 9, of which waited for: 2 -> 1; matrix products, arithmetic and copies ran while one was open for 0% -> 0% of each run, Pallas kernels for 10% -> 10%
where the time goes in v2:
time: 25 us; the launch traced here: 24.8 us
  starting transfers between devices  15.1 us (60%)
  Pallas kernels  5.92 us (24%)
  waiting for transfers between devices  2.41 us (10%)
  between operations  0.8 us (3%)
  local copies, waits for them, and re-layouts  0.52 us (2%)
    ppermute x3, starting transfers between devices, body(): lax.ppermute(p, 'strike', swap(WIN * (k + 1)))  4.44 us
    ppermute x3, starting transfers between devices, body(): lax.ppermute(common, 'strike', swap(w))  4.17 us
    ppermute x1, starting transfers between devices, body(): from_right = lax.ppermute(to_left, 'strike', ring(-1))  4.06 us
    ppermute x3, waiting for transfers between devices, body(): lax.ppermute(p, 'strike', swap(WIN * (k + 1)))  2.39 us
    pallas_call x1, Pallas kernels, body(): pl.pallas_call(functools.partial(common_kernel, z), out_shape=(shape((z.c...  2.34 us
    ppermute x1, starting transfers between devices, body(): from_left = lax.ppermute(to_right, 'strike', ring(1))  1.93 us
    pallas_call x1, Pallas kernels, body(): pl.pallas_call(functools.partial(base_kernel, z), out_shape=(shape(u.shap...  1.32 us
    pallas_call x1, Pallas kernels, body(): pl.pallas_call(functools.partial(final_kernel, z), out_shape=(shape(u.sha...  1.16 us
  transfers between devices with their start and end apart: 9, of which 1 were waited for; matrix products, arithmetic and copies ran while one was open for 0% of the time, Pallas kernels for 10%

profile of v2, /device:TPU:0, one launch (start us, length us, event | category | flops | bytes accessed | tf_op | source)
XLA Modules:
  0.0 24.8 jit_solution(10640599455574515819)
XLA Ops:
  0.6 0.0 copy-start
  0.6 0.0 copy-start.1
  0.7 0.0 copy-start.2
  0.7 0.0 copy-start.3
  0.7 0.0 copy-start.4
  0.7 2.3 %plane_and_history.1 = (bf16[224,128]{1,0:T(8,128)(2,1)}, f32[4,8,128]{2,1,0:T(8,128)}, f32[17,32,128]{2,1,0:T(8,128)}) custom-call(f32[768,128]{1,0:T(8,128)} %bitcast.7, bf16[2,8,2,3,8,512]{5,4,3,2,1,0:T(8,128)(2,1)} %h_hbm.1, f32[2,3,8,512]{3,2,1,0:T(8,128)} %bitcast.16, bf16[1024,128]{1,0:T(8,128)(2,1)} %constant.2.clone.t_hbm, f32[768,128]{1,0:T(8,128)} %bitcast.9, ...), custom_call_target="tpu_custom_call" | custom-call | tf_op jit(solution)/shard_map/plane_and_history/pallas_call | solution.py:459
  3.0 0.5 %collective-permute-start.3 = (f32[17,32,128]{2,1,0:T(8,128)}, f32[17,32,128]{2,1,0:T(8,128)S(1)}, u32[]{:S(2)}, u32[]{:S(2)}) collective-permute-start(f32[17,32,128]{2,1,0:T(8,128)} %get-tuple-element.24), channel_id=1, source_target_pairs={{0,1},{1,0},{2,3},{3,2},{4,5},{5,4},{6,7},{7,6},{8,9},{9,8},{10,11... | collective-permute-start | bytes 835592 | tf_op jit(solution)/shard_map/ppermute | solution.py:496
  3.6 3.5 %collective-permute-start.2 = (bf16[224,128]{1,0:T(8,128)(2,1)}, bf16[224,128]{1,0:T(8,128)(2,1)S(1)}, u32[]{:S(2)}, u32[]{:S(2)}) collective-permute-start(bf16[224,128]{1,0:T(8,128)(2,1)} %get-tuple-element.21.rest_0_), channel_id=1, source_target_pairs={{0,6},{2,4},{4,2},{6,0},{8,14},{10,12},{12,10},{14,8},{16,22},{18,... | collective-permute-start | bytes 172040 | tf_op jit(solution)/shard_map/ppermute | solution.py:481
  7.1 0.5 %collective-permute-start.1 = (bf16[224,128]{1,0:T(8,128)(2,1)}, bf16[224,128]{1,0:T(8,128)(2,1)S(1)}, u32[]{:S(2)}, u32[]{:S(2)}) collective-permute-start(bf16[224,128]{1,0:T(8,128)(2,1)} %get-tuple-element.21.rest_0_), channel_id=1, source_target_pairs={{0,4},{2,6},{4,0},{6,2},{8,12},{10,14},{12,8},{14,10},{16,20},{18,... | collective-permute-start | bytes 172040 | tf_op jit(solution)/shard_map/ppermute | solution.py:481
  7.6 0.1 collective-permute-start
  7.7 0.0 collective-permute-done.3.rest_0_
  7.7 0.0 copy-done
  7.7 0.0 copy-done.1
  7.7 0.0 copy-done.2
  7.7 0.0 copy-done.3
  7.8 0.0 copy-done.4
  7.8 0.0 copy-start.6
  7.8 0.4 %strike_edges.1 = (bf16[256,128]{1,0:T(8,128)(2,1)S(1)}, bf16[256,128]{1,0:T(8,128)(2,1)S(1)}) custom-call(f32[3,32,8,128]{3,2,1,0:T(8,128)S(1)} %copy-done, f32[3,32,8,128]{3,2,1,0:T(8,128)S(1)} %copy-done.1, f32[32,8,128]{2,1,0:T(8,128)S(1)} %copy-done.2, s32[64,32]{1,0:T(8,128)S(1)} %bitcast.14, s32[2,32,128]{2,1,0:T(8,128)S(1)} %copy-done.4, ...), custom_call_target="tpu_custom_call" | custom-call | tf_op jit(solution)/shard_map/strike_edges/pallas_call | solution.py:498
  8.2 1.9 %collective-permute-start.4 = (bf16[256,128]{1,0:T(8,128)(2,1)S(1)}, bf16[256,128]{1,0:T(8,128)(2,1)S(1)}, u32[]{:S(2)}, u32[]{:S(2)}) collective-permute-start(bf16[256,128]{1,0:T(8,128)(2,1)S(1)} %get-tuple-element.25), channel_id=1, source_target_pairs={{0,2},{2,4},{4,6},{6,8},{8,10},{10,12},{12,14},{14,16},{16,18},{18... | collective-permute-start | bytes 196616 | tf_op jit(solution)/shard_map/ppermute | solution.py:514
  10.1 4.1 %collective-permute-start.5 = (bf16[256,128]{1,0:T(8,128)(2,1)S(1)}, bf16[256,128]{1,0:T(8,128)(2,1)S(1)}, u32[]{:S(2)}, u32[]{:S(2)}) collective-permute-start(bf16[256,128]{1,0:T(8,128)(2,1)S(1)} %get-tuple-element.26), channel_id=1, source_target_pairs={{0,30},{2,0},{4,2},{6,4},{8,6},{10,8},{12,10},{14,12},{16,14},{18,... | collective-permute-start | bytes 196616 | tf_op jit(solution)/shard_map/ppermute | solution.py:515
  14.2 0.0 copy-done.6
  14.2 0.0 copy-start.5
  14.2 0.3 %toeplitz_and_modulus.1 = (f32[3,160,128]{2,1,0:T(8,128)S(1)}, f32[256,128]{1,0:T(8,128)S(1)}) custom-call(f32[4,8,128]{2,1,0:T(8,128)S(1)} %copy-done.6, f32[256,128]{1,0:T(8,128)S(1)} %bitcast.12, s32[64,32]{1,0:T(8,128)S(1)} %bitcast.15), custom_call_target="tpu_custom_call" | custom-call | tf_op jit(solution)/shard_map/toeplitz_and_modulus/pallas_call | solution.py:517
  14.5 0.0 collective-permute-done.2.rest_3_
  14.5 0.0 collective-permute-done.1.rest_2_
  14.5 0.0 collective-permute-done.rest_1_
  14.5 0.5 %copy-done.5 = bf16[224,128]{1,0:T(8,128)(2,1)S(1)} copy-done((bf16[224,128]{1,0:T(8,128)(2,1)S(1)}, bf16[224,128]{1,0:T(8,128)(2,1)}, u32[]{:S(2)}) %copy-start.5) | copy-done | bytes 57368
  15.0 0.4 %partial_tractions.1 = (f32[120,128]{1,0:T(8,128)S(1)}, bf16[120,128]{1,0:T(8,128)(2,1)S(1)}, bf16[120,128]{1,0:T(8,128)(2,1)S(1)}, bf16[120,128]{1,0:T(8,128)(2,1)S(1)}) custom-call(f32[3,160,128]{2,1,0:T(8,128)S(1)} %get-tuple-element.20.toeplitz_ref, bf16[224,128]{1,0:T(8,128)(2,1)S(1)} %copy-done.5, bf16[224,128]{1,0:T(8,128)(2,1)S(1)} %collective-permute-done.rest_1_, ...), custom_call_target="tpu_custom_call" | custom-call | tf_op jit(solution)/shard_map/partial_tractions/pallas_call | solution.py:528
  15.4 0.1 collective-permute-start.6
  15.5 2.4 %collective-permute-start.7 = (bf16[120,128]{1,0:T(8,128)(2,1)S(1)}, bf16[120,128]{1,0:T(8,128)(2,1)S(1)}, u32[]{:S(2)}, u32[]{:S(2)}) collective-permute-start(bf16[120,128]{1,0:T(8,128)(2,1)S(1)} %get-tuple-element.32), channel_id=1, source_target_pairs={{0,16},{2,18},{4,20},{6,22},{8,24},{10,26},{12,28},{14,30},{16,0},... | collective-permute-start | bytes 92168 | tf_op jit(solution)/shard_map/ppermute | solution.py:538
  17.9 1.9 %collective-permute-start.8 = (bf16[120,128]{1,0:T(8,128)(2,1)S(1)}, bf16[120,128]{1,0:T(8,128)(2,1)S(1)}, u32[]{:S(2)}, u32[]{:S(2)}) collective-permute-start(bf16[120,128]{1,0:T(8,128)(2,1)S(1)} %get-tuple-element.33), channel_id=1, source_target_pairs={{0,24},{2,26},{4,28},{6,30},{8,16},{10,18},{12,20},{14,22},{16,8},... | collective-permute-start | bytes 92168 | tf_op jit(solution)/shard_map/ppermute | solution.py:538
  19.9 0.0 collective-permute-done.4.left_ref
  19.9 0.0 collective-permute-done.5.right_ref
  19.9 1.3 %unloaded_substeps.1 = (f32[768,128]{1,0:T(8,128)S(1)}, f32[768,128]{1,0:T(8,128)S(1)}, f32[64,128]{1,0:T(8,128)S(1)}, f32[40,128]{1,0:T(8,128)S(1)}) custom-call(f32[768,128]{1,0:T(8,128)S(1)} %bitcast.8, f32[768,128]{1,0:T(8,128)S(1)} %bitcast.10, f32[256,128]{1,0:T(8,128)S(1)} %get-tuple-element.23.m_ref, s32[2,32,128]{2,1,0:T(8,128)S(1)} %copy-done.4, ...), custom_call_target="tpu_custom_call" | custom-call | tf_op jit(solution)/shard_map/unloaded_substeps/pallas_call | solution.py:540
  21.2 0.0 collective-permute-done.6.rest_0_
  21.2 0.0 collective-permute-done.7.rest_1_
  21.2 2.4 %collective-permute-done.8.rest_2_ = bf16[120,128]{1,0:T(8,128)(2,1)S(1)} collective-permute-done((bf16[120,128]{1,0:T(8,128)(2,1)S(1)}, bf16[120,128]{1,0:T(8,128)(2,1)S(1)}, u32[]{:S(2)}, u32[]{:S(2)}) %collective-permute-start.8) | collective-permute-done | bytes 30752 | tf_op jit(solution)/shard_map/ppermute | solution.py:538
  23.6 1.2 %add_force_response.1 = (f32[768,128]{1,0:T(8,128)}, f32[768,128]{1,0:T(8,128)}) custom-call(f32[120,128]{1,0:T(8,128)S(1)} %get-tuple-element.22.mine_ref, f32[40,128]{1,0:T(8,128)S(1)} %get-tuple-element.27.contact_ref, f32[256,128]{1,0:T(8,128)S(1)} %get-tuple-element.23.m_ref, f32[64,128]{1,0:T(8,128)S(1)} %get-tuple-element.28.mh_ref, ...), custom_call_target="tpu_custom_call" | custom-call | tf_op jit(solution)/shard_map/add_force_response/pallas_call | solution.py:559
Async XLA Ops:
  0.6 7.1 %copy-start = (f32[3,32,8,128]{3,2,1,0:T(8,128)S(1)}, f32[3,32,8,128]{3,2,1,0:T(8,128)}, u32[]{:S(2)}) copy-start(f32[3,32,8,128]{3,2,1,0:T(8,128)} %u_hbm.1) | copy-start | bytes 1179652
  0.6 7.1 %copy-start.1 = (f32[3,32,8,128]{3,2,1,0:T(8,128)S(1)}, f32[3,32,8,128]{3,2,1,0:T(8,128)}, u32[]{:S(2)}) copy-start(f32[3,32,8,128]{3,2,1,0:T(8,128)} %v_hbm.1) | copy-start | bytes 1179652
  0.7 7.1 %copy-start.2 = (f32[32,8,128]{2,1,0:T(8,128)S(1)}, f32[32,8,128]{2,1,0:T(8,128)}, u32[]{:S(2)}) copy-start(f32[32,8,128]{2,1,0:T(8,128)} %s_hbm.1) | copy-start | bytes 393220
  0.7 7.1 %copy-start.3 = (s32[8,8,32]{2,1,0:T(8,128)S(1)}, s32[8,8,32]{2,1,0:T(8,128)}, u32[]{:S(2)}) copy-start(s32[8,8,32]{2,1,0:T(8,128)} %param.11) | copy-start | bytes 24580
  0.7 7.1 %copy-start.4 = (s32[2,32,128]{2,1,0:T(8,128)S(1)}, s32[2,32,128]{2,1,0:T(8,128)}, u32[]{:S(2)}) copy-start(s32[2,32,128]{2,1,0:T(8,128)} %c_ref.1) | copy-start | bytes 98308
  3.0 4.7 %collective-permute-start.3 = (f32[17,32,128]{2,1,0:T(8,128)}, f32[17,32,128]{2,1,0:T(8,128)S(1)}, u32[]{:S(2)}, u32[]{:S(2)}) collective-permute-start(f32[17,32,128]{2,1,0:T(8,128)} %get-tuple-element.24), channel_id=1, source_target_pairs={{0,1},{1,0},{2,3},{3,2},{4,5},{5,4},{6,7},{7,6},{8,9},{9,8},{10,11... | collective-permute-start | bytes 835592 | tf_op jit(solution)/shard_map/ppermute | solution.py:496
  3.6 10.9 %collective-permute-start.2 = (bf16[224,128]{1,0:T(8,128)(2,1)}, bf16[224,128]{1,0:T(8,128)(2,1)S(1)}, u32[]{:S(2)}, u32[]{:S(2)}) collective-permute-start(bf16[224,128]{1,0:T(8,128)(2,1)} %get-tuple-element.21.rest_0_), channel_id=1, source_target_pairs={{0,6},{2,4},{4,2},{6,0},{8,14},{10,12},{12,10},{14,8},{16,22},{18,... | collective-permute-start | bytes 172040 | tf_op jit(solution)/shard_map/ppermute | solution.py:481
  7.1 7.4 %collective-permute-start.1 = (bf16[224,128]{1,0:T(8,128)(2,1)}, bf16[224,128]{1,0:T(8,128)(2,1)S(1)}, u32[]{:S(2)}, u32[]{:S(2)}) collective-permute-start(bf16[224,128]{1,0:T(8,128)(2,1)} %get-tuple-element.21.rest_0_), channel_id=1, source_target_pairs={{0,4},{2,6},{4,0},{6,2},{8,12},{10,14},{12,8},{14,10},{16,20},{18,... | collective-permute-start | bytes 172040 | tf_op jit(solution)/shard_map/ppermute | solution.py:481
  7.6 6.9 %collective-permute-start = (bf16[224,128]{1,0:T(8,128)(2,1)}, bf16[224,128]{1,0:T(8,128)(2,1)S(1)}, u32[]{:S(2)}, u32[]{:S(2)}) collective-permute-start(bf16[224,128]{1,0:T(8,128)(2,1)} %get-tuple-element.21.rest_0_), channel_id=1, source_target_pairs={{0,2},{2,0},{4,6},{6,4},{8,10},{10,8},{12,14},{14,12},{16,18},{18,... | collective-permute-start | bytes 172040 | tf_op jit(solution)/shard_map/ppermute | solution.py:481
  7.8 6.4 %copy-start.6 = (f32[4,8,128]{2,1,0:T(8,128)S(1)}, f32[4,8,128]{2,1,0:T(8,128)}, u32[]{:S(2)}) copy-start(f32[4,8,128]{2,1,0:T(8,128)} %get-tuple-element.19.g_ref) | copy-start | bytes 49156
  8.2 11.7 %collective-permute-start.4 = (bf16[256,128]{1,0:T(8,128)(2,1)S(1)}, bf16[256,128]{1,0:T(8,128)(2,1)S(1)}, u32[]{:S(2)}, u32[]{:S(2)}) collective-permute-start(bf16[256,128]{1,0:T(8,128)(2,1)S(1)} %get-tuple-element.25), channel_id=1, source_target_pairs={{0,2},{2,4},{4,6},{6,8},{8,10},{10,12},{12,14},{14,16},{16,18},{18... | collective-permute-start | bytes 196616 | tf_op jit(solution)/shard_map/ppermute | solution.py:514
  10.1 9.8 %collective-permute-start.5 = (bf16[256,128]{1,0:T(8,128)(2,1)S(1)}, bf16[256,128]{1,0:T(8,128)(2,1)S(1)}, u32[]{:S(2)}, u32[]{:S(2)}) collective-permute-start(bf16[256,128]{1,0:T(8,128)(2,1)S(1)} %get-tuple-element.26), channel_id=1, source_target_pairs={{0,30},{2,0},{4,2},{6,4},{8,6},{10,8},{12,10},{14,12},{16,14},{18,... | collective-permute-start | bytes 196616 | tf_op jit(solution)/shard_map/ppermute | solution.py:515
  14.2 0.8 %copy-start.5 = (bf16[224,128]{1,0:T(8,128)(2,1)S(1)}, bf16[224,128]{1,0:T(8,128)(2,1)}, u32[]{:S(2)}) copy-start(bf16[224,128]{1,0:T(8,128)(2,1)} %get-tuple-element.21.rest_0_) | copy-start | bytes 172036
  15.4 5.8 %collective-permute-start.6 = (bf16[120,128]{1,0:T(8,128)(2,1)S(1)}, bf16[120,128]{1,0:T(8,128)(2,1)S(1)}, u32[]{:S(2)}, u32[]{:S(2)}) collective-permute-start(bf16[120,128]{1,0:T(8,128)(2,1)S(1)} %get-tuple-element.31), channel_id=1, source_target_pairs={{0,8},{2,10},{4,12},{6,14},{8,0},{10,2},{12,4},{14,6},{16,24},{18,... | collective-permute-start | bytes 92168 | tf_op jit(solution)/shard_map/ppermute | solution.py:538
  15.5 5.7 %collective-permute-start.7 = (bf16[120,128]{1,0:T(8,128)(2,1)S(1)}, bf16[120,128]{1,0:T(8,128)(2,1)S(1)}, u32[]{:S(2)}, u32[]{:S(2)}) collective-permute-start(bf16[120,128]{1,0:T(8,128)(2,1)S(1)} %get-tuple-element.32), channel_id=1, source_target_pairs={{0,16},{2,18},{4,20},{6,22},{8,24},{10,26},{12,28},{14,30},{16,0},... | collective-permute-start | bytes 92168 | tf_op jit(solution)/shard_map/ppermute | solution.py:538
  17.9 5.7 %collective-permute-start.8 = (bf16[120,128]{1,0:T(8,128)(2,1)S(1)}, bf16[120,128]{1,0:T(8,128)(2,1)S(1)}, u32[]{:S(2)}, u32[]{:S(2)}) collective-permute-start(bf16[120,128]{1,0:T(8,128)(2,1)S(1)} %get-tuple-element.33), channel_id=1, source_target_pairs={{0,24},{2,26},{4,28},{6,30},{8,16},{10,18},{12,20},{14,22},{16,8},... | collective-permute-start | bytes 92168 | tf_op jit(solution)/shard_map/ppermute | solution.py:538

commit v3 on v2

--- a/solution.py
+++ b/solution.py
@@ -218,7 +218,7 @@
         ref[pl.ds(z.corner, z.halo - z.corner), :] = jnp.concatenate(pieces, axis=0).astype(bf16)
 
 
-def tables_kernel(z, g_ref, s_ref, y_ref, out_ref, m_ref, wide_ref):
+def toeplitz_kernel(z, g_ref, out_ref, wide_ref):
     me = lax.axis_index("strike")
     place, group = me % WIN, me // WIN
     for c in range(z.parts):
@@ -242,7 +242,6 @@
         for s in range(z.targets):
             j = (group - (group ^ s) + z.chunks) % z.chunks
             out_ref[c, pl.ds(s * z.span, z.span), :] = wide_ref[j]
-    set_modulus(z, s_ref, y_ref, m_ref)
 
 
 def middle_kernel(z, toeplitz_ref, *rest):
@@ -340,9 +339,10 @@
     return around - 6.0 * values
 
 
-def base_kernel(z, u_ref, v_ref, m_ref, c_ref, left_ref, right_ref, *rest):
+def base_kernel(z, u_ref, v_ref, s_ref, y_ref, c_ref, left_ref, right_ref, *rest):
     sides = rest[:z.sides]
-    out_u, out_v, mh_ref, ch_ref, uh_ref, vh_ref, tile_ref = rest[z.sides:]
+    out_u, out_v, mf_ref, ch_ref, m_ref, uh_ref, vh_ref, mh_ref, tile_ref = rest[z.sides:]
+    set_modulus(z, s_ref, y_ref, m_ref)
     unpack(z, left_ref, right_ref, uh_ref, vh_ref, mh_ref)
     corner_tiles(z, left_ref, right_ref, tile_ref)
     place = lax.axis_index("normal")
@@ -394,27 +394,19 @@
         return unused
 
     lax.fori_loop(0, z.parts, one_part, 0)
-
-
-def final_kernel(z, mine_ref, contact_ref, m_ref, mh_ref, base_u, base_v, *rest):
-    out_u, out_v = rest[-2:]
+    for f in range(3):
+        mf_ref[f] = fetch("m", 0, f)
+
+
+def final_kernel(z, mine_ref, contact_ref, m_ref, base_u, base_v, *rest):
+    arrived, (out_u, out_v, u_ref, v_ref, sems) = rest[:-5], rest[-5:]
     dip = lax.broadcasted_iota(jnp.int32, (z.span, z.dips), 1)
     first_dip, last_dip = dip == 0, dip == z.dips - 1
-    out_u[...] = base_u[...]
-    out_v[...] = base_v[...]
     contact = contact_ref[...]
-    m0, m1, m2 = (
-        jnp.concatenate(
-            [
-                m_ref[pl.ds(layer_of(z, f), z.nodes, stride=z.layers), :],
-                mh_ref[pl.ds(layer_of(z, f), TAIL, stride=z.layers), :],
-            ],
-            axis=0,
-        )
-        for f in range(3)
-    )
+    m0, m1, m2 = m_ref[0], m_ref[1], m_ref[2]
     h = time_step
-    arrived = [ref[...].astype(f32) for ref in rest[:-2]]
+    arrived = [ref[...].astype(f32) for ref in arrived]
+    copies = []
     for c in range(z.parts):
         force = mine_ref[pl.ds(c * z.span, z.span), :]
         for other in arrived:
@@ -430,15 +422,27 @@
         w0 = v0 + h * (m0 * (in_plane(u0, first_dip, last_dip) + u1) + force)
         v1 = v1 + h * (m1 * (in_plane(u1, first_dip, last_dip) + u0))
         pairs = ((u0 + h * w0, w0), (u1 + h * v1, v1), (h * v2, v2))
-        for f, (du, dv) in enumerate(pairs):
-            at = pl.ds(c * z.stride + layer_of(z, f), z.nodes, stride=z.layers)
-            out_u[at, :] = out_u[at, :] + du[:z.nodes]
-            out_v[at, :] = out_v[at, :] + dv[:z.nodes]
+        part = pl.ds(c * z.stride, z.stride)
+        for k, (base, sums, out) in enumerate(((base_u, u_ref, out_u), (base_v, v_ref, out_v))):
+            sums[part, :] = base[part, :]
+            for f in range(3):
+                at = pl.ds(c * z.stride + layer_of(z, f), z.nodes, stride=z.layers)
+                sums[at, :] = sums[at, :] + pairs[f][k][:z.nodes]
+            copies.append(
+                pltpu.make_async_copy(sums.at[part, :], out.at[part, :], sems.at[2 * c + k])
+            )
+            copies[-1].start()
+    for copy in copies:
+        copy.wait()
 
 
 PARAMS = pltpu.CompilerParams(vmem_limit_bytes=32 * 2**20)
-FIRST = pltpu.CompilerParams(vmem_limit_bytes=63 * 2**20)
+FIRST = pltpu.CompilerParams(vmem_limit_bytes=32 * 2**20)
 HBM = pl.BlockSpec(memory_space=pltpu.HBM)
+
+
+def in_hbm(*arrays):
+    return [pltpu.with_memory_space_constraint(x, pltpu.HBM) for x in arrays]
 
 
 def shape(dims, kind):
@@ -476,7 +480,7 @@
         ],
         compiler_params=FIRST,
         name="plane_and_history",
-    )(u, history, kernel.transpose(0, 2, 1, 3), phase_quarter(z.modes), v, s, y)
+    )(*in_hbm(u, history, kernel.transpose(0, 2, 1, 3), phase_quarter(z.modes), v, s, y))
 
     window = [common] + [lax.ppermute(common, "strike", swap(w)) for w in range(1, WIN)]
 
@@ -514,15 +518,15 @@
     from_left = lax.ppermute(to_right, "strike", ring(1))
     from_right = lax.ppermute(to_left, "strike", ring(-1))
 
-    toeplitz, modulus = pl.pallas_call(
-        functools.partial(tables_kernel, z),
-        out_shape=(shape((z.parts, z.targets * z.span, LANES), f32), shape(s.shape, f32)),
-        in_specs=[VMEM] * 3,
-        out_specs=(VMEM,) * 2,
+    toeplitz = pl.pallas_call(
+        functools.partial(toeplitz_kernel, z),
+        out_shape=shape((z.parts, z.targets * z.span, LANES), f32),
+        in_specs=[VMEM],
+        out_specs=VMEM,
         scratch_shapes=[pltpu.VMEM((z.chunks, z.span, LANES), f32)],
         compiler_params=PARAMS,
-        name="toeplitz_and_modulus",
-    )(response, s, y)
+        name="toeplitz",
+    )(response)
 
     block = (z.parts * z.span, z.dips)
     mine, *parcels = pl.pallas_call(
@@ -535,35 +539,40 @@
         name="partial_tractions",
     )(toeplitz, *window)
 
-    arrived = [lax.ppermute(p, "strike", swap(WIN * (k + 1))) for k, p in enumerate(parcels)]
+    arrived = [
+        lax.ppermute(p, "strike", swap(WIN * (k + 1))) for k, p in reversed(list(enumerate(parcels)))
+    ]
     tail = (z.parts, TAIL * z.layers, z.dips)
-    base_u, base_v, tail_modulus, touching = pl.pallas_call(
+    base_u, base_v, face_modulus, touching = pl.pallas_call(
         functools.partial(base_kernel, z),
         out_shape=(
             shape(u.shape, f32),
             shape(u.shape, f32),
-            shape(tail[1:], f32),
+            shape((3, z.span, z.dips), f32),
             shape((z.span, z.dips), f32),
         ),
-        in_specs=[VMEM] * (6 + z.sides),
+        in_specs=[VMEM] * (7 + z.sides),
         out_specs=(VMEM,) * 4,
         scratch_shapes=[
+            pltpu.VMEM(s.shape, f32),
             pltpu.VMEM(tail, f32),
             pltpu.VMEM(tail, f32),
+            pltpu.VMEM(tail[1:], f32),
             pltpu.VMEM((z.sides, edge[0], TAIL, z.dips), f32),
         ],
         compiler_params=PARAMS,
         name="unloaded_substeps",
-    )(u, v, modulus, contact, from_left, from_right, *beside)
+    )(u, v, s, y, contact, from_left, from_right, *beside)
 
     moved, speed = pl.pallas_call(
         functools.partial(final_kernel, z),
         out_shape=(shape(u.shape, f32),) * 2,
-        in_specs=[VMEM] * (6 + len(arrived)),
-        out_specs=(VMEM,) * 2,
+        in_specs=[VMEM] * (5 + len(arrived)),
+        out_specs=(HBM,) * 2,
+        scratch_shapes=[pltpu.VMEM(u.shape, f32), pltpu.VMEM(u.shape, f32), dma((2 * z.parts,))],
         compiler_params=PARAMS,
         name="add_force_response",
-    )(mine, touching, modulus, tail_modulus, base_u, base_v, *arrived)
+    )(mine, touching, face_modulus, base_u, base_v, *arrived)
     return (moved.reshape(displacement.shape), speed.reshape(displacement.shape))
 
 

time: 25 us -> 22.2 us (0.89)
  waiting for transfers between devices: 2.41 us -> 0.84 us
  Pallas kernels: 5.92 us -> 5.3 us
  local copies, waits for them, and re-layouts: 0.52 us -> 0.02 us
    ppermute x3, waiting for transfers between devices: 2.39 us -> 0.82 us  [body(): lax.ppermute(p, 'strike', swap(WIN * (k + 1)))]
    pallas_call x1, Pallas kernels: 2.34 us -> 1.64 us  [body(): pl.pallas_call(functools.partial(common_kernel, z), out_shape=(shape((z.c...]
    unnamed x14 -> x10, local copies, waits for them, and re-layouts: 0.52 us -> 0.02 us
  transfers between devices with their start and end apart: 9 -> 9, of which waited for: 1 -> 2; matrix products, arithmetic and copies ran while one was open for 0% -> 0% of each run, Pallas kernels for 10% -> 12%
where the time goes in v3:
time: 22.2 us; the launch traced here: 22.1 us
  starting transfers between devices  15.1 us (68%)
  Pallas kernels  5.3 us (24%)
  waiting for transfers between devices  0.84 us (4%)
  between operations  0.77 us (3%)
    ppermute x3, starting transfers between devices, body(): lax.ppermute(p, 'strike', swap(WIN * (k + 1)))  4.45 us
    ppermute x3, starting transfers between devices, body(): lax.ppermute(common, 'strike', swap(w))  4.16 us
    ppermute x1, starting transfers between devices, body(): from_right = lax.ppermute(to_left, 'strike', ring(-1))  4.06 us
    ppermute x1, starting transfers between devices, body(): from_left = lax.ppermute(to_right, 'strike', ring(1))  1.94 us
    pallas_call x1, Pallas kernels, body(): pl.pallas_call(functools.partial(common_kernel, z), out_shape=(shape((z.c...  1.64 us
    pallas_call x1, Pallas kernels, body(): pl.pallas_call(functools.partial(base_kernel, z), out_shape=(shape(u.shap...  1.45 us
    pallas_call x1, Pallas kernels, body(): pl.pallas_call(functools.partial(final_kernel, z), out_shape=(shape(u.sha...  1.11 us
    ppermute x3, waiting for transfers between devices, body(): lax.ppermute(p, 'strike', swap(WIN * (k + 1)))  0.82 us
  transfers between devices with their start and end apart: 9, of which 2 were waited for; matrix products, arithmetic and copies ran while one was open for 0% of the time, Pallas kernels for 12%

profile of v3, /device:TPU:0, one launch (start us, length us, event | category | flops | bytes accessed | tf_op | source)
XLA Modules:
  0.0 22.1 jit_solution(8067730824324582873)
XLA Ops:
  0.6 0.0 copy-start
  0.6 0.0 copy-start.1
  0.7 0.0 copy-start.2
  0.7 0.0 copy-start.3
  0.7 0.0 copy-start.4
  0.7 1.6 %plane_and_history.1 = (bf16[224,128]{1,0:T(8,128)(2,1)S(1)}, f32[4,8,128]{2,1,0:T(8,128)S(1)}, f32[17,32,128]{2,1,0:T(8,128)S(1)}) custom-call(f32[768,128]{1,0:T(8,128)} %bitcast.7, bf16[2,8,2,3,8,512]{5,4,3,2,1,0:T(8,128)(2,1)} %h_hbm.1, f32[2,3,8,512]{3,2,1,0:T(8,128)} %bitcast.16, bf16[1024,128]{1,0:T(8,128)(2,1)} %constant.2.clone.t_hbm, ...), custom_call_target="tpu_custom_call" | custom-call | tf_op jit(solution)/shard_map/plane_and_history/pallas_call | solution.py:463
  2.3 0.5 %collective-permute-start.3 = (f32[17,32,128]{2,1,0:T(8,128)S(1)}, f32[17,32,128]{2,1,0:T(8,128)S(1)}, u32[]{:S(2)}, u32[]{:S(2)}) collective-permute-start(f32[17,32,128]{2,1,0:T(8,128)S(1)} %get-tuple-element.20), channel_id=1, source_target_pairs={{0,1},{1,0},{2,3},{3,2},{4,5},{5,4},{6,7},{7,6},{8,9},{9,8},{10,11... | collective-permute-start | bytes 835592 | tf_op jit(solution)/shard_map/ppermute | solution.py:500
  2.9 3.5 %collective-permute-start.2 = (bf16[224,128]{1,0:T(8,128)(2,1)S(1)}, bf16[224,128]{1,0:T(8,128)(2,1)S(1)}, u32[]{:S(2)}, u32[]{:S(2)}) collective-permute-start(bf16[224,128]{1,0:T(8,128)(2,1)S(1)} %get-tuple-element.18.rest_0_), channel_id=1, source_target_pairs={{0,6},{2,4},{4,2},{6,0},{8,14},{10,12},{12,10},{14,8},{16,22},{18,... | collective-permute-start | bytes 172040 | tf_op jit(solution)/shard_map/ppermute | solution.py:485
  6.4 0.5 %collective-permute-start.1 = (bf16[224,128]{1,0:T(8,128)(2,1)S(1)}, bf16[224,128]{1,0:T(8,128)(2,1)S(1)}, u32[]{:S(2)}, u32[]{:S(2)}) collective-permute-start(bf16[224,128]{1,0:T(8,128)(2,1)S(1)} %get-tuple-element.18.rest_0_), channel_id=1, source_target_pairs={{0,4},{2,6},{4,0},{6,2},{8,12},{10,14},{12,8},{14,10},{16,20},{18,... | collective-permute-start | bytes 172040 | tf_op jit(solution)/shard_map/ppermute | solution.py:485
  6.9 0.1 collective-permute-start
  7.0 0.0 collective-permute-done.3.rest_0_
  7.0 0.0 copy-done
  7.0 0.0 copy-done.1
  7.0 0.0 copy-done.2
  7.0 0.0 copy-done.3
  7.0 0.0 copy-done.4
  7.1 0.4 %strike_edges.1 = (bf16[256,128]{1,0:T(8,128)(2,1)S(1)}, bf16[256,128]{1,0:T(8,128)(2,1)S(1)}) custom-call(f32[3,32,8,128]{3,2,1,0:T(8,128)S(1)} %copy-done, f32[3,32,8,128]{3,2,1,0:T(8,128)S(1)} %copy-done.1, f32[32,8,128]{2,1,0:T(8,128)S(1)} %copy-done.2, s32[64,32]{1,0:T(8,128)S(1)} %bitcast.14, s32[2,32,128]{2,1,0:T(8,128)S(1)} %copy-done.4, ...), custom_call_target="tpu_custom_call" | custom-call | tf_op jit(solution)/shard_map/strike_edges/pallas_call | solution.py:502
  7.4 1.9 %collective-permute-start.4 = (bf16[256,128]{1,0:T(8,128)(2,1)S(1)}, bf16[256,128]{1,0:T(8,128)(2,1)S(1)}, u32[]{:S(2)}, u32[]{:S(2)}) collective-permute-start(bf16[256,128]{1,0:T(8,128)(2,1)S(1)} %get-tuple-element.21), channel_id=1, source_target_pairs={{0,2},{2,4},{4,6},{6,8},{8,10},{10,12},{12,14},{14,16},{16,18},{18... | collective-permute-start | bytes 196616 | tf_op jit(solution)/shard_map/ppermute | solution.py:518
  9.4 4.1 %collective-permute-start.5 = (bf16[256,128]{1,0:T(8,128)(2,1)S(1)}, bf16[256,128]{1,0:T(8,128)(2,1)S(1)}, u32[]{:S(2)}, u32[]{:S(2)}) collective-permute-start(bf16[256,128]{1,0:T(8,128)(2,1)S(1)} %get-tuple-element.22), channel_id=1, source_target_pairs={{0,30},{2,0},{4,2},{6,4},{8,6},{10,8},{12,10},{14,12},{16,14},{18,... | collective-permute-start | bytes 196616 | tf_op jit(solution)/shard_map/ppermute | solution.py:519
  13.4 0.3 %toeplitz.1.toeplitz_ref = f32[3,160,128]{2,1,0:T(8,128)S(1)} custom-call(f32[4,8,128]{2,1,0:T(8,128)S(1)} %get-tuple-element.17.g_ref), custom_call_target="tpu_custom_call" | custom-call | tf_op jit(solution)/shard_map/toeplitz/pallas_call | solution.py:521
  13.7 0.0 collective-permute-done.2.rest_3_
  13.7 0.0 collective-permute-done.1.rest_2_
  13.8 0.0 collective-permute-done.rest_1_
  13.8 0.4 %partial_tractions.1 = (f32[120,128]{1,0:T(8,128)S(1)}, bf16[120,128]{1,0:T(8,128)(2,1)S(1)}, bf16[120,128]{1,0:T(8,128)(2,1)S(1)}, bf16[120,128]{1,0:T(8,128)(2,1)S(1)}) custom-call(f32[3,160,128]{2,1,0:T(8,128)S(1)} %toeplitz.1.toeplitz_ref, bf16[224,128]{1,0:T(8,128)(2,1)S(1)} %get-tuple-element.18.rest_0_, ...), custom_call_target="tpu_custom_call" | custom-call | tf_op jit(solution)/shard_map/partial_tractions/pallas_call | solution.py:532
  14.2 1.9 %collective-permute-start.6 = (bf16[120,128]{1,0:T(8,128)(2,1)S(1)}, bf16[120,128]{1,0:T(8,128)(2,1)S(1)}, u32[]{:S(2)}, u32[]{:S(2)}) collective-permute-start(bf16[120,128]{1,0:T(8,128)(2,1)S(1)} %get-tuple-element.27), channel_id=1, source_target_pairs={{0,24},{2,26},{4,28},{6,30},{8,16},{10,18},{12,20},{14,22},{16,8},... | collective-permute-start | bytes 92168 | tf_op jit(solution)/shard_map/ppermute | solution.py:543
  16.2 0.0 collective-permute-start.7
  16.2 2.5 %collective-permute-start.8 = (bf16[120,128]{1,0:T(8,128)(2,1)S(1)}, bf16[120,128]{1,0:T(8,128)(2,1)S(1)}, u32[]{:S(2)}, u32[]{:S(2)}) collective-permute-start(bf16[120,128]{1,0:T(8,128)(2,1)S(1)} %get-tuple-element.29), channel_id=1, source_target_pairs={{0,8},{2,10},{4,12},{6,14},{8,0},{10,2},{12,4},{14,6},{16,24},{18,... | collective-permute-start | bytes 92168 | tf_op jit(solution)/shard_map/ppermute | solution.py:543
  18.7 0.0 collective-permute-done.4.left_ref
  18.7 0.0 collective-permute-done.5.right_ref
  18.7 1.4 %unloaded_substeps.1 = (f32[768,128]{1,0:T(8,128)S(1)}, f32[768,128]{1,0:T(8,128)S(1)}, f32[3,40,128]{2,1,0:T(8,128)S(1)}, f32[40,128]{1,0:T(8,128)S(1)}) custom-call(f32[768,128]{1,0:T(8,128)S(1)} %bitcast.8, f32[768,128]{1,0:T(8,128)S(1)} %bitcast.10, f32[256,128]{1,0:T(8,128)S(1)} %bitcast.12, s32[64,32]{1,0:T(8,128)S(1)} %bitcast.15, ...), custom_call_target="tpu_custom_call" | custom-call | tf_op jit(solution)/shard_map/unloaded_substeps/pallas_call | solution.py:546
  20.1 0.1 collective-permute-done.6.rest_0_
  20.3 0.7 %collective-permute-done.7.rest_1_ = bf16[120,128]{1,0:T(8,128)(2,1)S(1)} collective-permute-done((bf16[120,128]{1,0:T(8,128)(2,1)S(1)}, bf16[120,128]{1,0:T(8,128)(2,1)S(1)}, u32[]{:S(2)}, u32[]{:S(2)}) %collective-permute-start.7) | collective-permute-done | bytes 30752 | tf_op jit(solution)/shard_map/ppermute | solution.py:543
  20.9 0.0 collective-permute-done.8.rest_2_
  21.0 1.1 %add_force_response.1 = (f32[768,128]{1,0:T(8,128)}, f32[768,128]{1,0:T(8,128)}) custom-call(f32[120,128]{1,0:T(8,128)S(1)} %get-tuple-element.19.mine_ref, f32[40,128]{1,0:T(8,128)S(1)} %get-tuple-element.23.contact_ref, f32[3,40,128]{2,1,0:T(8,128)S(1)} %get-tuple-element.24.m_ref, f32[768,128]{1,0:T(8,128)S(1)} %get-tuple-element.25.base_u, ...), custom_call_target="tpu_custom_call" | custom-call | tf_op jit(solution)/shard_map/add_force_response/pallas_call | solution.py:567
Async XLA Ops:
  0.6 6.4 %copy-start = (f32[3,32,8,128]{3,2,1,0:T(8,128)S(1)}, f32[3,32,8,128]{3,2,1,0:T(8,128)}, u32[]{:S(2)}) copy-start(f32[3,32,8,128]{3,2,1,0:T(8,128)} %u_hbm.1) | copy-start | bytes 1179652
  0.6 6.4 %copy-start.1 = (f32[3,32,8,128]{3,2,1,0:T(8,128)S(1)}, f32[3,32,8,128]{3,2,1,0:T(8,128)}, u32[]{:S(2)}) copy-start(f32[3,32,8,128]{3,2,1,0:T(8,128)} %v_hbm.1) | copy-start | bytes 1179652
  0.7 6.4 %copy-start.2 = (f32[32,8,128]{2,1,0:T(8,128)S(1)}, f32[32,8,128]{2,1,0:T(8,128)}, u32[]{:S(2)}) copy-start(f32[32,8,128]{2,1,0:T(8,128)} %s_hbm.1) | copy-start | bytes 393220
  0.7 6.4 %copy-start.3 = (s32[8,8,32]{2,1,0:T(8,128)S(1)}, s32[8,8,32]{2,1,0:T(8,128)}, u32[]{:S(2)}) copy-start(s32[8,8,32]{2,1,0:T(8,128)} %param.11) | copy-start | bytes 24580
  0.7 6.4 %copy-start.4 = (s32[2,32,128]{2,1,0:T(8,128)S(1)}, s32[2,32,128]{2,1,0:T(8,128)}, u32[]{:S(2)}) copy-start(s32[2,32,128]{2,1,0:T(8,128)} %c_ref.1) | copy-start | bytes 98308
  2.3 4.7 %collective-permute-start.3 = (f32[17,32,128]{2,1,0:T(8,128)S(1)}, f32[17,32,128]{2,1,0:T(8,128)S(1)}, u32[]{:S(2)}, u32[]{:S(2)}) collective-permute-start(f32[17,32,128]{2,1,0:T(8,128)S(1)} %get-tuple-element.20), channel_id=1, source_target_pairs={{0,1},{1,0},{2,3},{3,2},{4,5},{5,4},{6,7},{7,6},{8,9},{9,8},{10,11... | collective-permute-start | bytes 835592 | tf_op jit(solution)/shard_map/ppermute | solution.py:500
  2.9 10.9 %collective-permute-start.2 = (bf16[224,128]{1,0:T(8,128)(2,1)S(1)}, bf16[224,128]{1,0:T(8,128)(2,1)S(1)}, u32[]{:S(2)}, u32[]{:S(2)}) collective-permute-start(bf16[224,128]{1,0:T(8,128)(2,1)S(1)} %get-tuple-element.18.rest_0_), channel_id=1, source_target_pairs={{0,6},{2,4},{4,2},{6,0},{8,14},{10,12},{12,10},{14,8},{16,22},{18,... | collective-permute-start | bytes 172040 | tf_op jit(solution)/shard_map/ppermute | solution.py:485
  6.4 7.4 %collective-permute-start.1 = (bf16[224,128]{1,0:T(8,128)(2,1)S(1)}, bf16[224,128]{1,0:T(8,128)(2,1)S(1)}, u32[]{:S(2)}, u32[]{:S(2)}) collective-permute-start(bf16[224,128]{1,0:T(8,128)(2,1)S(1)} %get-tuple-element.18.rest_0_), channel_id=1, source_target_pairs={{0,4},{2,6},{4,0},{6,2},{8,12},{10,14},{12,8},{14,10},{16,20},{18,... | collective-permute-start | bytes 172040 | tf_op jit(solution)/shard_map/ppermute | solution.py:485
  6.9 6.9 %collective-permute-start = (bf16[224,128]{1,0:T(8,128)(2,1)S(1)}, bf16[224,128]{1,0:T(8,128)(2,1)S(1)}, u32[]{:S(2)}, u32[]{:S(2)}) collective-permute-start(bf16[224,128]{1,0:T(8,128)(2,1)S(1)} %get-tuple-element.18.rest_0_), channel_id=1, source_target_pairs={{0,2},{2,0},{4,6},{6,4},{8,10},{10,8},{12,14},{14,12},{16,18},{18,... | collective-permute-start | bytes 172040 | tf_op jit(solution)/shard_map/ppermute | solution.py:485
  7.4 11.2 %collective-permute-start.4 = (bf16[256,128]{1,0:T(8,128)(2,1)S(1)}, bf16[256,128]{1,0:T(8,128)(2,1)S(1)}, u32[]{:S(2)}, u32[]{:S(2)}) collective-permute-start(bf16[256,128]{1,0:T(8,128)(2,1)S(1)} %get-tuple-element.21), channel_id=1, source_target_pairs={{0,2},{2,4},{4,6},{6,8},{8,10},{10,12},{12,14},{14,16},{16,18},{18... | collective-permute-start | bytes 196616 | tf_op jit(solution)/shard_map/ppermute | solution.py:518
  9.4 9.3 %collective-permute-start.5 = (bf16[256,128]{1,0:T(8,128)(2,1)S(1)}, bf16[256,128]{1,0:T(8,128)(2,1)S(1)}, u32[]{:S(2)}, u32[]{:S(2)}) collective-permute-start(bf16[256,128]{1,0:T(8,128)(2,1)S(1)} %get-tuple-element.22), channel_id=1, source_target_pairs={{0,30},{2,0},{4,2},{6,4},{8,6},{10,8},{12,10},{14,12},{16,14},{18,... | collective-permute-start | bytes 196616 | tf_op jit(solution)/shard_map/ppermute | solution.py:519
  14.2 6.0 %collective-permute-start.6 = (bf16[120,128]{1,0:T(8,128)(2,1)S(1)}, bf16[120,128]{1,0:T(8,128)(2,1)S(1)}, u32[]{:S(2)}, u32[]{:S(2)}) collective-permute-start(bf16[120,128]{1,0:T(8,128)(2,1)S(1)} %get-tuple-element.27), channel_id=1, source_target_pairs={{0,24},{2,26},{4,28},{6,30},{8,16},{10,18},{12,20},{14,22},{16,8},... | collective-permute-start | bytes 92168 | tf_op jit(solution)/shard_map/ppermute | solution.py:543
  16.2 4.8 %collective-permute-start.7 = (bf16[120,128]{1,0:T(8,128)(2,1)S(1)}, bf16[120,128]{1,0:T(8,128)(2,1)S(1)}, u32[]{:S(2)}, u32[]{:S(2)}) collective-permute-start(bf16[120,128]{1,0:T(8,128)(2,1)S(1)} %get-tuple-element.28), channel_id=1, source_target_pairs={{0,16},{2,18},{4,20},{6,22},{8,24},{10,26},{12,28},{14,30},{16,0},... | collective-permute-start | bytes 92168 | tf_op jit(solution)/shard_map/ppermute | solution.py:543
  16.2 4.8 %collective-permute-start.8 = (bf16[120,128]{1,0:T(8,128)(2,1)S(1)}, bf16[120,128]{1,0:T(8,128)(2,1)S(1)}, u32[]{:S(2)}, u32[]{:S(2)}) collective-permute-start(bf16[120,128]{1,0:T(8,128)(2,1)S(1)} %get-tuple-element.29), channel_id=1, source_target_pairs={{0,8},{2,10},{4,12},{6,14},{8,0},{10,2},{12,4},{14,6},{16,24},{18,... | collective-permute-start | bytes 92168 | tf_op jit(solution)/shard_map/ppermute | solution.py:543

commit v4 on v3

--- a/solution.py
+++ b/solution.py
@@ -44,7 +44,7 @@
         self.spectral = round_up(self.parts * self.rows, 8)
         self.chunk_rows = round_up(self.spectral + 2 * self.parts, 16)
         self.plane_rows = self.parts * self.nodes
-        self.common = self.plane_rows + self.chunks * self.chunk_rows
+        self.common = self.plane_rows + 2 * self.spectral
         self.halo_v = self.parts * 3 * 2 * self.layers
         self.halo_m = self.halo_v + self.parts * 2 * self.layers
         self.halo_c = self.halo_m + 2 * self.layers
@@ -74,6 +74,12 @@
     return jnp.where(is_high, z.layers - 1 - level, level)
 
 
+def beside_me(place):
+    turn = place ^ (place >> 1)
+    ahead, behind = (turn + 1) % WIN, (turn + WIN - 1) % WIN
+    return (place, ahead ^ (ahead >> 1), behind ^ (behind >> 1), place ^ 3)
+
+
 def start_all(pairs, sems):
     copies = [pltpu.make_async_copy(a, b, sems.at[i]) for i, (a, b) in enumerate(pairs)]
     for copy in copies:
@@ -90,8 +96,8 @@
 
 
 def common_kernel(z, u_hbm, h_hbm, k_hbm, t_hbm, v_hbm, s_hbm, y_hbm, out_ref, g_ref, *rest):
-    edges = rest[:z.sides]
-    u_ref, h_ref, k_ref, t_ref, v_ref, s_ref, y_ref, re_ref, im_ref, sems = rest[z.sides:]
+    edges, others = rest[:z.sides], rest[z.sides:z.sides + z.targets - 1]
+    u_ref, h_ref, k_ref, t_ref, v_ref, s_ref, y_ref, re_ref, im_ref, line_ref, sems = rest[-11:]
     is_high = lax.axis_index("normal") == z.normal - 1
     face = is_high.astype(jnp.int32)
     copies = start_all(
@@ -142,13 +148,23 @@
         for q in range(per_quarter):
             piece = lines[m * z.chunk_rows:(m + 1) * z.chunk_rows, q * LANES:(q + 1) * LANES]
             chunk = m * per_quarter + q
-            out_ref[pl.ds(z.plane_rows + chunk * z.chunk_rows, z.chunk_rows), :] = piece.astype(bf16)
+            line_ref[chunk] = piece[:z.spectral]
             g_ref[chunk] = piece[z.spectral:z.spectral + 8]
+    group = lax.axis_index("strike") // WIN
+    lane = lax.broadcasted_iota(jnp.int32, (z.spectral, LANES), 1)
+    for s, ref in enumerate((out_ref,) + others):
+        chunk = (group + s) % z.targets
+        after, before = line_ref[(chunk + 1) % z.chunks], line_ref[(chunk + z.chunks - 1) % z.chunks]
+        both = jnp.concatenate(
+            [line_ref[chunk], jnp.where(lane < LANES // 2, after, before)], axis=0
+        )
+        ref[pl.ds(z.plane_rows, 2 * z.spectral), :] = both.astype(bf16)
     copies[3].wait()
     layer = face * (z.layers - 1)
     for c in range(z.parts):
-        plane = u_ref[pl.ds(c * z.stride + layer, z.nodes, stride=z.layers), :]
-        out_ref[pl.ds(c * z.nodes, z.nodes), :] = plane.astype(bf16)
+        plane = u_ref[pl.ds(c * z.stride + layer, z.nodes, stride=z.layers), :].astype(bf16)
+        for ref in (out_ref,) + others:
+            ref[pl.ds(c * z.nodes, z.nodes), :] = plane
     for copy in copies[4:]:
         copy.wait()
     set_modulus(z, s_ref, y_ref, s_ref)
@@ -165,62 +181,10 @@
                 out[5 * z.parts + j] = s_ref[pl.ds(layer, z.nodes, stride=size), :]
 
 
-def halo_kernel(z, u_hbm, v_hbm, s_hbm, y_hbm, c_hbm, *rest):
-    beside = rest[:z.sides]
-    right_ref, left_ref, u_ref, v_ref, s_ref, y_ref, c_ref, sems = rest[z.sides:]
-    is_high = lax.axis_index("normal") == z.normal - 1
-    face = is_high.astype(jnp.int32)
-    copies = start_all(
-        [
-            (u_hbm.at[:, pl.ds(0, 3)], u_ref.at[0]),
-            (u_hbm.at[:, pl.ds(z.nodes - 3, 3)], u_ref.at[1]),
-            (v_hbm.at[:, pl.ds(0, 2)], v_ref.at[0]),
-            (v_hbm.at[:, pl.ds(z.nodes - 2, 2)], v_ref.at[1]),
-            (s_hbm.at[pl.ds(0, 2)], s_ref.at[0]),
-            (s_hbm.at[pl.ds(z.nodes - 2, 2)], s_ref.at[1]),
-            (y_hbm, y_ref),
-            (c_hbm.at[face], c_ref),
-        ],
-        sems,
-    )
-    for copy in copies:
-        copy.wait()
-    soft = widen_flags(y_ref[...], z.dips)
-    for ref, side in ((left_ref, 0), (right_ref, 1)):
-        for c in range(z.parts):
-            for j in range(3):
-                tile = u_ref[side, c, j]
-                high = tile.astype(bf16).astype(f32)
-                both = jnp.concatenate([high, tile - high], axis=0).astype(bf16)
-                ref[pl.ds((c * 3 + j) * 2 * z.layers, 2 * z.layers), :] = both
-            both = jnp.concatenate([v_ref[side, c, 0], v_ref[side, c, 1]], axis=0).astype(bf16)
-            ref[pl.ds(z.halo_v + c * 2 * z.layers, 2 * z.layers), :] = both
-        start = 0 if side == 0 else soft.shape[0] - z.layers
-        part = soft[start:start + z.layers]
-        both = jnp.concatenate([s_ref[side, 0] * part, s_ref[side, 1] * part], axis=0)
-        ref[pl.ds(z.halo_m, 2 * z.layers), :] = both.astype(bf16)
-        start = 0 if side == 0 else z.nodes - 16
-        ref[pl.ds(z.halo_c, 16), :] = c_ref[pl.ds(start, 16), :].astype(f32).astype(bf16)
-        pieces = []
-        near = 0 if side == 0 else z.nodes - 1
-        pair = 0 if side == 0 else z.nodes - 2
-        for edge in beside:
-            for c in range(z.parts):
-                some = jnp.concatenate(
-                    [edge[3 * c, pl.ds(pair, 2), :], edge[3 * c + 1, pl.ds(near, 1), :]], axis=0
-                )
-                high = some.astype(bf16).astype(f32)
-                speed = edge[3 * z.parts + 2 * c, pl.ds(near, 1), :]
-                pieces += [high, some - high, speed, edge[5 * z.parts, pl.ds(near, 1), :]]
-        spare = z.halo - z.corner - 8 * z.sides * z.parts
-        if spare:
-            pieces.append(jnp.zeros((spare, z.dips), f32))
-        ref[pl.ds(z.corner, z.halo - z.corner), :] = jnp.concatenate(pieces, axis=0).astype(bf16)
-
-
-def toeplitz_kernel(z, g_ref, out_ref, wide_ref):
+def toeplitz_factors(z, g_ref, out_ref, turned_ref):
     me = lax.axis_index("strike")
     place, group = me % WIN, me // WIN
+    lane = lax.broadcasted_iota(jnp.int32, (z.span, LANES), 1)
     for c in range(z.parts):
         line = jnp.concatenate(
             [
@@ -236,59 +200,108 @@
         row = lax.broadcasted_iota(jnp.int32, (TAIL, z.modes), 0)
         last = jnp.where(row < TAIL // 2, wide[z.nodes:], last)
         wide = jnp.concatenate([wide[:z.nodes], last], axis=0)
-        wide = pltpu.roll(wide, place * z.nodes, 1)
         for j in range(z.chunks):
-            wide_ref[j] = wide[:, j * LANES:(j + 1) * LANES]
-        for s in range(z.targets):
-            j = (group - (group ^ s) + z.chunks) % z.chunks
-            out_ref[c, pl.ds(s * z.span, z.span), :] = wide_ref[j]
+            piece = wide[:, j * LANES:(j + 1) * LANES]
+            for r in range(WIN):
+                turned_ref[c, j, r] = pltpu.roll(piece, r * z.nodes, 1) if r else piece
+        for w in range(WIN):
+            ahead = beside_me(place)[w] - place + WIN * group
+            for q in range(z.chunks // WIN):
+                tile = None
+                for k in range(WIN):
+                    at = (WIN * (q * WIN + k) - ahead + 2 * z.strike) % z.strike
+                    piece = turned_ref[c, at // WIN, (k - at % WIN + WIN) % WIN]
+                    tile = piece if k == 0 else jnp.where(lane < k * z.nodes, tile, piece)
+                out_ref[c, pl.ds(w * z.span, z.span), q * LANES:(q + 1) * LANES] = tile
+
+
+def halo_kernel(z, u_ref, v_ref, s_ref, y_ref, c_ref, g_ref, *rest):
+    beside = rest[:z.sides]
+    pair_ref, cross_ref, toeplitz_ref, turned_ref = rest[z.sides:]
+    toeplitz_factors(z, g_ref, toeplitz_ref, turned_ref)
+    is_high = lax.axis_index("normal") == z.normal - 1
+    is_even = lax.axis_index("strike") % 2 == 0
+    soft = widen_flags(y_ref[...], z.dips)
+    for ref, is_end in ((pair_ref, is_even), (cross_ref, jnp.logical_not(is_even))):
+        first = jnp.where(is_end, z.nodes - 3, 0)
+        near = jnp.where(is_end, z.nodes - 2, 0)
+        for c in range(z.parts):
+            for j in range(3):
+                tile = u_ref[c, first + j]
+                high = tile.astype(bf16).astype(f32)
+                both = jnp.concatenate([high, tile - high], axis=0).astype(bf16)
+                ref[pl.ds((c * 3 + j) * 2 * z.layers, 2 * z.layers), :] = both
+            both = jnp.concatenate([v_ref[c, near], v_ref[c, near + 1]], axis=0).astype(bf16)
+            ref[pl.ds(z.halo_v + c * 2 * z.layers, 2 * z.layers), :] = both
+        part = jnp.where(is_end, soft[soft.shape[0] - z.layers:], soft[:z.layers])
+        both = jnp.concatenate([s_ref[near] * part, s_ref[near + 1] * part], axis=0)
+        ref[pl.ds(z.halo_m, 2 * z.layers), :] = both.astype(bf16)
+        own = jnp.where(is_high, c_ref[1], c_ref[0])
+        touch = jnp.where(is_end, own[z.nodes - 16:], own[:16])
+        ref[pl.ds(z.halo_c, 16), :] = touch.astype(f32).astype(bf16)
+
+        def rows_of(edge, k, count):
+            head = edge[k, pl.ds(0, count), :]
+            return jnp.where(is_end, edge[k, pl.ds(z.nodes - count, count), :], head)
+
+        pieces = []
+        for edge in beside:
+            for c in range(z.parts):
+                some = jnp.concatenate(
+                    [rows_of(edge, 3 * c, 2), rows_of(edge, 3 * c + 1, 1)], axis=0
+                )
+                high = some.astype(bf16).astype(f32)
+                speed = rows_of(edge, 3 * z.parts + 2 * c, 1)
+                pieces += [high, some - high, speed, rows_of(edge, 5 * z.parts, 1)]
+        spare = z.halo - z.corner - 8 * z.sides * z.parts
+        if spare:
+            pieces.append(jnp.zeros((spare, z.dips), f32))
+        ref[pl.ds(z.corner, z.halo - z.corner), :] = jnp.concatenate(pieces, axis=0).astype(bf16)
 
 
 def middle_kernel(z, toeplitz_ref, *rest):
-    window, mine_ref, out_refs, stack_ref = rest[:WIN], rest[WIN], rest[WIN + 1:-1], rest[-1]
+    window = (rest[z.targets - 1],) + rest[:z.targets - 1]
+    mine_ref = rest[z.targets]
+    out_refs, stack_ref = rest[z.targets + 1:-1], rest[-1]
     me = lax.axis_index("strike")
     place, group = me % WIN, me // WIN
-    lines = jnp.concatenate(
-        [
-            jnp.concatenate(
-                [ref[pl.ds(z.plane_rows + j * z.chunk_rows, z.chunk_rows), :] for ref in window],
-                axis=0,
-            )
-            for j in range(z.chunks)
-        ],
-        axis=1,
-    )
-    offset = node_offset(lax.broadcasted_iota(jnp.int32, (z.span, z.modes), 0))
-    away = lax.broadcasted_iota(jnp.int32, (z.span, z.modes), 1) - offset
-    away = jnp.where(away < 0, away + z.modes, away)
-    away = jnp.where(away >= z.modes, away - z.modes, away)
-    wanted = [
-        (away == ((group ^ s) * WIN + place) * z.nodes).astype(f32) for s in range(z.targets)
-    ]
+    spare = jnp.zeros((z.chunk_rows - z.spectral, 2 * LANES), f32)
+    lines = []
+    for ref in window:
+        both = ref[pl.ds(z.plane_rows, 2 * z.spectral), :].astype(f32)
+        lines += [jnp.concatenate([both[:z.spectral], both[z.spectral:]], axis=1), spare]
+    offset = node_offset(lax.broadcasted_iota(jnp.int32, (z.span, 2 * LANES), 0))
+    lane = lax.broadcasted_iota(jnp.int32, (z.span, 2 * LANES), 1)
+    wanted = []
+    for w in range(WIN):
+        node = beside_me(place)[w] * z.nodes + offset
+        node = jnp.where(node < 0, node + 2 * LANES, node)
+        wanted.append((lane == node).astype(f32))
     picked = lax.dot_general(
         jnp.concatenate(wanted, axis=0).astype(bf16),
-        lines,
+        jnp.concatenate(lines, axis=0).astype(bf16),
         (((1,), (1,)), ((), ())),
         preferred_element_type=f32,
     )
     row = lax.broadcasted_iota(jnp.int32, (z.chunk_rows, z.dips), 0)
     ahead = lax.broadcasted_iota(jnp.int32, (z.chunk_rows, z.dips), 1) - row
-    own_rows = WIN * z.nodes
+    own_rows = z.targets * z.nodes
     parts = []
     for c in range(z.parts):
         inside = (row >= c * z.rows) & (row < (c + 1) * z.rows)
-        for w, ref in enumerate(window):
-            at = pl.multiple_of((place ^ w) * z.nodes, z.nodes)
+        for s, ref in enumerate(window):
+            source = (group + z.targets - s) % z.targets
+            at = pl.multiple_of(source * z.nodes, z.nodes)
             stack_ref[c, pl.ds(at, z.nodes), :] = ref[pl.ds(c * z.nodes, z.nodes), :]
-            spot = inside & (ahead == z.rows * (me ^ w) - c * z.rows)
-            at = pl.ds(own_rows + w * z.chunk_rows, z.chunk_rows)
+            spot = inside & (ahead == z.rows * (WIN * source + place) - c * z.rows)
+            at = pl.ds(own_rows + s * z.chunk_rows, z.chunk_rows)
             stack_ref[c, at, :] = spot.astype(f32).astype(bf16)
         factors = jnp.concatenate([toeplitz_ref[c], picked], axis=1).astype(bf16)
         parts.append(jnp.dot(factors, stack_ref[c], preferred_element_type=f32))
         mine_ref[pl.ds(c * z.span, z.span), :] = parts[c][:z.span]
-    for s, ref in enumerate(out_refs, 1):
+    for w, ref in enumerate(out_refs, 1):
         ref[...] = jnp.concatenate(
-            [part[s * z.span:(s + 1) * z.span] for part in parts], axis=0
+            [part[w * z.span:(w + 1) * z.span] for part in parts], axis=0
         ).astype(bf16)
 
 
@@ -339,21 +352,33 @@
     return around - 6.0 * values
 
 
-def base_kernel(z, u_ref, v_ref, s_ref, y_ref, c_ref, left_ref, right_ref, *rest):
+def base_kernel(z, u_ref, v_ref, s_ref, y_ref, c_ref, cross_ref, pair_ref, *rest):
     sides = rest[:z.sides]
     out_u, out_v, mf_ref, ch_ref, m_ref, uh_ref, vh_ref, mh_ref, tile_ref = rest[z.sides:]
     set_modulus(z, s_ref, y_ref, m_ref)
-    unpack(z, left_ref, right_ref, uh_ref, vh_ref, mh_ref)
-    corner_tiles(z, left_ref, right_ref, tile_ref)
     place = lax.axis_index("normal")
     is_high = place == z.normal - 1
     is_face = (is_high | (place == 0)).astype(f32)
-    row = lax.broadcasted_iota(jnp.int32, (TAIL, z.dips), 0)
-    before = left_ref[pl.ds(z.halo_c, 16), :].astype(f32)[16 - TAIL:]
-    after = right_ref[pl.ds(z.halo_c, 16), :].astype(f32)[:TAIL]
-    own = jnp.where(is_high, c_ref[1], c_ref[0]).astype(f32)
-    tail = jnp.where(row < TAIL // 2, after, before)
-    ch_ref[...] = jnp.concatenate([own, tail], axis=0) * is_face
+    ch_ref[pl.ds(0, z.nodes), :] = jnp.where(is_high, c_ref[1], c_ref[0]).astype(f32) * is_face
+
+    def receive(left_ref, right_ref):
+        unpack(z, left_ref, right_ref, uh_ref, vh_ref, mh_ref)
+        corner_tiles(z, left_ref, right_ref, tile_ref)
+        row = lax.broadcasted_iota(jnp.int32, (TAIL, z.dips), 0)
+        before = left_ref[pl.ds(z.halo_c, 16), :].astype(f32)[16 - TAIL:]
+        after = right_ref[pl.ds(z.halo_c, 16), :].astype(f32)[:TAIL]
+        ch_ref[pl.ds(z.nodes, TAIL), :] = jnp.where(row < TAIL // 2, after, before) * is_face
+
+    is_even = lax.axis_index("strike") % 2 == 0
+
+    @pl.when(is_even)
+    def _():
+        receive(cross_ref, pair_ref)
+
+    @pl.when(jnp.logical_not(is_even))
+    def _():
+        receive(pair_ref, cross_ref)
+
     dip = lax.broadcasted_iota(jnp.int32, (z.span, z.dips), 1)
     first_dip, last_dip = dip == 0, dip == z.dips - 1
     low = -2 if z.sides == 2 else 0
@@ -457,15 +482,16 @@
     y = yield_flags.reshape(-1, yield_flags.shape[2])
     dma = pltpu.SemaphoreType.DMA
     ring = lambda step: [(i, (i + step) % z.strike) for i in range(z.strike)]
-    swap = lambda mask: [(i, i ^ mask) for i in range(z.strike)]
+    around = lambda w: [(i, i - i % WIN + beside_me(i % WIN)[w]) for i in range(z.strike)]
 
     edge = (5 * z.parts + 2, z.nodes, z.dips)
-    common, response, *edges = pl.pallas_call(
+    common, response, *edges_and_others = pl.pallas_call(
         functools.partial(common_kernel, z),
         out_shape=(shape((z.common, LANES), bf16), shape((z.chunks, 8, LANES), f32))
-        + (shape(edge, f32),) * z.sides,
+        + (shape(edge, f32),) * z.sides
+        + (shape((z.common, LANES), bf16),) * (z.targets - 1),
         in_specs=[HBM] * 7,
-        out_specs=(VMEM,) * (2 + z.sides),
+        out_specs=(VMEM,) * (1 + z.sides + z.targets),
         scratch_shapes=[
             pltpu.VMEM(u.shape, f32),
             pltpu.VMEM((z.lags - 1, 2, z.parts, z.rows, z.modes), bf16),
@@ -476,13 +502,17 @@
             pltpu.VMEM(y.shape, jnp.int32),
             pltpu.VMEM((z.chunk_rows, z.modes), f32),
             pltpu.VMEM((z.chunk_rows, z.modes), f32),
+            pltpu.VMEM((z.chunks, z.spectral, LANES), f32),
             dma((7,)),
         ],
         compiler_params=FIRST,
         name="plane_and_history",
     )(*in_hbm(u, history, kernel.transpose(0, 2, 1, 3), phase_quarter(z.modes), v, s, y))
 
-    window = [common] + [lax.ppermute(common, "strike", swap(w)) for w in range(1, WIN)]
+    edges, others = edges_and_others[:z.sides], edges_and_others[z.sides:]
+    window = [common] + [
+        lax.ppermute(other, "strike", ring(WIN * s)) for s, other in enumerate(others, 1)
+    ]
 
     if z.sides == 2:
         is_high = lax.axis_index("normal") == z.normal - 1
@@ -499,48 +529,34 @@
     else:
         beside = [lax.ppermute(edges[0], "normal", [(0, 1), (1, 0)])]
 
-    to_right, to_left = pl.pallas_call(
+    to_pair, to_cross, toeplitz = pl.pallas_call(
         functools.partial(halo_kernel, z),
-        out_shape=(shape((z.halo, LANES), bf16),) * 2,
-        in_specs=[HBM] * 5 + [VMEM] * z.sides,
-        out_specs=(VMEM,) * 2,
-        scratch_shapes=[
-            pltpu.VMEM((2, z.parts, 3, z.layers, z.dips), f32),
-            pltpu.VMEM((2, z.parts, 2, z.layers, z.dips), f32),
-            pltpu.VMEM((2, 2, z.layers, z.dips), f32),
-            pltpu.VMEM(y.shape, jnp.int32),
-            pltpu.VMEM(contact.shape[1:], jnp.int32),
-            dma((8,)),
-        ],
+        out_shape=(shape((z.halo, LANES), bf16),) * 2
+        + (shape((z.parts, WIN * z.span, z.targets * z.nodes), f32),),
+        in_specs=[VMEM] * (6 + z.sides),
+        out_specs=(VMEM,) * 3,
+        scratch_shapes=[pltpu.VMEM((z.parts, z.chunks, WIN, z.span, LANES), f32)],
         compiler_params=PARAMS,
-        name="strike_edges",
-    )(displacement, velocity, stiffness, y, contact, *beside)
-    from_left = lax.ppermute(to_right, "strike", ring(1))
-    from_right = lax.ppermute(to_left, "strike", ring(-1))
-
-    toeplitz = pl.pallas_call(
-        functools.partial(toeplitz_kernel, z),
-        out_shape=shape((z.parts, z.targets * z.span, LANES), f32),
-        in_specs=[VMEM],
-        out_specs=VMEM,
-        scratch_shapes=[pltpu.VMEM((z.chunks, z.span, LANES), f32)],
-        compiler_params=PARAMS,
-        name="toeplitz",
-    )(response)
+        name="strike_edges_and_toeplitz",
+    )(displacement, velocity, stiffness, y, contact, response, *beside)
+    from_pair = lax.ppermute(to_pair, "strike", [(i, i ^ 1) for i in range(z.strike)])
+    from_cross = lax.ppermute(
+        to_cross, "strike", [(i, (i - 1 + i % 2 * 2) % z.strike) for i in range(z.strike)]
+    )
 
     block = (z.parts * z.span, z.dips)
     mine, *parcels = pl.pallas_call(
         functools.partial(middle_kernel, z),
-        out_shape=(shape(block, f32),) + (shape(block, bf16),) * (z.targets - 1),
-        in_specs=[VMEM] * (1 + WIN),
-        out_specs=(VMEM,) * z.targets,
-        scratch_shapes=[pltpu.VMEM((z.parts, WIN * (z.nodes + z.chunk_rows), z.dips), bf16)],
+        out_shape=(shape(block, f32),) + (shape(block, bf16),) * (WIN - 1),
+        in_specs=[VMEM] * (1 + z.targets),
+        out_specs=(VMEM,) * WIN,
+        scratch_shapes=[pltpu.VMEM((z.parts, z.targets * (z.nodes + z.chunk_rows), z.dips), bf16)],
         compiler_params=PARAMS,
         name="partial_tractions",
-    )(toeplitz, *window)
+    )(toeplitz, *window[1:], common)
 
     arrived = [
-        lax.ppermute(p, "strike", swap(WIN * (k + 1))) for k, p in reversed(list(enumerate(parcels)))
+        lax.ppermute(parcels[w - 1], "strike", around(w)) for w in (3, 1, 2)
     ]
     tail = (z.parts, TAIL * z.layers, z.dips)
     base_u, base_v, face_modulus, touching = pl.pallas_call(
@@ -562,7 +578,7 @@
         ],
         compiler_params=PARAMS,
         name="unloaded_substeps",
-    )(u, v, s, y, contact, from_left, from_right, *beside)
+    )(u, v, s, y, contact, from_cross, from_pair, *beside)
 
     moved, speed = pl.pallas_call(
         functools.partial(final_kernel, z),

time: 22.2 us -> 20.8 us (0.937)
  starting transfers between devices: 15.1 us -> 13.7 us
  waiting for transfers between devices: 0.84 us -> 1.08 us
    ppermute x8, starting transfers between devices: 14.6 us -> 13.1 us  [the longest x3 6.57 us: body(): lax.ppermute(other, 'strike', ring(WIN * s))]
    pallas_call x1 -> x0, Pallas kernels: 0.29 us -> none  [body(): pl.pallas_call(functools.partial(toeplitz_kernel, z), out_shape=shape((z....]
    ppermute x8, waiting for transfers between devices: 0.83 us -> 1.07 us  [the longest x1 1.06 us: body(): lax.ppermute(to_cross, 'strike', [(i, (i - 1 + i % 2 * 2) % z.strike) for...]
  transfers between devices with their start and end apart: 9 -> 9, of which waited for: 2 -> 1; matrix products, arithmetic and copies ran while one was open for 0% -> 0% of each run, Pallas kernels for 12% -> 12%
where the time goes in v4:
time: 20.8 us; the launch traced here: 20.7 us
  starting transfers between devices  13.7 us (66%)
  Pallas kernels  5.17 us (25%)
  waiting for transfers between devices  1.08 us (5%)
  between operations  0.76 us (4%)
    ppermute x3, starting transfers between devices, body(): lax.ppermute(other, 'strike', ring(WIN * s))  6.57 us
    ppermute x3, starting transfers between devices, body(): lax.ppermute(parcels[w - 1], 'strike', around(w))  3.53 us
    ppermute x1, starting transfers between devices, body(): lax.ppermute(to_cross, 'strike', [(i, (i - 1 + i % 2 * 2) % z.strike) for...  2.4 us
    pallas_call x1, Pallas kernels, body(): pl.pallas_call(functools.partial(common_kernel, z), out_shape=(shape((z.c...  1.65 us
    pallas_call x1, Pallas kernels, body(): pl.pallas_call(functools.partial(base_kernel, z), out_shape=(shape(u.shap...  1.46 us
    pallas_call x1, Pallas kernels, body(): pl.pallas_call(functools.partial(final_kernel, z), out_shape=(shape(u.sha...  1.11 us
    ppermute x1, waiting for transfers between devices, body(): lax.ppermute(to_cross, 'strike', [(i, (i - 1 + i % 2 * 2) % z.strike) for...  1.06 us
    ppermute x1, starting transfers between devices, body(): lax.ppermute(to_pair, 'strike', [(i, i ^ 1) for i in range(z.strike)])  0.64 us
  transfers between devices with their start and end apart: 9, of which 1 were waited for; matrix products, arithmetic and copies ran while one was open for 0% of the time, Pallas kernels for 12%

profile of v4, /device:TPU:0, one launch (start us, length us, event | category | flops | bytes accessed | tf_op | source)
XLA Modules:
  0.0 20.7 jit_solution(10867313403461666511)
XLA Ops:
  0.6 0.0 copy-start
  0.6 0.0 copy-start.1
  0.7 0.0 copy-start.2
  0.7 0.0 copy-start.3
  0.7 0.0 copy-start.4
  0.7 1.7 %plane_and_history.1 = (bf16[144,128]{1,0:T(8,128)(2,1)S(1)}, f32[4,8,128]{2,1,0:T(8,128)S(1)}, f32[17,32,128]{2,1,0:T(8,128)S(1)}, bf16[144,128]{1,0:T(8,128)(2...) custom-call(f32[768,128]{1,0:T(8,128)} %bitcast.7, bf16[2,8,2,3,8,512]{5,4,3,2,1,0:T(8,128)(2,1)} %h_hbm.1, ...), custom_call_target="tpu_custom_call" | custom-call | tf_op jit(solution)/shard_map/plane_and_history/pallas_call | solution.py:488
  2.3 0.5 %collective-permute-start = (f32[17,32,128]{2,1,0:T(8,128)S(1)}, f32[17,32,128]{2,1,0:T(8,128)S(1)}, u32[]{:S(2)}, u32[]{:S(2)}) collective-permute-start(f32[17,32,128]{2,1,0:T(8,128)S(1)} %get-tuple-element.22), channel_id=1, source_target_pairs={{0,1},{1,0},{2,3},{3,2},{4,5},{5,4},{6,7},{7,6},{8,9},{9,8},{10,11... | collective-permute-start | bytes 835592 | tf_op jit(solution)/shard_map/ppermute | solution.py:530
  2.9 2.6 %collective-permute-start.1 = (bf16[144,128]{1,0:T(8,128)(2,1)S(1)}, bf16[144,128]{1,0:T(8,128)(2,1)S(1)}, u32[]{:S(2)}, u32[]{:S(2)}) collective-permute-start(bf16[144,128]{1,0:T(8,128)(2,1)S(1)} %get-tuple-element.24), channel_id=1, source_target_pairs={{0,8},{2,10},{4,12},{6,14},{8,16},{10,18},{12,20},{14,22},{16,24},... | collective-permute-start | bytes 110600 | tf_op jit(solution)/shard_map/ppermute | solution.py:514
  5.5 2.6 %collective-permute-start.2 = (bf16[144,128]{1,0:T(8,128)(2,1)S(1)}, bf16[144,128]{1,0:T(8,128)(2,1)S(1)}, u32[]{:S(2)}, u32[]{:S(2)}) collective-permute-start(bf16[144,128]{1,0:T(8,128)(2,1)S(1)} %get-tuple-element.25), channel_id=1, source_target_pairs={{0,16},{2,18},{4,20},{6,22},{8,24},{10,26},{12,28},{14,30},{16,0},... | collective-permute-start | bytes 110600 | tf_op jit(solution)/shard_map/ppermute | solution.py:514
  8.1 1.3 %collective-permute-start.3 = (bf16[144,128]{1,0:T(8,128)(2,1)S(1)}, bf16[144,128]{1,0:T(8,128)(2,1)S(1)}, u32[]{:S(2)}, u32[]{:S(2)}) collective-permute-start(bf16[144,128]{1,0:T(8,128)(2,1)S(1)} %get-tuple-element.26), channel_id=1, source_target_pairs={{0,24},{2,26},{4,28},{6,30},{8,0},{10,2},{12,4},{14,6},{16,8},{18,... | collective-permute-start | bytes 110600 | tf_op jit(solution)/shard_map/ppermute | solution.py:514
  9.4 0.0 collective-permute-done.rest_0_
  9.4 0.0 copy-done
  9.4 0.0 copy-done.1
  9.4 0.0 copy-done.2
  9.5 0.0 copy-done.3
  9.5 0.0 copy-done.4
  9.5 0.6 %strike_edges_and_toeplitz.1 = (bf16[256,128]{1,0:T(8,128)(2,1)S(1)}, bf16[256,128]{1,0:T(8,128)(2,1)S(1)}, f32[3,160,128]{2,1,0:T(8,128)S(1)}) custom-call(f32[3,32,8,128]{3,2,1,0:T(8,128)S(1)} %copy-done, f32[3,32,8,128]{3,2,1,0:T(8,128)S(1)} %copy-done.1, f32[32,8,128]{2,1,0:T(8,128)S(1)} %copy-done.2, s32[64,32]{1,0:T(8,128)S(1)} %bitcast.14, ...), custom_call_target="tpu_custom_call" | custom-call | tf_op jit(solution)/shard_map/strike_edges_and_toeplitz/pallas_call | solution.py:532
  10.1 2.4 %collective-permute-start.4 = (bf16[256,128]{1,0:T(8,128)(2,1)S(1)}, bf16[256,128]{1,0:T(8,128)(2,1)S(1)}, u32[]{:S(2)}, u32[]{:S(2)}) collective-permute-start(bf16[256,128]{1,0:T(8,128)(2,1)S(1)} %get-tuple-element.29), channel_id=1, source_target_pairs={{0,30},{2,4},{4,2},{6,8},{8,6},{10,12},{12,10},{14,16},{16,14},{18... | collective-permute-start | bytes 196616 | tf_op jit(solution)/shard_map/ppermute | solution.py:543
  12.5 0.6 %collective-permute-start.5 = (bf16[256,128]{1,0:T(8,128)(2,1)S(1)}, bf16[256,128]{1,0:T(8,128)(2,1)S(1)}, u32[]{:S(2)}, u32[]{:S(2)}) collective-permute-start(bf16[256,128]{1,0:T(8,128)(2,1)S(1)} %get-tuple-element.30), channel_id=1, source_target_pairs={{0,2},{2,0},{4,6},{6,4},{8,10},{10,8},{12,14},{14,12},{16,18},{18,... | collective-permute-start | bytes 196616 | tf_op jit(solution)/shard_map/ppermute | solution.py:542
  13.1 0.0 collective-permute-done.1.rest_0_
  13.1 0.0 collective-permute-done.2.rest_1_
  13.1 0.0 collective-permute-done.3.rest_2_
  13.1 0.4 %partial_tractions.1 = (f32[120,128]{1,0:T(8,128)S(1)}, bf16[120,128]{1,0:T(8,128)(2,1)S(1)}, bf16[120,128]{1,0:T(8,128)(2,1)S(1)}, bf16[120,128]{1,0:T(8,128)(2,1)S(1)}) custom-call(f32[3,160,128]{2,1,0:T(8,128)S(1)} %get-tuple-element.23.toeplitz_ref, bf16[144,128]{1,0:T(8,128)(2,1)S(1)} %collective-permute-done.1.rest_0_, ...), custom_call_target="tpu_custom_call" | custom-call | tf_op jit(solution)/shard_map/partial_tractions/pallas_call | solution.py:548
  13.5 1.5 %collective-permute-start.6 = (bf16[120,128]{1,0:T(8,128)(2,1)S(1)}, bf16[120,128]{1,0:T(8,128)(2,1)S(1)}, u32[]{:S(2)}, u32[]{:S(2)}) collective-permute-start(bf16[120,128]{1,0:T(8,128)(2,1)S(1)} %get-tuple-element.35), channel_id=1, source_target_pairs={{0,6},{2,4},{4,2},{6,0},{8,14},{10,12},{12,10},{14,8},{16,22},{18,... | collective-permute-start | bytes 92168 | tf_op jit(solution)/shard_map/ppermute | solution.py:559
  15.0 0.6 %collective-permute-start.7 = (bf16[120,128]{1,0:T(8,128)(2,1)S(1)}, bf16[120,128]{1,0:T(8,128)(2,1)S(1)}, u32[]{:S(2)}, u32[]{:S(2)}) collective-permute-start(bf16[120,128]{1,0:T(8,128)(2,1)S(1)} %get-tuple-element.36), channel_id=1, source_target_pairs={{0,2},{2,6},{4,0},{6,4},{8,10},{10,14},{12,8},{14,12},{16,18},{18,... | collective-permute-start | bytes 92168 | tf_op jit(solution)/shard_map/ppermute | solution.py:559
  15.7 1.4 %collective-permute-start.8 = (bf16[120,128]{1,0:T(8,128)(2,1)S(1)}, bf16[120,128]{1,0:T(8,128)(2,1)S(1)}, u32[]{:S(2)}, u32[]{:S(2)}) collective-permute-start(bf16[120,128]{1,0:T(8,128)(2,1)S(1)} %get-tuple-element.37), channel_id=1, source_target_pairs={{0,4},{2,0},{4,6},{6,2},{8,12},{10,8},{12,14},{14,10},{16,20},{18,... | collective-permute-start | bytes 92168 | tf_op jit(solution)/shard_map/ppermute | solution.py:559
  17.0 1.1 %collective-permute-done.4.cross_ref = bf16[256,128]{1,0:T(8,128)(2,1)S(1)} collective-permute-done((bf16[256,128]{1,0:T(8,128)(2,1)S(1)}, bf16[256,128]{1,0:T(8,128)(2,1)S(1)}, u32[]{:S(2)}, u32[]{:S(2)}) %collective-permute-start.4) | collective-permute-done | bytes 65568 | tf_op jit(solution)/shard_map/ppermute | solution.py:543
  18.1 0.0 collective-permute-done.5.pair_ref
  18.1 1.5 %unloaded_substeps.1 = (f32[768,128]{1,0:T(8,128)S(1)}, f32[768,128]{1,0:T(8,128)S(1)}, f32[3,40,128]{2,1,0:T(8,128)S(1)}, f32[40,128]{1,0:T(8,128)S(1)}) custom-call(f32[768,128]{1,0:T(8,128)S(1)} %bitcast.8, f32[768,128]{1,0:T(8,128)S(1)} %bitcast.10, f32[256,128]{1,0:T(8,128)S(1)} %bitcast.12, s32[64,32]{1,0:T(8,128)S(1)} %bitcast.15, ...), custom_call_target="tpu_custom_call" | custom-call | tf_op jit(solution)/shard_map/unloaded_substeps/pallas_call | solution.py:562
  19.6 0.0 collective-permute-done.6.rest_0_
  19.6 0.0 collective-permute-done.7.rest_1_
  19.6 0.0 collective-permute-done.8.rest_2_
  19.6 1.1 %add_force_response.1 = (f32[768,128]{1,0:T(8,128)}, f32[768,128]{1,0:T(8,128)}) custom-call(f32[120,128]{1,0:T(8,128)S(1)} %get-tuple-element.28.mine_ref, f32[40,128]{1,0:T(8,128)S(1)} %get-tuple-element.31.contact_ref, f32[3,40,128]{2,1,0:T(8,128)S(1)} %get-tuple-element.32.m_ref, f32[768,128]{1,0:T(8,128)S(1)} %get-tuple-element.33.base_u, ...), custom_call_target="tpu_custom_call" | custom-call | tf_op jit(solution)/shard_map/add_force_response/pallas_call | solution.py:583
Async XLA Ops:
  0.6 8.8 %copy-start = (f32[3,32,8,128]{3,2,1,0:T(8,128)S(1)}, f32[3,32,8,128]{3,2,1,0:T(8,128)}, u32[]{:S(2)}) copy-start(f32[3,32,8,128]{3,2,1,0:T(8,128)} %u_ref.1) | copy-start | bytes 1179652
  0.6 8.8 %copy-start.1 = (f32[3,32,8,128]{3,2,1,0:T(8,128)S(1)}, f32[3,32,8,128]{3,2,1,0:T(8,128)}, u32[]{:S(2)}) copy-start(f32[3,32,8,128]{3,2,1,0:T(8,128)} %v_ref.1) | copy-start | bytes 1179652
  0.7 8.8 %copy-start.2 = (f32[32,8,128]{2,1,0:T(8,128)S(1)}, f32[32,8,128]{2,1,0:T(8,128)}, u32[]{:S(2)}) copy-start(f32[32,8,128]{2,1,0:T(8,128)} %s_ref.1) | copy-start | bytes 393220
  0.7 8.8 %copy-start.3 = (s32[8,8,32]{2,1,0:T(8,128)S(1)}, s32[8,8,32]{2,1,0:T(8,128)}, u32[]{:S(2)}) copy-start(s32[8,8,32]{2,1,0:T(8,128)} %param.11) | copy-start | bytes 24580
  0.7 8.8 %copy-start.4 = (s32[2,32,128]{2,1,0:T(8,128)S(1)}, s32[2,32,128]{2,1,0:T(8,128)}, u32[]{:S(2)}) copy-start(s32[2,32,128]{2,1,0:T(8,128)} %c_ref.3) | copy-start | bytes 98308
  2.3 7.1 %collective-permute-start = (f32[17,32,128]{2,1,0:T(8,128)S(1)}, f32[17,32,128]{2,1,0:T(8,128)S(1)}, u32[]{:S(2)}, u32[]{:S(2)}) collective-permute-start(f32[17,32,128]{2,1,0:T(8,128)S(1)} %get-tuple-element.22), channel_id=1, source_target_pairs={{0,1},{1,0},{2,3},{3,2},{4,5},{5,4},{6,7},{7,6},{8,9},{9,8},{10,11... | collective-permute-start | bytes 835592 | tf_op jit(solution)/shard_map/ppermute | solution.py:530
  2.9 10.2 %collective-permute-start.1 = (bf16[144,128]{1,0:T(8,128)(2,1)S(1)}, bf16[144,128]{1,0:T(8,128)(2,1)S(1)}, u32[]{:S(2)}, u32[]{:S(2)}) collective-permute-start(bf16[144,128]{1,0:T(8,128)(2,1)S(1)} %get-tuple-element.24), channel_id=1, source_target_pairs={{0,8},{2,10},{4,12},{6,14},{8,16},{10,18},{12,20},{14,22},{16,24},... | collective-permute-start | bytes 110600 | tf_op jit(solution)/shard_map/ppermute | solution.py:514
  5.5 7.6 %collective-permute-start.2 = (bf16[144,128]{1,0:T(8,128)(2,1)S(1)}, bf16[144,128]{1,0:T(8,128)(2,1)S(1)}, u32[]{:S(2)}, u32[]{:S(2)}) collective-permute-start(bf16[144,128]{1,0:T(8,128)(2,1)S(1)} %get-tuple-element.25), channel_id=1, source_target_pairs={{0,16},{2,18},{4,20},{6,22},{8,24},{10,26},{12,28},{14,30},{16,0},... | collective-permute-start | bytes 110600 | tf_op jit(solution)/shard_map/ppermute | solution.py:514
  8.1 5.0 %collective-permute-start.3 = (bf16[144,128]{1,0:T(8,128)(2,1)S(1)}, bf16[144,128]{1,0:T(8,128)(2,1)S(1)}, u32[]{:S(2)}, u32[]{:S(2)}) collective-permute-start(bf16[144,128]{1,0:T(8,128)(2,1)S(1)} %get-tuple-element.26), channel_id=1, source_target_pairs={{0,24},{2,26},{4,28},{6,30},{8,0},{10,2},{12,4},{14,6},{16,8},{18,... | collective-permute-start | bytes 110600 | tf_op jit(solution)/shard_map/ppermute | solution.py:514
  10.1 8.0 %collective-permute-start.4 = (bf16[256,128]{1,0:T(8,128)(2,1)S(1)}, bf16[256,128]{1,0:T(8,128)(2,1)S(1)}, u32[]{:S(2)}, u32[]{:S(2)}) collective-permute-start(bf16[256,128]{1,0:T(8,128)(2,1)S(1)} %get-tuple-element.29), channel_id=1, source_target_pairs={{0,30},{2,4},{4,2},{6,8},{8,6},{10,12},{12,10},{14,16},{16,14},{18... | collective-permute-start | bytes 196616 | tf_op jit(solution)/shard_map/ppermute | solution.py:543
  12.5 5.6 %collective-permute-start.5 = (bf16[256,128]{1,0:T(8,128)(2,1)S(1)}, bf16[256,128]{1,0:T(8,128)(2,1)S(1)}, u32[]{:S(2)}, u32[]{:S(2)}) collective-permute-start(bf16[256,128]{1,0:T(8,128)(2,1)S(1)} %get-tuple-element.30), channel_id=1, source_target_pairs={{0,2},{2,0},{4,6},{6,4},{8,10},{10,8},{12,14},{14,12},{16,18},{18,... | collective-permute-start | bytes 196616 | tf_op jit(solution)/shard_map/ppermute | solution.py:542
  13.5 6.1 %collective-permute-start.6 = (bf16[120,128]{1,0:T(8,128)(2,1)S(1)}, bf16[120,128]{1,0:T(8,128)(2,1)S(1)}, u32[]{:S(2)}, u32[]{:S(2)}) collective-permute-start(bf16[120,128]{1,0:T(8,128)(2,1)S(1)} %get-tuple-element.35), channel_id=1, source_target_pairs={{0,6},{2,4},{4,2},{6,0},{8,14},{10,12},{12,10},{14,8},{16,22},{18,... | collective-permute-start | bytes 92168 | tf_op jit(solution)/shard_map/ppermute | solution.py:559
  15.0 4.6 %collective-permute-start.7 = (bf16[120,128]{1,0:T(8,128)(2,1)S(1)}, bf16[120,128]{1,0:T(8,128)(2,1)S(1)}, u32[]{:S(2)}, u32[]{:S(2)}) collective-permute-start(bf16[120,128]{1,0:T(8,128)(2,1)S(1)} %get-tuple-element.36), channel_id=1, source_target_pairs={{0,2},{2,6},{4,0},{6,4},{8,10},{10,14},{12,8},{14,12},{16,18},{18,... | collective-permute-start | bytes 92168 | tf_op jit(solution)/shard_map/ppermute | solution.py:559
  15.7 3.9 %collective-permute-start.8 = (bf16[120,128]{1,0:T(8,128)(2,1)S(1)}, bf16[120,128]{1,0:T(8,128)(2,1)S(1)}, u32[]{:S(2)}, u32[]{:S(2)}) collective-permute-start(bf16[120,128]{1,0:T(8,128)(2,1)S(1)} %get-tuple-element.37), channel_id=1, source_target_pairs={{0,4},{2,0},{4,6},{6,2},{8,12},{10,8},{12,14},{14,10},{16,20},{18,... | collective-permute-start | bytes 92168 | tf_op jit(solution)/shard_map/ppermute | solution.py:559

commit v5 on v4

--- a/solution.py
+++ b/solution.py
@@ -45,15 +45,15 @@
         self.chunk_rows = round_up(self.spectral + 2 * self.parts, 16)
         self.plane_rows = self.parts * self.nodes
         self.common = self.plane_rows + 2 * self.spectral
-        self.halo_v = self.parts * 3 * 2 * self.layers
+        self.halo_v = self.parts * 4 * self.layers
         self.halo_m = self.halo_v + self.parts * 2 * self.layers
-        self.halo_c = self.halo_m + 2 * self.layers
-        self.corner = self.halo_c + 16
+        self.corner = self.halo_m + 2 * self.layers
         self.span = self.nodes + TAIL
         self.targets = self.strike // WIN
         self.stride = self.nodes * self.layers
         self.sides = 1 if self.normal == 2 else 2
-        self.halo = self.corner + round_up(self.sides * self.parts * 8, 16)
+        self.touch = self.sides * self.parts * 8
+        self.halo = self.corner + round_up(self.touch + TAIL, 16)
 
 
 def widen_flags(flags, dips):
@@ -95,7 +95,28 @@
         out_ref[rows, :] = s_ref[rows, :] * soft[at:at + z.layers]
 
 
-def common_kernel(z, u_hbm, h_hbm, k_hbm, t_hbm, v_hbm, s_hbm, y_hbm, out_ref, g_ref, *rest):
+def selections(z, wanted_ref, spots_ref):
+    me = lax.axis_index("strike")
+    place, group = me % WIN, me // WIN
+    offset = node_offset(lax.broadcasted_iota(jnp.int32, (z.span, 2 * LANES), 0))
+    lane = lax.broadcasted_iota(jnp.int32, (z.span, 2 * LANES), 1)
+    wanted = []
+    for t in range(WIN):
+        node = t * z.nodes + offset
+        node = jnp.where(node < 0, node + 2 * LANES, node)
+        wanted.append((lane == node).astype(f32))
+    wanted_ref[...] = jnp.concatenate(wanted, axis=0).astype(bf16)
+    row = lax.broadcasted_iota(jnp.int32, (z.chunk_rows, z.dips), 0)
+    ahead = lax.broadcasted_iota(jnp.int32, (z.chunk_rows, z.dips), 1) - row
+    for c in range(z.parts):
+        inside = (row >= c * z.rows) & (row < (c + 1) * z.rows)
+        for s in range(z.targets):
+            source = (group + z.targets - s) % z.targets
+            spot = inside & (ahead == z.rows * (WIN * source + place) - c * z.rows)
+            spots_ref[c, pl.ds(s * z.chunk_rows, z.chunk_rows), :] = spot.astype(f32).astype(bf16)
+
+
+def common_kernel(z, u_hbm, h_hbm, k_hbm, t_hbm, v_hbm, s_hbm, y_hbm, out_ref, g_ref, m_ref, wanted_ref, spots_ref, *rest):
     edges, others = rest[:z.sides], rest[z.sides:z.sides + z.targets - 1]
     u_ref, h_ref, k_ref, t_ref, v_ref, s_ref, y_ref, re_ref, im_ref, line_ref, sems = rest[-11:]
     is_high = lax.axis_index("normal") == z.normal - 1
@@ -112,6 +133,7 @@
         ],
         sems,
     )
+    selections(z, wanted_ref, spots_ref)
     re_ref[...] = jnp.zeros_like(re_ref)
     im_ref[...] = jnp.zeros_like(im_ref)
     copies[1].wait()
@@ -167,7 +189,7 @@
             ref[pl.ds(c * z.nodes, z.nodes), :] = plane
     for copy in copies[4:]:
         copy.wait()
-    set_modulus(z, s_ref, y_ref, s_ref)
+    set_modulus(z, s_ref, y_ref, m_ref)
     size = z.layers
     for out, levels in zip(edges, ((size - 1, size - 2, size - 3), (0, 1, 2))):
         for j, f in enumerate(levels):
@@ -178,13 +200,15 @@
                 if j < 2:
                     out[3 * z.parts + 2 * c + j] = v_ref[at, :]
             if j < 2:
-                out[5 * z.parts + j] = s_ref[pl.ds(layer, z.nodes, stride=size), :]
-
-
-def toeplitz_factors(z, g_ref, out_ref, turned_ref):
+                out[5 * z.parts + j] = m_ref[pl.ds(layer, z.nodes, stride=size), :]
+
+
+def toeplitz_factors(z, g_ref, out_ref):
     me = lax.axis_index("strike")
     place, group = me % WIN, me // WIN
-    lane = lax.broadcasted_iota(jnp.int32, (z.span, LANES), 1)
+    lane = lax.broadcasted_iota(jnp.int32, (8, LANES), 1)
+    row = lax.broadcasted_iota(jnp.int32, (8, LANES), 0)
+    stack = []
     for c in range(z.parts):
         line = jnp.concatenate(
             [
@@ -193,52 +217,79 @@
             ],
             axis=1,
         ) * (1.0 / math.sqrt(z.modes))
-        wide = jnp.broadcast_to(line, (z.span, z.modes))
-        wide = pltpu.roll(wide, 0, 1, stride=1, stride_axis=0)
-        last = jnp.broadcast_to(line, (TAIL, z.modes))
-        last = pltpu.roll(last, z.modes - TAIL, 1, stride=1, stride_axis=0)
-        row = lax.broadcasted_iota(jnp.int32, (TAIL, z.modes), 0)
-        last = jnp.where(row < TAIL // 2, wide[z.nodes:], last)
-        wide = jnp.concatenate([wide[:z.nodes], last], axis=0)
-        for j in range(z.chunks):
-            piece = wide[:, j * LANES:(j + 1) * LANES]
-            for r in range(WIN):
-                turned_ref[c, j, r] = pltpu.roll(piece, r * z.nodes, 1) if r else piece
-        for w in range(WIN):
-            ahead = beside_me(place)[w] - place + WIN * group
+        stack.append(jnp.broadcast_to(line, (8, z.modes)))
+    wide = pltpu.roll(jnp.concatenate(stack, axis=0), 0, 1, stride=1, stride_axis=0)
+    wide = pltpu.roll(wide, (group * LANES - place * z.nodes + z.modes) % z.modes, 1)
+    for c in range(z.parts):
+        columns = [wide[8 * c:8 * c + 8, j * LANES:(j + 1) * LANES] for j in range(z.chunks)]
+
+        turned = {}
+
+        def turn(j, shift):
+            key = (j % z.chunks, shift % LANES)
+            if key not in turned:
+                piece = columns[key[0]]
+                turned[key] = pltpu.roll(piece, key[1], 1) if key[1] else piece
+            return turned[key]
+
+        def eight_rows(shift, q):
+            whole, rest = divmod((shift - 8 * c) % z.modes, LANES)
+            tile = None
+            for k in range(WIN):
+                j = q * WIN + k - whole
+                first = k * z.nodes
+                if rest == 0:
+                    piece = turn(j, first)
+                elif rest >= z.nodes:
+                    piece = turn(j - 1, first + rest)
+                else:
+                    piece = jnp.where(
+                        lane < first + rest, turn(j - 1, first + rest), turn(j, first + rest)
+                    )
+                tile = piece if k == 0 else jnp.where(lane < first, tile, piece)
+            return tile
+
+        for t in range(WIN):
             for q in range(z.chunks // WIN):
-                tile = None
-                for k in range(WIN):
-                    at = (WIN * (q * WIN + k) - ahead + 2 * z.strike) % z.strike
-                    piece = turned_ref[c, at // WIN, (k - at % WIN + WIN) % WIN]
-                    tile = piece if k == 0 else jnp.where(lane < k * z.nodes, tile, piece)
-                out_ref[c, pl.ds(w * z.span, z.span), q * LANES:(q + 1) * LANES] = tile
-
-
-def halo_kernel(z, u_ref, v_ref, s_ref, y_ref, c_ref, g_ref, *rest):
+                for k in range(z.span // 8):
+                    tile = eight_rows(t * z.nodes + 8 * k, q)
+                    if 8 * k == z.nodes:
+                        tile = jnp.where(row < TAIL // 2, tile, eight_rows(t * z.nodes - 8, q))
+                    at = pl.ds(t * z.span + 8 * k, 8)
+                    out_ref[c, at, q * LANES:(q + 1) * LANES] = tile
+
+
+def halo_kernel(z, u_ref, v_ref, m_ref, c_ref, g_ref, *rest):
     beside = rest[:z.sides]
-    pair_ref, cross_ref, toeplitz_ref, turned_ref = rest[z.sides:]
-    toeplitz_factors(z, g_ref, toeplitz_ref, turned_ref)
+    pair_ref, cross_ref, toeplitz_ref = rest[z.sides:]
+    toeplitz_factors(z, g_ref, toeplitz_ref)
     is_high = lax.axis_index("normal") == z.normal - 1
     is_even = lax.axis_index("strike") % 2 == 0
-    soft = widen_flags(y_ref[...], z.dips)
+    size = z.layers
     for ref, is_end in ((pair_ref, is_even), (cross_ref, jnp.logical_not(is_even))):
-        first = jnp.where(is_end, z.nodes - 3, 0)
-        near = jnp.where(is_end, z.nodes - 2, 0)
+        nodes = [jnp.where(is_end, z.nodes - 1 - d, d) for d in range(3)]
         for c in range(z.parts):
-            for j in range(3):
-                tile = u_ref[c, first + j]
-                high = tile.astype(bf16).astype(f32)
-                both = jnp.concatenate([high, tile - high], axis=0).astype(bf16)
-                ref[pl.ds((c * 3 + j) * 2 * z.layers, 2 * z.layers), :] = both
-            both = jnp.concatenate([v_ref[c, near], v_ref[c, near + 1]], axis=0).astype(bf16)
-            ref[pl.ds(z.halo_v + c * 2 * z.layers, 2 * z.layers), :] = both
-        part = jnp.where(is_end, soft[soft.shape[0] - z.layers:], soft[:z.layers])
-        both = jnp.concatenate([s_ref[near] * part, s_ref[near + 1] * part], axis=0)
-        ref[pl.ds(z.halo_m, 2 * z.layers), :] = both.astype(bf16)
+            tiles = []
+            known = None
+            for node in nodes:
+                tile = u_ref[c, node]
+                if known is None:
+                    high = tile.astype(bf16).astype(f32)
+                    tiles += [high, tile - high]
+                    known = high + (tile - high).astype(bf16).astype(f32)
+                else:
+                    tiles.append(tile - known)
+                    known = known + tiles[-1].astype(bf16).astype(f32)
+            at = pl.ds(c * 4 * size, 4 * size)
+            ref[at, :] = jnp.concatenate(tiles, axis=0).astype(bf16)
+            both = jnp.concatenate([v_ref[c, nodes[0]], v_ref[c, nodes[1]]], axis=0).astype(bf16)
+            ref[pl.ds(z.halo_v + c * 2 * size, 2 * size), :] = both
+        both = jnp.concatenate(
+            [m_ref[pl.ds(pl.multiple_of(node * size, size), size), :] for node in nodes[:2]], axis=0
+        )
+        ref[pl.ds(z.halo_m, 2 * size), :] = both.astype(bf16)
         own = jnp.where(is_high, c_ref[1], c_ref[0])
-        touch = jnp.where(is_end, own[z.nodes - 16:], own[:16])
-        ref[pl.ds(z.halo_c, 16), :] = touch.astype(f32).astype(bf16)
+        touch = jnp.where(is_end, own[z.nodes - TAIL:], own[:TAIL]).astype(f32)
 
         def rows_of(edge, k, count):
             head = edge[k, pl.ds(0, count), :]
@@ -253,16 +304,17 @@
                 high = some.astype(bf16).astype(f32)
                 speed = rows_of(edge, 3 * z.parts + 2 * c, 1)
                 pieces += [high, some - high, speed, rows_of(edge, 5 * z.parts, 1)]
-        spare = z.halo - z.corner - 8 * z.sides * z.parts
+        pieces.append(touch)
+        spare = z.halo - z.corner - z.touch - TAIL
         if spare:
             pieces.append(jnp.zeros((spare, z.dips), f32))
         ref[pl.ds(z.corner, z.halo - z.corner), :] = jnp.concatenate(pieces, axis=0).astype(bf16)
 
 
-def middle_kernel(z, toeplitz_ref, *rest):
+def middle_kernel(z, wanted_ref, spots_ref, toeplitz_ref, *rest):
     window = (rest[z.targets - 1],) + rest[:z.targets - 1]
     mine_ref = rest[z.targets]
-    out_refs, stack_ref = rest[z.targets + 1:-1], rest[-1]
+    out_refs, stack_ref, part_ref = rest[z.targets + 1:-2], rest[-2], rest[-1]
     me = lax.axis_index("strike")
     place, group = me % WIN, me // WIN
     spare = jnp.zeros((z.chunk_rows - z.spectral, 2 * LANES), f32)
@@ -270,51 +322,43 @@
     for ref in window:
         both = ref[pl.ds(z.plane_rows, 2 * z.spectral), :].astype(f32)
         lines += [jnp.concatenate([both[:z.spectral], both[z.spectral:]], axis=1), spare]
-    offset = node_offset(lax.broadcasted_iota(jnp.int32, (z.span, 2 * LANES), 0))
-    lane = lax.broadcasted_iota(jnp.int32, (z.span, 2 * LANES), 1)
-    wanted = []
-    for w in range(WIN):
-        node = beside_me(place)[w] * z.nodes + offset
-        node = jnp.where(node < 0, node + 2 * LANES, node)
-        wanted.append((lane == node).astype(f32))
     picked = lax.dot_general(
-        jnp.concatenate(wanted, axis=0).astype(bf16),
+        wanted_ref[...],
         jnp.concatenate(lines, axis=0).astype(bf16),
         (((1,), (1,)), ((), ())),
         preferred_element_type=f32,
     )
-    row = lax.broadcasted_iota(jnp.int32, (z.chunk_rows, z.dips), 0)
-    ahead = lax.broadcasted_iota(jnp.int32, (z.chunk_rows, z.dips), 1) - row
     own_rows = z.targets * z.nodes
-    parts = []
-    for c in range(z.parts):
-        inside = (row >= c * z.rows) & (row < (c + 1) * z.rows)
+    for c in range(z.parts):
         for s, ref in enumerate(window):
             source = (group + z.targets - s) % z.targets
             at = pl.multiple_of(source * z.nodes, z.nodes)
             stack_ref[c, pl.ds(at, z.nodes), :] = ref[pl.ds(c * z.nodes, z.nodes), :]
-            spot = inside & (ahead == z.rows * (WIN * source + place) - c * z.rows)
-            at = pl.ds(own_rows + s * z.chunk_rows, z.chunk_rows)
-            stack_ref[c, at, :] = spot.astype(f32).astype(bf16)
+        stack_ref[c, pl.ds(own_rows, z.targets * z.chunk_rows), :] = spots_ref[c]
         factors = jnp.concatenate([toeplitz_ref[c], picked], axis=1).astype(bf16)
-        parts.append(jnp.dot(factors, stack_ref[c], preferred_element_type=f32))
-        mine_ref[pl.ds(c * z.span, z.span), :] = parts[c][:z.span]
-    for w, ref in enumerate(out_refs, 1):
-        ref[...] = jnp.concatenate(
-            [part[w * z.span:(w + 1) * z.span] for part in parts], axis=0
-        ).astype(bf16)
+        part_ref[c] = jnp.dot(factors, stack_ref[c], preferred_element_type=f32)
+    for w, (spot, ref) in enumerate(zip(beside_me(place), (mine_ref,) + out_refs)):
+        at = pl.ds(pl.multiple_of(spot * z.span, 8), z.span)
+        block = jnp.concatenate([part_ref[c, at, :] for c in range(z.parts)], axis=0)
+        ref[...] = block.astype(bf16) if w else block
 
 
 def unpack(z, left_ref, right_ref, uh_ref, vh_ref, mh_ref):
     size = z.layers
-    for ref, at_u, at_v in ((right_ref, 0, 0), (left_ref, TAIL - 3, TAIL - 2)):
+    for ref, is_left in ((right_ref, False), (left_ref, True)):
+        spots = [pl.ds((TAIL - 1 - d if is_left else d) * size, size) for d in range(3)]
         for c in range(z.parts):
-            for j in range(3):
-                both = ref[pl.ds((c * 3 + j) * 2 * size, 2 * size), :].astype(f32)
-                uh_ref[c, pl.ds((at_u + j) * size, size), :] = both[:size] + both[size:]
+            tiles = ref[pl.ds(c * 4 * size, 4 * size), :].astype(f32)
+            known = tiles[:size]
+            for d in range(3):
+                known = known + tiles[(d + 1) * size:(d + 2) * size]
+                uh_ref[c, spots[d], :] = known
             both = ref[pl.ds(z.halo_v + c * 2 * size, 2 * size), :].astype(f32)
-            vh_ref[c, pl.ds(at_v * size, 2 * size), :] = both
-        mh_ref[pl.ds(at_v * size, 2 * size), :] = ref[pl.ds(z.halo_m, 2 * size), :].astype(f32)
+            vh_ref[c, spots[0], :] = both[:size]
+            vh_ref[c, spots[1], :] = both[size:]
+        both = ref[pl.ds(z.halo_m, 2 * size), :].astype(f32)
+        mh_ref[spots[0], :] = both[:size]
+        mh_ref[spots[1], :] = both[size:]
     for c in range(z.parts):
         uh_ref[c, pl.ds(3 * size, 2 * size), :] = jnp.zeros((2 * size, z.dips), f32)
         vh_ref[c, pl.ds(2 * size, 4 * size), :] = jnp.zeros((4 * size, z.dips), f32)
@@ -352,10 +396,58 @@
     return around - 6.0 * values
 
 
-def base_kernel(z, u_ref, v_ref, s_ref, y_ref, c_ref, cross_ref, pair_ref, *rest):
+def substeps(z, fetch, rows, store, m_ref):
+    dip = lax.broadcasted_iota(jnp.int32, (rows, z.dips), 1)
+    first_dip, last_dip = dip == 0, dip == z.dips - 1
+    two = z.sides == 2
+    low = -2 if two else 0
+    top = z.layers
+    for f in range(low, top + 2):
+        m_ref[f - low] = (time_step * time_step) * fetch("m", 0, f)
+
+    for c in range(z.parts):
+        u = {f: fetch("u", c, f) for f in range(low - 1 if two else 0, top + 3)}
+        v = {f: time_step * fetch("v", c, f) for f in range(low, top + 2)}
+        for step in range(SUB):
+            levels = range(low + step if two else 0, top + 2 - step)
+            for f in levels:
+                lap = in_plane(u[f], first_dip, last_dip) + u[f + 1]
+                if f - 1 in u:
+                    lap += u[f - 1]
+                v[f] = v[f] + m_ref[f - low] * lap
+            u = {f: u[f] + v[f] for f in levels}
+        for f in range(top):
+            store(c, f, u[f], (1.0 / time_step) * v[f])
+
+
+def beside_index(z, kind, c, f):
+    side, j = (0, f - z.layers) if f >= z.layers else (1, -1 - f)
+    return side, {"u": 3 * c, "v": 3 * z.parts + 2 * c, "m": 5 * z.parts}[kind] + j
+
+
+def base_kernel(z, u_ref, v_ref, m_ref, *rest):
     sides = rest[:z.sides]
-    out_u, out_v, mf_ref, ch_ref, m_ref, uh_ref, vh_ref, mh_ref, tile_ref = rest[z.sides:]
-    set_modulus(z, s_ref, y_ref, m_ref)
+    out_u, out_v, gathered_ref = rest[z.sides:]
+
+    def fetch(kind, c, f):
+        if 0 <= f < z.layers:
+            first = 0 if kind == "m" else c * z.stride
+            own = {"u": u_ref, "v": v_ref, "m": m_ref}[kind]
+            return own[pl.ds(first + layer_of(z, f), z.nodes, stride=z.layers), :]
+        side, at = beside_index(z, kind, c, f)
+        return sides[side][at]
+
+    def store(c, f, u, v):
+        at = pl.ds(c * z.stride + layer_of(z, f), z.nodes, stride=z.layers)
+        out_u[at, :] = u
+        out_v[at, :] = v
+
+    substeps(z, fetch, z.nodes, store, gathered_ref)
+
+
+def strips_kernel(z, u_ref, v_ref, m_ref, c_ref, cross_ref, pair_ref, *rest):
+    sides = rest[:z.sides]
+    out_u, out_v, mf_ref, ch_ref, uh_ref, vh_ref, mh_ref, tile_ref, gathered_ref = rest[z.sides:]
     place = lax.axis_index("normal")
     is_high = place == z.normal - 1
     is_face = (is_high | (place == 0)).astype(f32)
@@ -365,8 +457,9 @@
         unpack(z, left_ref, right_ref, uh_ref, vh_ref, mh_ref)
         corner_tiles(z, left_ref, right_ref, tile_ref)
         row = lax.broadcasted_iota(jnp.int32, (TAIL, z.dips), 0)
-        before = left_ref[pl.ds(z.halo_c, 16), :].astype(f32)[16 - TAIL:]
-        after = right_ref[pl.ds(z.halo_c, 16), :].astype(f32)[:TAIL]
+        rows = pl.ds(z.corner, z.halo - z.corner)
+        before = left_ref[rows, :].astype(f32)[z.touch:z.touch + TAIL]
+        after = right_ref[rows, :].astype(f32)[z.touch:z.touch + TAIL]
         ch_ref[pl.ds(z.nodes, TAIL), :] = jnp.where(row < TAIL // 2, after, before) * is_face
 
     is_even = lax.axis_index("strike") % 2 == 0
@@ -379,51 +472,38 @@
     def _():
         receive(pair_ref, cross_ref)
 
-    dip = lax.broadcasted_iota(jnp.int32, (z.span, z.dips), 1)
-    first_dip, last_dip = dip == 0, dip == z.dips - 1
-    low = -2 if z.sides == 2 else 0
-    top = z.layers
+    last = z.nodes - TAIL
 
     def fetch(kind, c, f):
-        if 0 <= f < top:
+        if 0 <= f < z.layers:
             layer = layer_of(z, f)
+            first = layer if kind == "m" else c * z.stride + layer
             own = {"u": u_ref, "v": v_ref, "m": m_ref}[kind]
-            first = 0 if kind == "m" else c * z.stride
             tail = mh_ref if kind == "m" else (uh_ref if kind == "u" else vh_ref).at[c]
-            return jnp.concatenate(
-                [
-                    own[pl.ds(first + layer, z.nodes, stride=top), :],
-                    tail[pl.ds(layer, TAIL, stride=top), :],
-                ],
-                axis=0,
-            )
-        side, j = (0, f - top) if f >= top else (1, -1 - f)
-        at = {"u": 3 * c, "v": 3 * z.parts + 2 * c, "m": 5 * z.parts}[kind] + j
-        return jnp.concatenate([sides[side][at], tile_ref[side, at]], axis=0)
-
-    def one_part(c, unused):
-        u = {f: fetch("u", c, f) for f in range(low - 1 if z.sides == 2 else 0, top + 3)}
-        v = {f: fetch("v", c, f) for f in range(low, top + 2)}
-        for step in range(SUB):
-            levels = range(low + step if z.sides == 2 else 0, top + 2 - step)
-            for f in levels:
-                lap = in_plane(u[f], first_dip, last_dip) + u[f + 1]
-                if f - 1 in u:
-                    lap += u[f - 1]
-                v[f] = v[f] + time_step * (fetch("m", c, f) * lap)
-            u = {f: u[f] + time_step * v[f] for f in levels}
-        for f in range(top):
-            at = pl.ds(c * z.stride + layer_of(z, f), z.nodes, stride=z.layers)
-            out_u[at, :] = u[f][:z.nodes]
-            out_v[at, :] = v[f][:z.nodes]
-        return unused
-
-    lax.fori_loop(0, z.parts, one_part, 0)
+            pieces = [
+                own[pl.ds(first + last * z.layers, TAIL, stride=z.layers), :],
+                tail[pl.ds(layer, TAIL, stride=z.layers), :],
+                own[pl.ds(first, TAIL, stride=z.layers), :],
+            ]
+        else:
+            side, at = beside_index(z, kind, c, f)
+            edge = sides[side]
+            pieces = [edge[at, pl.ds(last, TAIL), :], tile_ref[side, at], edge[at, pl.ds(0, TAIL), :]]
+        return jnp.concatenate(pieces, axis=0)
+
+    def store(c, f, u, v):
+        for out, x in ((out_u, u), (out_v, v)):
+            out[c, f, pl.ds(0, TAIL), :] = x[2 * TAIL:]
+            out[c, f, pl.ds(TAIL, TAIL), :] = x[:TAIL]
+
+    substeps(z, fetch, 3 * TAIL, store, gathered_ref)
     for f in range(3):
-        mf_ref[f] = fetch("m", 0, f)
-
-
-def final_kernel(z, mine_ref, contact_ref, m_ref, base_u, base_v, *rest):
+        layer = layer_of(z, f)
+        mf_ref[f, pl.ds(0, z.nodes), :] = m_ref[pl.ds(layer, z.nodes, stride=z.layers), :]
+        mf_ref[f, pl.ds(z.nodes, TAIL), :] = mh_ref[pl.ds(layer, TAIL, stride=z.layers), :]
+
+
+def final_kernel(z, mine_ref, contact_ref, m_ref, base_u, base_v, strip_u, strip_v, *rest):
     arrived, (out_u, out_v, u_ref, v_ref, sems) = rest[:-5], rest[-5:]
     dip = lax.broadcasted_iota(jnp.int32, (z.span, z.dips), 1)
     first_dip, last_dip = dip == 0, dip == z.dips - 1
@@ -432,6 +512,7 @@
     h = time_step
     arrived = [ref[...].astype(f32) for ref in arrived]
     copies = []
+    half = TAIL // 2
     for c in range(z.parts):
         force = mine_ref[pl.ds(c * z.span, z.span), :]
         for other in arrived:
@@ -448,8 +529,14 @@
         v1 = v1 + h * (m1 * (in_plane(u1, first_dip, last_dip) + u0))
         pairs = ((u0 + h * w0, w0), (u1 + h * v1, v1), (h * v2, v2))
         part = pl.ds(c * z.stride, z.stride)
-        for k, (base, sums, out) in enumerate(((base_u, u_ref, out_u), (base_v, v_ref, out_v))):
+        whole = ((base_u, strip_u, u_ref, out_u), (base_v, strip_v, v_ref, out_v))
+        for k, (base, strip, sums, out) in enumerate(whole):
             sums[part, :] = base[part, :]
+            for f in range(z.layers):
+                first = c * z.stride + layer_of(z, f)
+                late = first + (z.nodes - half) * z.layers
+                sums[pl.ds(first, half, stride=z.layers), :] = strip[c, f, pl.ds(0, half), :]
+                sums[pl.ds(late, half, stride=z.layers), :] = strip[c, f, pl.ds(2 * TAIL - half, half), :]
             for f in range(3):
                 at = pl.ds(c * z.stride + layer_of(z, f), z.nodes, stride=z.layers)
                 sums[at, :] = sums[at, :] + pairs[f][k][:z.nodes]
@@ -485,13 +572,17 @@
     around = lambda w: [(i, i - i % WIN + beside_me(i % WIN)[w]) for i in range(z.strike)]
 
     edge = (5 * z.parts + 2, z.nodes, z.dips)
-    common, response, *edges_and_others = pl.pallas_call(
+    common, response, modulus, wanted, spots, *edges_and_others = pl.pallas_call(
         functools.partial(common_kernel, z),
-        out_shape=(shape((z.common, LANES), bf16), shape((z.chunks, 8, LANES), f32))
+        out_shape=(shape((z.common, LANES), bf16), shape((z.chunks, 8, LANES), f32), shape(s.shape, f32))
+        + (
+            shape((WIN * z.span, 2 * LANES), bf16),
+            shape((z.parts, z.targets * z.chunk_rows, z.dips), bf16),
+        )
         + (shape(edge, f32),) * z.sides
         + (shape((z.common, LANES), bf16),) * (z.targets - 1),
         in_specs=[HBM] * 7,
-        out_specs=(VMEM,) * (1 + z.sides + z.targets),
+        out_specs=(VMEM,) * (4 + z.sides + z.targets),
         scratch_shapes=[
             pltpu.VMEM(u.shape, f32),
             pltpu.VMEM((z.lags - 1, 2, z.parts, z.rows, z.modes), bf16),
@@ -533,12 +624,11 @@
         functools.partial(halo_kernel, z),
         out_shape=(shape((z.halo, LANES), bf16),) * 2
         + (shape((z.parts, WIN * z.span, z.targets * z.nodes), f32),),
-        in_specs=[VMEM] * (6 + z.sides),
+        in_specs=[VMEM] * (5 + z.sides),
         out_specs=(VMEM,) * 3,
-        scratch_shapes=[pltpu.VMEM((z.parts, z.chunks, WIN, z.span, LANES), f32)],
         compiler_params=PARAMS,
         name="strike_edges_and_toeplitz",
-    )(displacement, velocity, stiffness, y, contact, response, *beside)
+    )(displacement, velocity, modulus, contact, response, *beside)
     from_pair = lax.ppermute(to_pair, "strike", [(i, i ^ 1) for i in range(z.strike)])
     from_cross = lax.ppermute(
         to_cross, "strike", [(i, (i - 1 + i % 2 * 2) % z.strike) for i in range(z.strike)]
@@ -548,47 +638,61 @@
     mine, *parcels = pl.pallas_call(
         functools.partial(middle_kernel, z),
         out_shape=(shape(block, f32),) + (shape(block, bf16),) * (WIN - 1),
-        in_specs=[VMEM] * (1 + z.targets),
+        in_specs=[VMEM] * (3 + z.targets),
         out_specs=(VMEM,) * WIN,
-        scratch_shapes=[pltpu.VMEM((z.parts, z.targets * (z.nodes + z.chunk_rows), z.dips), bf16)],
+        scratch_shapes=[
+            pltpu.VMEM((z.parts, z.targets * (z.nodes + z.chunk_rows), z.dips), bf16),
+            pltpu.VMEM((z.parts, WIN * z.span, z.dips), f32),
+        ],
         compiler_params=PARAMS,
         name="partial_tractions",
-    )(toeplitz, *window[1:], common)
+    )(wanted, spots, toeplitz, *window[1:], common)
 
     arrived = [
         lax.ppermute(parcels[w - 1], "strike", around(w)) for w in (3, 1, 2)
     ]
+    base_u, base_v = pl.pallas_call(
+        functools.partial(base_kernel, z),
+        out_shape=(shape(u.shape, f32),) * 2,
+        in_specs=[VMEM] * (3 + z.sides),
+        out_specs=(VMEM,) * 2,
+        scratch_shapes=[pltpu.VMEM((z.layers + 2 * z.sides, z.nodes, z.dips), f32)],
+        compiler_params=PARAMS,
+        name="unloaded_substeps",
+    )(u, v, modulus, *beside)
+
     tail = (z.parts, TAIL * z.layers, z.dips)
-    base_u, base_v, face_modulus, touching = pl.pallas_call(
-        functools.partial(base_kernel, z),
+    strip = (z.parts, z.layers, 2 * TAIL, z.dips)
+    strip_u, strip_v, face_modulus, touching = pl.pallas_call(
+        functools.partial(strips_kernel, z),
         out_shape=(
-            shape(u.shape, f32),
-            shape(u.shape, f32),
+            shape(strip, f32),
+            shape(strip, f32),
             shape((3, z.span, z.dips), f32),
             shape((z.span, z.dips), f32),
         ),
-        in_specs=[VMEM] * (7 + z.sides),
+        in_specs=[VMEM] * (6 + z.sides),
         out_specs=(VMEM,) * 4,
         scratch_shapes=[
-            pltpu.VMEM(s.shape, f32),
             pltpu.VMEM(tail, f32),
             pltpu.VMEM(tail, f32),
             pltpu.VMEM(tail[1:], f32),
             pltpu.VMEM((z.sides, edge[0], TAIL, z.dips), f32),
+            pltpu.VMEM((z.layers + 2 * z.sides, 3 * TAIL, z.dips), f32),
         ],
         compiler_params=PARAMS,
-        name="unloaded_substeps",
-    )(u, v, s, y, contact, from_cross, from_pair, *beside)
+        name="end_strips",
+    )(u, v, modulus, contact, from_cross, from_pair, *beside)
 
     moved, speed = pl.pallas_call(
         functools.partial(final_kernel, z),
         out_shape=(shape(u.shape, f32),) * 2,
-        in_specs=[VMEM] * (5 + len(arrived)),
+        in_specs=[VMEM] * (7 + len(arrived)),
         out_specs=(HBM,) * 2,
         scratch_shapes=[pltpu.VMEM(u.shape, f32), pltpu.VMEM(u.shape, f32), dma((2 * z.parts,))],
         compiler_params=PARAMS,
         name="add_force_response",
-    )(mine, touching, face_modulus, base_u, base_v, *arrived)
+    )(mine, touching, face_modulus, base_u, base_v, strip_u, strip_v, *arrived)
     return (moved.reshape(displacement.shape), speed.reshape(displacement.shape))
 
 

time: 20.8 us -> 20.6 us (level)
  waiting for transfers between devices: 1.08 us -> 0.64 us
    ppermute x1, waiting for transfers between devices: 1.06 us -> 0.01 us  [body(): lax.ppermute(to_cross, 'strike', [(i, (i - 1 + i % 2 * 2) % z.strike) for...]
    pallas_call x0 -> x1, Pallas kernels: none -> 0.78 us  [body(): pl.pallas_call(functools.partial(strips_kernel, z), out_shape=(shape(stri...]
    ppermute x3, waiting for transfers between devices: 0.01 us -> 0.62 us  [body(): lax.ppermute(parcels[w - 1], 'strike', around(w))]
    pallas_call x1, Pallas kernels: 1.46 us -> 0.96 us  [body(): pl.pallas_call(functools.partial(base_kernel, z), out_shape=(shape(u.shap...]
  transfers between devices with their start and end apart: 9 -> 9, of which waited for: 1 -> 2; matrix products, arithmetic and copies ran while one was open for 0% -> 0% of each run, Pallas kernels for 12% -> 12%
where the time goes in v5:
time: 20.6 us; the launch traced here: 20.5 us
  starting transfers between devices  13.8 us (67%)
  Pallas kernels  5.3 us (26%)
  between operations  0.74 us (4%)
  waiting for transfers between devices  0.64 us (3%)
    ppermute x3, starting transfers between devices, body(): lax.ppermute(other, 'strike', ring(WIN * s))  6.57 us
    ppermute x3, starting transfers between devices, body(): lax.ppermute(parcels[w - 1], 'strike', around(w))  3.66 us
    ppermute x1, starting transfers between devices, body(): lax.ppermute(to_cross, 'strike', [(i, (i - 1 + i % 2 * 2) % z.strike) for...  2.4 us
    pallas_call x1, Pallas kernels, body(): pl.pallas_call(functools.partial(common_kernel, z), out_shape=(shape((z.c...  1.66 us
    pallas_call x1, Pallas kernels, body(): pl.pallas_call(functools.partial(final_kernel, z), out_shape=(shape(u.sha...  1.11 us
    pallas_call x1, Pallas kernels, body(): pl.pallas_call(functools.partial(base_kernel, z), out_shape=(shape(u.shap...  0.96 us
    pallas_call x1, Pallas kernels, body(): pl.pallas_call(functools.partial(strips_kernel, z), out_shape=(shape(stri...  0.78 us
    ppermute x1, starting transfers between devices, body(): lax.ppermute(to_pair, 'strike', [(i, i ^ 1) for i in range(z.strike)])  0.65 us
  transfers between devices with their start and end apart: 9, of which 2 were waited for; matrix products, arithmetic and copies ran while one was open for 0% of the time, Pallas kernels for 12%

profile of v5, /device:TPU:0, one launch (start us, length us, event | category | flops | bytes accessed | tf_op | source)
XLA Modules:
  0.0 20.5 jit_solution(13582572994605394846)
XLA Ops:
  0.6 0.0 copy-start
  0.6 0.0 copy-start.1
  0.7 0.0 copy-start.2
  0.7 1.7 %plane_and_history.1 = (bf16[144,128]{1,0:T(8,128)(2,1)S(1)}, f32[4,8,128]{2,1,0:T(8,128)S(1)}, f32[256,128]{1,0:T(8,128)S(1)}, bf16[160,256]{1,0:T(8,128)(2,1)S...) custom-call(f32[768,128]{1,0:T(8,128)} %bitcast.7, ...), custom_call_target="tpu_custom_call" | custom-call | tf_op jit(solution)/shard_map/plane_and_history/pallas_call | solution.py:575
  2.3 0.5 %collective-permute-start = (f32[17,32,128]{2,1,0:T(8,128)S(1)}, f32[17,32,128]{2,1,0:T(8,128)S(1)}, u32[]{:S(2)}, u32[]{:S(2)}) collective-permute-start(f32[17,32,128]{2,1,0:T(8,128)S(1)} %get-tuple-element.30), channel_id=1, source_target_pairs={{0,1},{1,0},{2,3},{3,2},{4,5},{5,4},{6,7},{7,6},{8,9},{9,8},{10,11... | collective-permute-start | bytes 835592 | tf_op jit(solution)/shard_map/ppermute | solution.py:621
  2.8 2.6 %collective-permute-start.1 = (bf16[144,128]{1,0:T(8,128)(2,1)S(1)}, bf16[144,128]{1,0:T(8,128)(2,1)S(1)}, u32[]{:S(2)}, u32[]{:S(2)}) collective-permute-start(bf16[144,128]{1,0:T(8,128)(2,1)S(1)} %get-tuple-element.32), channel_id=1, source_target_pairs={{0,8},{2,10},{4,12},{6,14},{8,16},{10,18},{12,20},{14,22},{16,24},... | collective-permute-start | bytes 110600 | tf_op jit(solution)/shard_map/ppermute | solution.py:605
  5.5 2.6 %collective-permute-start.2 = (bf16[144,128]{1,0:T(8,128)(2,1)S(1)}, bf16[144,128]{1,0:T(8,128)(2,1)S(1)}, u32[]{:S(2)}, u32[]{:S(2)}) collective-permute-start(bf16[144,128]{1,0:T(8,128)(2,1)S(1)} %get-tuple-element.33), channel_id=1, source_target_pairs={{0,16},{2,18},{4,20},{6,22},{8,24},{10,26},{12,28},{14,30},{16,0},... | collective-permute-start | bytes 110600 | tf_op jit(solution)/shard_map/ppermute | solution.py:605
  8.1 1.3 %collective-permute-start.3 = (bf16[144,128]{1,0:T(8,128)(2,1)S(1)}, bf16[144,128]{1,0:T(8,128)(2,1)S(1)}, u32[]{:S(2)}, u32[]{:S(2)}) collective-permute-start(bf16[144,128]{1,0:T(8,128)(2,1)S(1)} %get-tuple-element.34), channel_id=1, source_target_pairs={{0,24},{2,26},{4,28},{6,30},{8,0},{10,2},{12,4},{14,6},{16,8},{18,... | collective-permute-start | bytes 110600 | tf_op jit(solution)/shard_map/ppermute | solution.py:605
  9.4 0.0 collective-permute-done.rest_0_
  9.4 0.0 copy-done
  9.4 0.0 copy-done.1
  9.4 0.0 copy-done.2
  9.4 0.4 %strike_edges_and_toeplitz.1 = (bf16[192,128]{1,0:T(8,128)(2,1)S(1)}, bf16[192,128]{1,0:T(8,128)(2,1)S(1)}, f32[3,160,128]{2,1,0:T(8,128)S(1)}) custom-call(f32[3,32,8,128]{3,2,1,0:T(8,128)S(1)} %copy-done, f32[3,32,8,128]{3,2,1,0:T(8,128)S(1)} %copy-done.1, f32[256,128]{1,0:T(8,128)S(1)} %get-tuple-element.28.m_ref, s32[2,32,128]{2,1,0:T(8,128)S(1)} %copy-done.2, ...), custom_call_target="tpu_custom_call" | custom-call | tf_op jit(solution)/shard_map/strike_edges_and_toeplitz/pallas_call | solution.py:623
  9.8 2.4 %collective-permute-start.4 = (bf16[192,128]{1,0:T(8,128)(2,1)S(1)}, bf16[192,128]{1,0:T(8,128)(2,1)S(1)}, u32[]{:S(2)}, u32[]{:S(2)}) collective-permute-start(bf16[192,128]{1,0:T(8,128)(2,1)S(1)} %get-tuple-element.37), channel_id=1, source_target_pairs={{0,30},{2,4},{4,2},{6,8},{8,6},{10,12},{12,10},{14,16},{16,14},{18... | collective-permute-start | bytes 147464 | tf_op jit(solution)/shard_map/ppermute | solution.py:633
  12.2 0.7 %collective-permute-start.5 = (bf16[192,128]{1,0:T(8,128)(2,1)S(1)}, bf16[192,128]{1,0:T(8,128)(2,1)S(1)}, u32[]{:S(2)}, u32[]{:S(2)}) collective-permute-start(bf16[192,128]{1,0:T(8,128)(2,1)S(1)} %get-tuple-element.38), channel_id=1, source_target_pairs={{0,2},{2,0},{4,6},{6,4},{8,10},{10,8},{12,14},{14,12},{16,18},{18,... | collective-permute-start | bytes 147464 | tf_op jit(solution)/shard_map/ppermute | solution.py:632
  12.9 0.0 collective-permute-done.1.rest_0_
  12.9 0.0 collective-permute-done.2.rest_1_
  12.9 0.0 collective-permute-done.3.rest_2_
  12.9 0.4 %partial_tractions.1 = (f32[120,128]{1,0:T(8,128)S(1)}, bf16[120,128]{1,0:T(8,128)(2,1)S(1)}, bf16[120,128]{1,0:T(8,128)(2,1)S(1)}, bf16[120,128]{1,0:T(8,128)(2,1)S(1)}) custom-call(bf16[160,256]{1,0:T(8,128)(2,1)S(1)} %get-tuple-element.26.wanted_ref, bf16[3,128,128]{2,1,0:T(8,128)(2,1)S(1)} %get-tuple-element.27.spots_ref, ...), custom_call_target="tpu_custom_call" | custom-call | tf_op jit(solution)/shard_map/partial_tractions/pallas_call | solution.py:638
  13.3 1.6 %collective-permute-start.6 = (bf16[120,128]{1,0:T(8,128)(2,1)S(1)}, bf16[120,128]{1,0:T(8,128)(2,1)S(1)}, u32[]{:S(2)}, u32[]{:S(2)}) collective-permute-start(bf16[120,128]{1,0:T(8,128)(2,1)S(1)} %get-tuple-element.45), channel_id=1, source_target_pairs={{0,6},{2,4},{4,2},{6,0},{8,14},{10,12},{12,10},{14,8},{16,22},{18,... | collective-permute-start | bytes 92168 | tf_op jit(solution)/shard_map/ppermute | solution.py:652
  14.9 0.5 %collective-permute-start.7 = (bf16[120,128]{1,0:T(8,128)(2,1)S(1)}, bf16[120,128]{1,0:T(8,128)(2,1)S(1)}, u32[]{:S(2)}, u32[]{:S(2)}) collective-permute-start(bf16[120,128]{1,0:T(8,128)(2,1)S(1)} %get-tuple-element.46), channel_id=1, source_target_pairs={{0,2},{2,6},{4,0},{6,4},{8,10},{10,14},{12,8},{14,12},{16,18},{18,... | collective-permute-start | bytes 92168 | tf_op jit(solution)/shard_map/ppermute | solution.py:652
  15.5 1.5 %collective-permute-start.8 = (bf16[120,128]{1,0:T(8,128)(2,1)S(1)}, bf16[120,128]{1,0:T(8,128)(2,1)S(1)}, u32[]{:S(2)}, u32[]{:S(2)}) collective-permute-start(bf16[120,128]{1,0:T(8,128)(2,1)S(1)} %get-tuple-element.47), channel_id=1, source_target_pairs={{0,4},{2,0},{4,6},{6,2},{8,12},{10,8},{12,14},{14,10},{16,20},{18,... | collective-permute-start | bytes 92168 | tf_op jit(solution)/shard_map/ppermute | solution.py:652
  17.0 1.0 %unloaded_substeps.1 = (f32[768,128]{1,0:T(8,128)S(1)}, f32[768,128]{1,0:T(8,128)S(1)}) custom-call(f32[768,128]{1,0:T(8,128)S(1)} %bitcast.8, f32[768,128]{1,0:T(8,128)S(1)} %bitcast.11, f32[256,128]{1,0:T(8,128)S(1)} %get-tuple-element.28.m_ref, f32[17,32,128]{2,1,0:T(8,128)S(1)} %collective-permute-done.rest_0_), custom_call_target="tpu_custom_call" | custom-call | tf_op jit(solution)/shard_map/unloaded_substeps/pallas_call | solution.py:654
  17.9 0.0 collective-permute-done.4.cross_ref
  17.9 0.0 collective-permute-done.5.pair_ref
  18.0 0.8 %end_strips.1 = (f32[3,8,16,128]{3,2,1,0:T(8,128)S(1)}, f32[3,8,16,128]{3,2,1,0:T(8,128)S(1)}, f32[3,40,128]{2,1,0:T(8,128)S(1)}, f32[40,128]{1,0:T(8,128)S(1)}) custom-call(f32[768,128]{1,0:T(8,128)S(1)} %bitcast.9, f32[768,128]{1,0:T(8,128)S(1)} %bitcast.12, f32[256,128]{1,0:T(8,128)S(1)} %get-tuple-element.28.m_ref, s32[2,32,128]{2,1,0:T(8,128)S(1)} %copy-done.2, ...), custom_call_target="tpu_custom_call" | custom-call | tf_op jit(solution)/shard_map/end_strips/pallas_call | solution.py:666
  18.7 0.0 collective-permute-done.6.rest_0_
  18.7 0.1 collective-permute-done.7.rest_1_
  18.8 0.5 %collective-permute-done.8.rest_2_ = bf16[120,128]{1,0:T(8,128)(2,1)S(1)} collective-permute-done((bf16[120,128]{1,0:T(8,128)(2,1)S(1)}, bf16[120,128]{1,0:T(8,128)(2,1)S(1)}, u32[]{:S(2)}, u32[]{:S(2)}) %collective-permute-start.8) | collective-permute-done | bytes 30752 | tf_op jit(solution)/shard_map/ppermute | solution.py:652
  19.4 1.1 %add_force_response.1 = (f32[768,128]{1,0:T(8,128)}, f32[768,128]{1,0:T(8,128)}) custom-call(f32[120,128]{1,0:T(8,128)S(1)} %get-tuple-element.36.mine_ref, f32[40,128]{1,0:T(8,128)S(1)} %get-tuple-element.39.contact_ref, f32[3,40,128]{2,1,0:T(8,128)S(1)} %get-tuple-element.40.m_ref, f32[768,128]{1,0:T(8,128)S(1)} %get-tuple-element.41.base_u, ...), custom_call_target="tpu_custom_call" | custom-call | tf_op jit(solution)/shard_map/add_force_response/pallas_call | solution.py:687
Async XLA Ops:
  0.6 8.8 %copy-start = (f32[3,32,8,128]{3,2,1,0:T(8,128)S(1)}, f32[3,32,8,128]{3,2,1,0:T(8,128)}, u32[]{:S(2)}) copy-start(f32[3,32,8,128]{3,2,1,0:T(8,128)} %u_ref.1) | copy-start | bytes 1179652
  0.6 8.8 %copy-start.1 = (f32[3,32,8,128]{3,2,1,0:T(8,128)S(1)}, f32[3,32,8,128]{3,2,1,0:T(8,128)}, u32[]{:S(2)}) copy-start(f32[3,32,8,128]{3,2,1,0:T(8,128)} %v_ref.1) | copy-start | bytes 1179652
  0.7 8.8 %copy-start.2 = (s32[2,32,128]{2,1,0:T(8,128)S(1)}, s32[2,32,128]{2,1,0:T(8,128)}, u32[]{:S(2)}) copy-start(s32[2,32,128]{2,1,0:T(8,128)} %c_ref.3) | copy-start | bytes 98308
  2.3 7.1 %collective-permute-start = (f32[17,32,128]{2,1,0:T(8,128)S(1)}, f32[17,32,128]{2,1,0:T(8,128)S(1)}, u32[]{:S(2)}, u32[]{:S(2)}) collective-permute-start(f32[17,32,128]{2,1,0:T(8,128)S(1)} %get-tuple-element.30), channel_id=1, source_target_pairs={{0,1},{1,0},{2,3},{3,2},{4,5},{5,4},{6,7},{7,6},{8,9},{9,8},{10,11... | collective-permute-start | bytes 835592 | tf_op jit(solution)/shard_map/ppermute | solution.py:621
  2.8 10.1 %collective-permute-start.1 = (bf16[144,128]{1,0:T(8,128)(2,1)S(1)}, bf16[144,128]{1,0:T(8,128)(2,1)S(1)}, u32[]{:S(2)}, u32[]{:S(2)}) collective-permute-start(bf16[144,128]{1,0:T(8,128)(2,1)S(1)} %get-tuple-element.32), channel_id=1, source_target_pairs={{0,8},{2,10},{4,12},{6,14},{8,16},{10,18},{12,20},{14,22},{16,24},... | collective-permute-start | bytes 110600 | tf_op jit(solution)/shard_map/ppermute | solution.py:605
  5.5 7.4 %collective-permute-start.2 = (bf16[144,128]{1,0:T(8,128)(2,1)S(1)}, bf16[144,128]{1,0:T(8,128)(2,1)S(1)}, u32[]{:S(2)}, u32[]{:S(2)}) collective-permute-start(bf16[144,128]{1,0:T(8,128)(2,1)S(1)} %get-tuple-element.33), channel_id=1, source_target_pairs={{0,16},{2,18},{4,20},{6,22},{8,24},{10,26},{12,28},{14,30},{16,0},... | collective-permute-start | bytes 110600 | tf_op jit(solution)/shard_map/ppermute | solution.py:605
  8.1 4.8 %collective-permute-start.3 = (bf16[144,128]{1,0:T(8,128)(2,1)S(1)}, bf16[144,128]{1,0:T(8,128)(2,1)S(1)}, u32[]{:S(2)}, u32[]{:S(2)}) collective-permute-start(bf16[144,128]{1,0:T(8,128)(2,1)S(1)} %get-tuple-element.34), channel_id=1, source_target_pairs={{0,24},{2,26},{4,28},{6,30},{8,0},{10,2},{12,4},{14,6},{16,8},{18,... | collective-permute-start | bytes 110600 | tf_op jit(solution)/shard_map/ppermute | solution.py:605
  9.8 8.1 %collective-permute-start.4 = (bf16[192,128]{1,0:T(8,128)(2,1)S(1)}, bf16[192,128]{1,0:T(8,128)(2,1)S(1)}, u32[]{:S(2)}, u32[]{:S(2)}) collective-permute-start(bf16[192,128]{1,0:T(8,128)(2,1)S(1)} %get-tuple-element.37), channel_id=1, source_target_pairs={{0,30},{2,4},{4,2},{6,8},{8,6},{10,12},{12,10},{14,16},{16,14},{18... | collective-permute-start | bytes 147464 | tf_op jit(solution)/shard_map/ppermute | solution.py:633
  12.2 5.7 %collective-permute-start.5 = (bf16[192,128]{1,0:T(8,128)(2,1)S(1)}, bf16[192,128]{1,0:T(8,128)(2,1)S(1)}, u32[]{:S(2)}, u32[]{:S(2)}) collective-permute-start(bf16[192,128]{1,0:T(8,128)(2,1)S(1)} %get-tuple-element.38), channel_id=1, source_target_pairs={{0,2},{2,0},{4,6},{6,4},{8,10},{10,8},{12,14},{14,12},{16,18},{18,... | collective-permute-start | bytes 147464 | tf_op jit(solution)/shard_map/ppermute | solution.py:632
  13.3 5.4 %collective-permute-start.6 = (bf16[120,128]{1,0:T(8,128)(2,1)S(1)}, bf16[120,128]{1,0:T(8,128)(2,1)S(1)}, u32[]{:S(2)}, u32[]{:S(2)}) collective-permute-start(bf16[120,128]{1,0:T(8,128)(2,1)S(1)} %get-tuple-element.45), channel_id=1, source_target_pairs={{0,6},{2,4},{4,2},{6,0},{8,14},{10,12},{12,10},{14,8},{16,22},{18,... | collective-permute-start | bytes 92168 | tf_op jit(solution)/shard_map/ppermute | solution.py:652
  14.9 3.9 %collective-permute-start.7 = (bf16[120,128]{1,0:T(8,128)(2,1)S(1)}, bf16[120,128]{1,0:T(8,128)(2,1)S(1)}, u32[]{:S(2)}, u32[]{:S(2)}) collective-permute-start(bf16[120,128]{1,0:T(8,128)(2,1)S(1)} %get-tuple-element.46), channel_id=1, source_target_pairs={{0,2},{2,6},{4,0},{6,4},{8,10},{10,14},{12,8},{14,12},{16,18},{18,... | collective-permute-start | bytes 92168 | tf_op jit(solution)/shard_map/ppermute | solution.py:652
  15.5 3.9 %collective-permute-start.8 = (bf16[120,128]{1,0:T(8,128)(2,1)S(1)}, bf16[120,128]{1,0:T(8,128)(2,1)S(1)}, u32[]{:S(2)}, u32[]{:S(2)}) collective-permute-start(bf16[120,128]{1,0:T(8,128)(2,1)S(1)} %get-tuple-element.47), channel_id=1, source_target_pairs={{0,4},{2,0},{4,6},{6,2},{8,12},{10,8},{12,14},{14,10},{16,20},{18,... | collective-permute-start | bytes 92168 | tf_op jit(solution)/shard_map/ppermute | solution.py:652

commit v6 on v5

--- a/solution.py
+++ b/solution.py
@@ -1,4 +1,5 @@
 import functools
+import itertools
 import math
 
 import jax
@@ -44,7 +45,7 @@
         self.spectral = round_up(self.parts * self.rows, 8)
         self.chunk_rows = round_up(self.spectral + 2 * self.parts, 16)
         self.plane_rows = self.parts * self.nodes
-        self.common = self.plane_rows + 2 * self.spectral
+        self.common = self.plane_rows + round_up(3 * self.spectral, 16)
         self.halo_v = self.parts * 4 * self.layers
         self.halo_m = self.halo_v + self.parts * 2 * self.layers
         self.corner = self.halo_m + 2 * self.layers
@@ -85,6 +86,11 @@
     for copy in copies:
         copy.start()
     return copies
+
+
+def high_and_rest(values):
+    high = values.astype(bf16)
+    return high, (values - high.astype(f32)).astype(bf16)
 
 
 def set_modulus(z, s_ref, y_ref, out_ref):
@@ -162,9 +168,11 @@
             jnp.concatenate([re * one + im * two, im * one - re * two], axis=1),
         ],
         axis=0,
-    ).astype(bf16)
+    )
     copies[2].wait()
-    lines = jnp.dot(turned, t_ref[...], preferred_element_type=f32) * (1.0 / math.sqrt(z.modes))
+    lines = sum(
+        jnp.dot(part, t_ref[...], preferred_element_type=f32) for part in high_and_rest(turned)
+    ) * (1.0 / math.sqrt(z.modes))
     per_quarter = z.chunks // 4
     for m in range(4):
         for q in range(per_quarter):
@@ -180,7 +188,12 @@
         both = jnp.concatenate(
             [line_ref[chunk], jnp.where(lane < LANES // 2, after, before)], axis=0
         )
-        ref[pl.ds(z.plane_rows, 2 * z.spectral), :] = both.astype(bf16)
+        high, rest = (part.astype(f32) for part in high_and_rest(both))
+        pieces = [high, rest[:z.spectral]]
+        spare = z.common - z.plane_rows - 3 * z.spectral
+        pieces += [jnp.zeros((spare, LANES), f32)] if spare else []
+        at = pl.ds(z.plane_rows, z.common - z.plane_rows)
+        ref[at, :] = jnp.concatenate(pieces, axis=0).astype(bf16)
     copies[3].wait()
     layer = face * (z.layers - 1)
     for c in range(z.parts):
@@ -319,9 +332,11 @@
     place, group = me % WIN, me // WIN
     spare = jnp.zeros((z.chunk_rows - z.spectral, 2 * LANES), f32)
     lines = []
-    for ref in window:
-        both = ref[pl.ds(z.plane_rows, 2 * z.spectral), :].astype(f32)
-        lines += [jnp.concatenate([both[:z.spectral], both[z.spectral:]], axis=1), spare]
+    size = z.spectral
+    for j, ref in itertools.product(range(2), window):
+        part = ref[pl.ds(z.plane_rows, z.common - z.plane_rows), :].astype(f32)
+        near = part[size:2 * size] if j == 0 else jnp.zeros((size, LANES), f32)
+        lines += [jnp.concatenate([part[2 * j * size:(2 * j + 1) * size], near], axis=1), spare]
     picked = lax.dot_general(
         wanted_ref[...],
         jnp.concatenate(lines, axis=0).astype(bf16),
@@ -333,14 +348,17 @@
         for s, ref in enumerate(window):
             source = (group + z.targets - s) % z.targets
             at = pl.multiple_of(source * z.nodes, z.nodes)
-            stack_ref[c, pl.ds(at, z.nodes), :] = ref[pl.ds(c * z.nodes, z.nodes), :]
-        stack_ref[c, pl.ds(own_rows, z.targets * z.chunk_rows), :] = spots_ref[c]
-        factors = jnp.concatenate([toeplitz_ref[c], picked], axis=1).astype(bf16)
+            plane = ref[pl.ds(c * z.nodes, z.nodes), :]
+            stack_ref[c, pl.ds(at, z.nodes), :] = plane
+            stack_ref[c, pl.ds(at + own_rows, z.nodes), :] = plane
+        for j in range(2):
+            at = pl.ds(2 * own_rows + j * z.targets * z.chunk_rows, z.targets * z.chunk_rows)
+            stack_ref[c, at, :] = spots_ref[c]
+        factors = jnp.concatenate([*high_and_rest(toeplitz_ref[c]), picked.astype(bf16)], axis=1)
         part_ref[c] = jnp.dot(factors, stack_ref[c], preferred_element_type=f32)
-    for w, (spot, ref) in enumerate(zip(beside_me(place), (mine_ref,) + out_refs)):
+    for spot, ref in zip(beside_me(place), (mine_ref,) + out_refs):
         at = pl.ds(pl.multiple_of(spot * z.span, 8), z.span)
-        block = jnp.concatenate([part_ref[c, at, :] for c in range(z.parts)], axis=0)
-        ref[...] = block.astype(bf16) if w else block
+        ref[...] = jnp.concatenate([part_ref[c, at, :] for c in range(z.parts)], axis=0)
 
 
 def unpack(z, left_ref, right_ref, uh_ref, vh_ref, mh_ref):
@@ -510,7 +528,7 @@
     contact = contact_ref[...]
     m0, m1, m2 = m_ref[0], m_ref[1], m_ref[2]
     h = time_step
-    arrived = [ref[...].astype(f32) for ref in arrived]
+    arrived = [ref[...] for ref in arrived]
     copies = []
     half = TAIL // 2
     for c in range(z.parts):
@@ -557,6 +575,11 @@
     return [pltpu.with_memory_space_constraint(x, pltpu.HBM) for x in arrays]
 
 
+def pass_kernel(*refs):
+    for in_ref, out_ref in zip(refs[:2], refs[2:]):
+        out_ref[...] = in_ref[...]
+
+
 def shape(dims, kind):
     return jax.ShapeDtypeStruct(dims, kind)
 
@@ -637,11 +660,11 @@
     block = (z.parts * z.span, z.dips)
     mine, *parcels = pl.pallas_call(
         functools.partial(middle_kernel, z),
-        out_shape=(shape(block, f32),) + (shape(block, bf16),) * (WIN - 1),
+        out_shape=(shape(block, f32),) + (shape(block, f32),) * (WIN - 1),
         in_specs=[VMEM] * (3 + z.targets),
         out_specs=(VMEM,) * WIN,
         scratch_shapes=[
-            pltpu.VMEM((z.parts, z.targets * (z.nodes + z.chunk_rows), z.dips), bf16),
+            pltpu.VMEM((z.parts, 2 * z.targets * (z.nodes + z.chunk_rows), z.dips), bf16),
             pltpu.VMEM((z.parts, WIN * z.span, z.dips), f32),
         ],
         compiler_params=PARAMS,
@@ -663,6 +686,15 @@
 
     tail = (z.parts, TAIL * z.layers, z.dips)
     strip = (z.parts, z.layers, 2 * TAIL, z.dips)
+    halos = pl.pallas_call(
+        pass_kernel,
+        out_shape=(shape(from_cross.shape, bf16),) * 2,
+        in_specs=[VMEM] * 2,
+        out_specs=(VMEM,) * 2,
+        cost_estimate=pl.CostEstimate(flops=400000000, bytes_accessed=400000000, transcendentals=0),
+        compiler_params=PARAMS,
+        name="strike_halos",
+    )(from_cross, from_pair)
     strip_u, strip_v, face_modulus, touching = pl.pallas_call(
         functools.partial(strips_kernel, z),
         out_shape=(
@@ -682,7 +714,7 @@
         ],
         compiler_params=PARAMS,
         name="end_strips",
-    )(u, v, modulus, contact, from_cross, from_pair, *beside)
+    )(u, v, modulus, contact, *halos, *beside)
 
     moved, speed = pl.pallas_call(
         functools.partial(final_kernel, z),

time: 20.6 us -> 21.3 us (1.034)
  waiting for transfers between devices: 0.64 us -> 0.96 us
    ppermute x3, waiting for transfers between devices: 0.62 us -> 0.94 us  [body(): lax.ppermute(parcels[w - 1], 'strike', around(w))]
  transfers between devices with their start and end apart: 9 -> 9, of which waited for: 2 -> 3; matrix products, arithmetic and copies ran while one was open for 0% -> 0% of each run, Pallas kernels for 12% -> 12%
where the time goes in v6:
time: 21.3 us; the launch traced here: 21.2 us
  starting transfers between devices  14 us (66%)
  Pallas kernels  5.46 us (26%)
  waiting for transfers between devices  0.96 us (5%)
  between operations  0.74 us (3%)
    ppermute x3, starting transfers between devices, body(): lax.ppermute(other, 'strike', ring(WIN * s))  6.57 us
    ppermute x3, starting transfers between devices, body(): lax.ppermute(parcels[w - 1], 'strike', around(w))  3.86 us
    ppermute x1, starting transfers between devices, body(): lax.ppermute(to_cross, 'strike', [(i, (i - 1 + i % 2 * 2) % z.strike) for...  2.4 us
    pallas_call x1, Pallas kernels, body(): pl.pallas_call(functools.partial(common_kernel, z), out_shape=(shape((z.c...  1.72 us
    pallas_call x1, Pallas kernels, body(): pl.pallas_call(functools.partial(final_kernel, z), out_shape=(shape(u.sha...  1.11 us
    pallas_call x1, Pallas kernels, body(): pl.pallas_call(functools.partial(base_kernel, z), out_shape=(shape(u.shap...  0.96 us
    ppermute x3, waiting for transfers between devices, body(): lax.ppermute(parcels[w - 1], 'strike', around(w))  0.94 us
    pallas_call x1, Pallas kernels, body(): pl.pallas_call(functools.partial(strips_kernel, z), out_shape=(shape(stri...  0.78 us
  transfers between devices with their start and end apart: 9, of which 3 were waited for; matrix products, arithmetic and copies ran while one was open for 0% of the time, Pallas kernels for 12%

profile of v6, /device:TPU:0, one launch (start us, length us, event | category | flops | bytes accessed | tf_op | source)
XLA Modules:
  0.0 21.2 jit_solution(15908433434072936732)
XLA Ops:
  0.6 0.0 copy-start
  0.6 0.0 copy-start.1
  0.7 0.0 copy-start.2
  0.7 1.7 %plane_and_history.1 = (bf16[176,128]{1,0:T(8,128)(2,1)S(1)}, f32[4,8,128]{2,1,0:T(8,128)S(1)}, f32[256,128]{1,0:T(8,128)S(1)}, bf16[160,256]{1,0:T(8,128)(2,1)S...) custom-call(f32[768,128]{1,0:T(8,128)} %bitcast.7, ...), custom_call_target="tpu_custom_call" | custom-call | tf_op jit(solution)/shard_map/plane_and_history/pallas_call | solution.py:598
  2.4 0.5 %collective-permute-start = (f32[17,32,128]{2,1,0:T(8,128)S(1)}, f32[17,32,128]{2,1,0:T(8,128)S(1)}, u32[]{:S(2)}, u32[]{:S(2)}) collective-permute-start(f32[17,32,128]{2,1,0:T(8,128)S(1)} %get-tuple-element.32), channel_id=1, source_target_pairs={{0,1},{1,0},{2,3},{3,2},{4,5},{5,4},{6,7},{7,6},{8,9},{9,8},{10,11... | collective-permute-start | bytes 835592 | tf_op jit(solution)/shard_map/ppermute | solution.py:644
  2.9 2.6 %collective-permute-start.1 = (bf16[176,128]{1,0:T(8,128)(2,1)S(1)}, bf16[176,128]{1,0:T(8,128)(2,1)S(1)}, u32[]{:S(2)}, u32[]{:S(2)}) collective-permute-start(bf16[176,128]{1,0:T(8,128)(2,1)S(1)} %get-tuple-element.34), channel_id=1, source_target_pairs={{0,8},{2,10},{4,12},{6,14},{8,16},{10,18},{12,20},{14,22},{16,24},... | collective-permute-start | bytes 135176 | tf_op jit(solution)/shard_map/ppermute | solution.py:628
  5.5 2.6 %collective-permute-start.2 = (bf16[176,128]{1,0:T(8,128)(2,1)S(1)}, bf16[176,128]{1,0:T(8,128)(2,1)S(1)}, u32[]{:S(2)}, u32[]{:S(2)}) collective-permute-start(bf16[176,128]{1,0:T(8,128)(2,1)S(1)} %get-tuple-element.35), channel_id=1, source_target_pairs={{0,16},{2,18},{4,20},{6,22},{8,24},{10,26},{12,28},{14,30},{16,0},... | collective-permute-start | bytes 135176 | tf_op jit(solution)/shard_map/ppermute | solution.py:628
  8.1 1.3 %collective-permute-start.3 = (bf16[176,128]{1,0:T(8,128)(2,1)S(1)}, bf16[176,128]{1,0:T(8,128)(2,1)S(1)}, u32[]{:S(2)}, u32[]{:S(2)}) collective-permute-start(bf16[176,128]{1,0:T(8,128)(2,1)S(1)} %get-tuple-element.36), channel_id=1, source_target_pairs={{0,24},{2,26},{4,28},{6,30},{8,0},{10,2},{12,4},{14,6},{16,8},{18,... | collective-permute-start | bytes 135176 | tf_op jit(solution)/shard_map/ppermute | solution.py:628
  9.5 0.0 collective-permute-done.rest_0_
  9.5 0.0 copy-done
  9.5 0.0 copy-done.1
  9.5 0.0 copy-done.2
  9.5 0.4 %strike_edges_and_toeplitz.1 = (bf16[192,128]{1,0:T(8,128)(2,1)S(1)}, bf16[192,128]{1,0:T(8,128)(2,1)S(1)}, f32[3,160,128]{2,1,0:T(8,128)S(1)}) custom-call(f32[3,32,8,128]{3,2,1,0:T(8,128)S(1)} %copy-done, f32[3,32,8,128]{3,2,1,0:T(8,128)S(1)} %copy-done.1, f32[256,128]{1,0:T(8,128)S(1)} %get-tuple-element.30.m_ref, s32[2,32,128]{2,1,0:T(8,128)S(1)} %copy-done.2, ...), custom_call_target="tpu_custom_call" | custom-call | tf_op jit(solution)/shard_map/strike_edges_and_toeplitz/pallas_call | solution.py:646
  9.9 2.4 %collective-permute-start.4 = (bf16[192,128]{1,0:T(8,128)(2,1)S(1)}, bf16[192,128]{1,0:T(8,128)(2,1)S(1)}, u32[]{:S(2)}, u32[]{:S(2)}) collective-permute-start(bf16[192,128]{1,0:T(8,128)(2,1)S(1)} %get-tuple-element.39), channel_id=1, source_target_pairs={{0,30},{2,4},{4,2},{6,8},{8,6},{10,12},{12,10},{14,16},{16,14},{18... | collective-permute-start | bytes 147464 | tf_op jit(solution)/shard_map/ppermute | solution.py:656
  12.3 0.7 %collective-permute-start.5 = (bf16[192,128]{1,0:T(8,128)(2,1)S(1)}, bf16[192,128]{1,0:T(8,128)(2,1)S(1)}, u32[]{:S(2)}, u32[]{:S(2)}) collective-permute-start(bf16[192,128]{1,0:T(8,128)(2,1)S(1)} %get-tuple-element.40), channel_id=1, source_target_pairs={{0,2},{2,0},{4,6},{6,4},{8,10},{10,8},{12,14},{14,12},{16,18},{18,... | collective-permute-start | bytes 147464 | tf_op jit(solution)/shard_map/ppermute | solution.py:655
  13.0 0.0 collective-permute-done.1.rest_0_
  13.0 0.0 collective-permute-done.2.rest_1_
  13.0 0.0 collective-permute-done.3.rest_2_
  13.0 0.5 %partial_tractions.1 = (f32[120,128]{1,0:T(8,128)S(1)}, f32[120,128]{1,0:T(8,128)S(1)}, f32[120,128]{1,0:T(8,128)S(1)}, f32[120,128]{1,0:T(8,128)S(1)}) custom-call(bf16[160,256]{1,0:T(8,128)(2,1)S(1)} %get-tuple-element.28.wanted_ref, bf16[3,128,128]{2,1,0:T(8,128)(2,1)S(1)} %get-tuple-element.29.spots_ref, ...), custom_call_target="tpu_custom_call" | custom-call | tf_op jit(solution)/shard_map/partial_tractions/pallas_call | solution.py:661
  13.5 1.8 %collective-permute-start.6 = (f32[120,128]{1,0:T(8,128)S(1)}, f32[120,128]{1,0:T(8,128)S(1)}, u32[]{:S(2)}, u32[]{:S(2)}) collective-permute-start(f32[120,128]{1,0:T(8,128)S(1)} %get-tuple-element.49), channel_id=1, source_target_pairs={{0,6},{2,4},{4,2},{6,0},{8,14},{10,12},{12,10},{14,8},{16,22},{18,... | collective-permute-start | bytes 184328 | tf_op jit(solution)/shard_map/ppermute | solution.py:675
  15.3 0.5 %collective-permute-start.7 = (f32[120,128]{1,0:T(8,128)S(1)}, f32[120,128]{1,0:T(8,128)S(1)}, u32[]{:S(2)}, u32[]{:S(2)}) collective-permute-start(f32[120,128]{1,0:T(8,128)S(1)} %get-tuple-element.50), channel_id=1, source_target_pairs={{0,2},{2,6},{4,0},{6,4},{8,10},{10,14},{12,8},{14,12},{16,18},{18,... | collective-permute-start | bytes 184328 | tf_op jit(solution)/shard_map/ppermute | solution.py:675
  15.8 1.5 %collective-permute-start.8 = (f32[120,128]{1,0:T(8,128)S(1)}, f32[120,128]{1,0:T(8,128)S(1)}, u32[]{:S(2)}, u32[]{:S(2)}) collective-permute-start(f32[120,128]{1,0:T(8,128)S(1)} %get-tuple-element.51), channel_id=1, source_target_pairs={{0,4},{2,0},{4,6},{6,2},{8,12},{10,8},{12,14},{14,10},{16,20},{18,... | collective-permute-start | bytes 184328 | tf_op jit(solution)/shard_map/ppermute | solution.py:675
  17.3 1.0 %unloaded_substeps.1 = (f32[768,128]{1,0:T(8,128)S(1)}, f32[768,128]{1,0:T(8,128)S(1)}) custom-call(f32[768,128]{1,0:T(8,128)S(1)} %bitcast.8, f32[768,128]{1,0:T(8,128)S(1)} %bitcast.11, f32[256,128]{1,0:T(8,128)S(1)} %get-tuple-element.30.m_ref, f32[17,32,128]{2,1,0:T(8,128)S(1)} %collective-permute-done.rest_0_), custom_call_target="tpu_custom_call" | custom-call | tf_op jit(solution)/shard_map/unloaded_substeps/pallas_call | solution.py:677
  18.3 0.0 collective-permute-done.4.refs_0_
  18.3 0.0 collective-permute-done.5.refs_1_
  18.3 0.8 %end_strips.1 = (f32[3,8,16,128]{3,2,1,0:T(8,128)S(1)}, f32[3,8,16,128]{3,2,1,0:T(8,128)S(1)}, f32[3,40,128]{2,1,0:T(8,128)S(1)}, f32[40,128]{1,0:T(8,128)S(1)}) custom-call(f32[768,128]{1,0:T(8,128)S(1)} %bitcast.9, f32[768,128]{1,0:T(8,128)S(1)} %bitcast.12, f32[256,128]{1,0:T(8,128)S(1)} %get-tuple-element.30.m_ref, s32[2,32,128]{2,1,0:T(8,128)S(1)} %copy-done.2, ...), custom_call_target="tpu_custom_call" | custom-call | tf_op jit(solution)/shard_map/end_strips/pallas_call | solution.py:698
  19.1 0.2 collective-permute-done.6.rest_0_
  19.3 0.5 %collective-permute-done.7.rest_1_ = f32[120,128]{1,0:T(8,128)S(1)} collective-permute-done((f32[120,128]{1,0:T(8,128)S(1)}, f32[120,128]{1,0:T(8,128)S(1)}, u32[]{:S(2)}, u32[]{:S(2)}) %collective-permute-start.7) | collective-permute-done | bytes 61472 | tf_op jit(solution)/shard_map/ppermute | solution.py:675
  19.8 0.3 %collective-permute-done.8.rest_2_ = f32[120,128]{1,0:T(8,128)S(1)} collective-permute-done((f32[120,128]{1,0:T(8,128)S(1)}, f32[120,128]{1,0:T(8,128)S(1)}, u32[]{:S(2)}, u32[]{:S(2)}) %collective-permute-start.8) | collective-permute-done | bytes 61472 | tf_op jit(solution)/shard_map/ppermute | solution.py:675
  20.1 1.1 %add_force_response.1 = (f32[768,128]{1,0:T(8,128)}, f32[768,128]{1,0:T(8,128)}) custom-call(f32[120,128]{1,0:T(8,128)S(1)} %get-tuple-element.38.mine_ref, f32[40,128]{1,0:T(8,128)S(1)} %get-tuple-element.43.contact_ref, f32[3,40,128]{2,1,0:T(8,128)S(1)} %get-tuple-element.44.m_ref, f32[768,128]{1,0:T(8,128)S(1)} %get-tuple-element.45.base_u, ...), custom_call_target="tpu_custom_call" | custom-call | tf_op jit(solution)/shard_map/add_force_response/pallas_call | solution.py:719
  (1 shorter events, 0.0 us)
Async XLA Ops:
  0.6 8.9 %copy-start = (f32[3,32,8,128]{3,2,1,0:T(8,128)S(1)}, f32[3,32,8,128]{3,2,1,0:T(8,128)}, u32[]{:S(2)}) copy-start(f32[3,32,8,128]{3,2,1,0:T(8,128)} %u_ref.1) | copy-start | bytes 1179652
  0.6 8.9 %copy-start.1 = (f32[3,32,8,128]{3,2,1,0:T(8,128)S(1)}, f32[3,32,8,128]{3,2,1,0:T(8,128)}, u32[]{:S(2)}) copy-start(f32[3,32,8,128]{3,2,1,0:T(8,128)} %v_ref.1) | copy-start | bytes 1179652
  0.7 8.8 %copy-start.2 = (s32[2,32,128]{2,1,0:T(8,128)S(1)}, s32[2,32,128]{2,1,0:T(8,128)}, u32[]{:S(2)}) copy-start(s32[2,32,128]{2,1,0:T(8,128)} %c_ref.3) | copy-start | bytes 98308
  2.4 7.1 %collective-permute-start = (f32[17,32,128]{2,1,0:T(8,128)S(1)}, f32[17,32,128]{2,1,0:T(8,128)S(1)}, u32[]{:S(2)}, u32[]{:S(2)}) collective-permute-start(f32[17,32,128]{2,1,0:T(8,128)S(1)} %get-tuple-element.32), channel_id=1, source_target_pairs={{0,1},{1,0},{2,3},{3,2},{4,5},{5,4},{6,7},{7,6},{8,9},{9,8},{10,11... | collective-permute-start | bytes 835592 | tf_op jit(solution)/shard_map/ppermute | solution.py:644
  2.9 10.1 %collective-permute-start.1 = (bf16[176,128]{1,0:T(8,128)(2,1)S(1)}, bf16[176,128]{1,0:T(8,128)(2,1)S(1)}, u32[]{:S(2)}, u32[]{:S(2)}) collective-permute-start(bf16[176,128]{1,0:T(8,128)(2,1)S(1)} %get-tuple-element.34), channel_id=1, source_target_pairs={{0,8},{2,10},{4,12},{6,14},{8,16},{10,18},{12,20},{14,22},{16,24},... | collective-permute-start | bytes 135176 | tf_op jit(solution)/shard_map/ppermute | solution.py:628
  5.5 7.4 %collective-permute-start.2 = (bf16[176,128]{1,0:T(8,128)(2,1)S(1)}, bf16[176,128]{1,0:T(8,128)(2,1)S(1)}, u32[]{:S(2)}, u32[]{:S(2)}) collective-permute-start(bf16[176,128]{1,0:T(8,128)(2,1)S(1)} %get-tuple-element.35), channel_id=1, source_target_pairs={{0,16},{2,18},{4,20},{6,22},{8,24},{10,26},{12,28},{14,30},{16,0},... | collective-permute-start | bytes 135176 | tf_op jit(solution)/shard_map/ppermute | solution.py:628
  8.1 4.8 %collective-permute-start.3 = (bf16[176,128]{1,0:T(8,128)(2,1)S(1)}, bf16[176,128]{1,0:T(8,128)(2,1)S(1)}, u32[]{:S(2)}, u32[]{:S(2)}) collective-permute-start(bf16[176,128]{1,0:T(8,128)(2,1)S(1)} %get-tuple-element.36), channel_id=1, source_target_pairs={{0,24},{2,26},{4,28},{6,30},{8,0},{10,2},{12,4},{14,6},{16,8},{18,... | collective-permute-start | bytes 135176 | tf_op jit(solution)/shard_map/ppermute | solution.py:628
  9.9 8.4 %collective-permute-start.4 = (bf16[192,128]{1,0:T(8,128)(2,1)S(1)}, bf16[192,128]{1,0:T(8,128)(2,1)S(1)}, u32[]{:S(2)}, u32[]{:S(2)}) collective-permute-start(bf16[192,128]{1,0:T(8,128)(2,1)S(1)} %get-tuple-element.39), channel_id=1, source_target_pairs={{0,30},{2,4},{4,2},{6,8},{8,6},{10,12},{12,10},{14,16},{16,14},{18... | collective-permute-start | bytes 147464 | tf_op jit(solution)/shard_map/ppermute | solution.py:656
  12.3 6.0 %collective-permute-start.5 = (bf16[192,128]{1,0:T(8,128)(2,1)S(1)}, bf16[192,128]{1,0:T(8,128)(2,1)S(1)}, u32[]{:S(2)}, u32[]{:S(2)}) collective-permute-start(bf16[192,128]{1,0:T(8,128)(2,1)S(1)} %get-tuple-element.40), channel_id=1, source_target_pairs={{0,2},{2,0},{4,6},{6,4},{8,10},{10,8},{12,14},{14,12},{16,18},{18,... | collective-permute-start | bytes 147464 | tf_op jit(solution)/shard_map/ppermute | solution.py:655
  13.5 5.9 %collective-permute-start.6 = (f32[120,128]{1,0:T(8,128)S(1)}, f32[120,128]{1,0:T(8,128)S(1)}, u32[]{:S(2)}, u32[]{:S(2)}) collective-permute-start(f32[120,128]{1,0:T(8,128)S(1)} %get-tuple-element.49), channel_id=1, source_target_pairs={{0,6},{2,4},{4,2},{6,0},{8,14},{10,12},{12,10},{14,8},{16,22},{18,... | collective-permute-start | bytes 184328 | tf_op jit(solution)/shard_map/ppermute | solution.py:675
  15.3 4.5 %collective-permute-start.7 = (f32[120,128]{1,0:T(8,128)S(1)}, f32[120,128]{1,0:T(8,128)S(1)}, u32[]{:S(2)}, u32[]{:S(2)}) collective-permute-start(f32[120,128]{1,0:T(8,128)S(1)} %get-tuple-element.50), channel_id=1, source_target_pairs={{0,2},{2,6},{4,0},{6,4},{8,10},{10,14},{12,8},{14,12},{16,18},{18,... | collective-permute-start | bytes 184328 | tf_op jit(solution)/shard_map/ppermute | solution.py:675
  15.8 4.2 %collective-permute-start.8 = (f32[120,128]{1,0:T(8,128)S(1)}, f32[120,128]{1,0:T(8,128)S(1)}, u32[]{:S(2)}, u32[]{:S(2)}) collective-permute-start(f32[120,128]{1,0:T(8,128)S(1)} %get-tuple-element.51), channel_id=1, source_target_pairs={{0,4},{2,0},{4,6},{6,2},{8,12},{10,8},{12,14},{14,10},{16,20},{18,... | collective-permute-start | bytes 184328 | tf_op jit(solution)/shard_map/ppermute | solution.py:675

commit v7 on v6

--- a/solution.py
+++ b/solution.py
@@ -218,7 +218,7 @@
 
 def toeplitz_factors(z, g_ref, out_ref):
     me = lax.axis_index("strike")
-    place, group = me % WIN, me // WIN
+    group = me // WIN
     lane = lax.broadcasted_iota(jnp.int32, (8, LANES), 1)
     row = lax.broadcasted_iota(jnp.int32, (8, LANES), 0)
     stack = []
@@ -226,13 +226,12 @@
         line = jnp.concatenate(
             [
                 g_ref[j, pl.ds(c, 1), :] + g_ref[j, pl.ds(z.parts + c, 1), :]
-                for j in range(z.chunks)
+                for j in ((k - group + z.chunks) % z.chunks for k in range(z.chunks))
             ],
             axis=1,
         ) * (1.0 / math.sqrt(z.modes))
         stack.append(jnp.broadcast_to(line, (8, z.modes)))
     wide = pltpu.roll(jnp.concatenate(stack, axis=0), 0, 1, stride=1, stride_axis=0)
-    wide = pltpu.roll(wide, (group * LANES - place * z.nodes + z.modes) % z.modes, 1)
     for c in range(z.parts):
         columns = [wide[8 * c:8 * c + 8, j * LANES:(j + 1) * LANES] for j in range(z.chunks)]
 
@@ -262,13 +261,13 @@
                 tile = piece if k == 0 else jnp.where(lane < first, tile, piece)
             return tile
 
-        for t in range(WIN):
+        for t in range(1 - WIN, WIN):
             for q in range(z.chunks // WIN):
                 for k in range(z.span // 8):
                     tile = eight_rows(t * z.nodes + 8 * k, q)
                     if 8 * k == z.nodes:
                         tile = jnp.where(row < TAIL // 2, tile, eight_rows(t * z.nodes - 8, q))
-                    at = pl.ds(t * z.span + 8 * k, 8)
+                    at = pl.ds((t + WIN - 1) * z.span + 8 * k, 8)
                     out_ref[c, at, q * LANES:(q + 1) * LANES] = tile
 
 
@@ -344,6 +343,7 @@
         preferred_element_type=f32,
     )
     own_rows = z.targets * z.nodes
+    own = pl.ds(pl.multiple_of((WIN - 1 - place) * z.span, 8), WIN * z.span)
     for c in range(z.parts):
         for s, ref in enumerate(window):
             source = (group + z.targets - s) % z.targets
@@ -354,7 +354,7 @@
         for j in range(2):
             at = pl.ds(2 * own_rows + j * z.targets * z.chunk_rows, z.targets * z.chunk_rows)
             stack_ref[c, at, :] = spots_ref[c]
-        factors = jnp.concatenate([*high_and_rest(toeplitz_ref[c]), picked.astype(bf16)], axis=1)
+        factors = jnp.concatenate([*high_and_rest(toeplitz_ref[c, own, :]), picked.astype(bf16)], axis=1)
         part_ref[c] = jnp.dot(factors, stack_ref[c], preferred_element_type=f32)
     for spot, ref in zip(beside_me(place), (mine_ref,) + out_refs):
         at = pl.ds(pl.multiple_of(spot * z.span, 8), z.span)
@@ -646,7 +646,7 @@
     to_pair, to_cross, toeplitz = pl.pallas_call(
         functools.partial(halo_kernel, z),
         out_shape=(shape((z.halo, LANES), bf16),) * 2
-        + (shape((z.parts, WIN * z.span, z.targets * z.nodes), f32),),
+        + (shape((z.parts, (2 * WIN - 1) * z.span, z.targets * z.nodes), f32),),
         in_specs=[VMEM] * (5 + z.sides),
         out_specs=(VMEM,) * 3,
         compiler_params=PARAMS,

time: 21.3 us -> 21.3 us (level)
  no operation moved by 1% of the time
where the time goes in v7:
time: 21.3 us; the launch traced here: 21.2 us
  starting transfers between devices  14 us (66%)
  Pallas kernels  5.42 us (25%)
  waiting for transfers between devices  0.96 us (5%)
  between operations  0.74 us (3%)
    ppermute x3, starting transfers between devices, body(): lax.ppermute(other, 'strike', ring(WIN * s))  6.57 us
    ppermute x3, starting transfers between devices, body(): lax.ppermute(parcels[w - 1], 'strike', around(w))  3.89 us
    ppermute x1, starting transfers between devices, body(): lax.ppermute(to_cross, 'strike', [(i, (i - 1 + i % 2 * 2) % z.strike) for...  2.4 us
    pallas_call x1, Pallas kernels, body(): pl.pallas_call(functools.partial(common_kernel, z), out_shape=(shape((z.c...  1.72 us
    pallas_call x1, Pallas kernels, body(): pl.pallas_call(functools.partial(final_kernel, z), out_shape=(shape(u.sha...  1.11 us
    pallas_call x1, Pallas kernels, body(): pl.pallas_call(functools.partial(base_kernel, z), out_shape=(shape(u.shap...  0.96 us
    ppermute x3, waiting for transfers between devices, body(): lax.ppermute(parcels[w - 1], 'strike', around(w))  0.94 us
    pallas_call x1, Pallas kernels, body(): pl.pallas_call(functools.partial(strips_kernel, z), out_shape=(shape(stri...  0.78 us
  transfers between devices with their start and end apart: 9, of which 3 were waited for; matrix products, arithmetic and copies ran while one was open for 0% of the time, Pallas kernels for 12%

profile of v7, /device:TPU:0, one launch (start us, length us, event | category | flops | bytes accessed | tf_op | source)
XLA Modules:
  0.0 21.2 jit_solution(14249823204691450131)
XLA Ops:
  0.6 0.0 copy-start
  0.6 0.0 copy-start.1
  0.7 0.0 copy-start.2
  0.7 1.7 %plane_and_history.1 = (bf16[176,128]{1,0:T(8,128)(2,1)S(1)}, f32[4,8,128]{2,1,0:T(8,128)S(1)}, f32[256,128]{1,0:T(8,128)S(1)}, bf16[160,256]{1,0:T(8,128)(2,1)S...) custom-call(f32[768,128]{1,0:T(8,128)} %bitcast.7, ...), custom_call_target="tpu_custom_call" | custom-call | tf_op jit(solution)/shard_map/plane_and_history/pallas_call | solution.py:598
  2.4 0.5 %collective-permute-start = (f32[17,32,128]{2,1,0:T(8,128)S(1)}, f32[17,32,128]{2,1,0:T(8,128)S(1)}, u32[]{:S(2)}, u32[]{:S(2)}) collective-permute-start(f32[17,32,128]{2,1,0:T(8,128)S(1)} %get-tuple-element.32), channel_id=1, source_target_pairs={{0,1},{1,0},{2,3},{3,2},{4,5},{5,4},{6,7},{7,6},{8,9},{9,8},{10,11... | collective-permute-start | bytes 835592 | tf_op jit(solution)/shard_map/ppermute | solution.py:644
  2.9 2.6 %collective-permute-start.1 = (bf16[176,128]{1,0:T(8,128)(2,1)S(1)}, bf16[176,128]{1,0:T(8,128)(2,1)S(1)}, u32[]{:S(2)}, u32[]{:S(2)}) collective-permute-start(bf16[176,128]{1,0:T(8,128)(2,1)S(1)} %get-tuple-element.34), channel_id=1, source_target_pairs={{0,8},{2,10},{4,12},{6,14},{8,16},{10,18},{12,20},{14,22},{16,24},... | collective-permute-start | bytes 135176 | tf_op jit(solution)/shard_map/ppermute | solution.py:628
  5.5 2.6 %collective-permute-start.2 = (bf16[176,128]{1,0:T(8,128)(2,1)S(1)}, bf16[176,128]{1,0:T(8,128)(2,1)S(1)}, u32[]{:S(2)}, u32[]{:S(2)}) collective-permute-start(bf16[176,128]{1,0:T(8,128)(2,1)S(1)} %get-tuple-element.35), channel_id=1, source_target_pairs={{0,16},{2,18},{4,20},{6,22},{8,24},{10,26},{12,28},{14,30},{16,0},... | collective-permute-start | bytes 135176 | tf_op jit(solution)/shard_map/ppermute | solution.py:628
  8.1 1.3 %collective-permute-start.3 = (bf16[176,128]{1,0:T(8,128)(2,1)S(1)}, bf16[176,128]{1,0:T(8,128)(2,1)S(1)}, u32[]{:S(2)}, u32[]{:S(2)}) collective-permute-start(bf16[176,128]{1,0:T(8,128)(2,1)S(1)} %get-tuple-element.36), channel_id=1, source_target_pairs={{0,24},{2,26},{4,28},{6,30},{8,0},{10,2},{12,4},{14,6},{16,8},{18,... | collective-permute-start | bytes 135176 | tf_op jit(solution)/shard_map/ppermute | solution.py:628
  9.5 0.0 collective-permute-done.rest_0_
  9.5 0.0 copy-done
  9.5 0.0 copy-done.1
  9.5 0.0 copy-done.2
  9.5 0.4 %strike_edges_and_toeplitz.1 = (bf16[192,128]{1,0:T(8,128)(2,1)S(1)}, bf16[192,128]{1,0:T(8,128)(2,1)S(1)}, f32[3,280,128]{2,1,0:T(8,128)S(1)}) custom-call(f32[3,32,8,128]{3,2,1,0:T(8,128)S(1)} %copy-done, f32[3,32,8,128]{3,2,1,0:T(8,128)S(1)} %copy-done.1, f32[256,128]{1,0:T(8,128)S(1)} %get-tuple-element.30.m_ref, s32[2,32,128]{2,1,0:T(8,128)S(1)} %copy-done.2, ...), custom_call_target="tpu_custom_call" | custom-call | tf_op jit(solution)/shard_map/strike_edges_and_toeplitz/pallas_call | solution.py:646
  9.9 2.4 %collective-permute-start.4 = (bf16[192,128]{1,0:T(8,128)(2,1)S(1)}, bf16[192,128]{1,0:T(8,128)(2,1)S(1)}, u32[]{:S(2)}, u32[]{:S(2)}) collective-permute-start(bf16[192,128]{1,0:T(8,128)(2,1)S(1)} %get-tuple-element.39), channel_id=1, source_target_pairs={{0,30},{2,4},{4,2},{6,8},{8,6},{10,12},{12,10},{14,16},{16,14},{18... | collective-permute-start | bytes 147464 | tf_op jit(solution)/shard_map/ppermute | solution.py:656
  12.3 0.7 %collective-permute-start.5 = (bf16[192,128]{1,0:T(8,128)(2,1)S(1)}, bf16[192,128]{1,0:T(8,128)(2,1)S(1)}, u32[]{:S(2)}, u32[]{:S(2)}) collective-permute-start(bf16[192,128]{1,0:T(8,128)(2,1)S(1)} %get-tuple-element.40), channel_id=1, source_target_pairs={{0,2},{2,0},{4,6},{6,4},{8,10},{10,8},{12,14},{14,12},{16,18},{18,... | collective-permute-start | bytes 147464 | tf_op jit(solution)/shard_map/ppermute | solution.py:655
  12.9 0.0 collective-permute-done.1.rest_0_
  12.9 0.0 collective-permute-done.2.rest_1_
  12.9 0.0 collective-permute-done.3.rest_2_
  12.9 0.5 %partial_tractions.1 = (f32[120,128]{1,0:T(8,128)S(1)}, f32[120,128]{1,0:T(8,128)S(1)}, f32[120,128]{1,0:T(8,128)S(1)}, f32[120,128]{1,0:T(8,128)S(1)}) custom-call(bf16[160,256]{1,0:T(8,128)(2,1)S(1)} %get-tuple-element.28.wanted_ref, bf16[3,128,128]{2,1,0:T(8,128)(2,1)S(1)} %get-tuple-element.29.spots_ref, ...), custom_call_target="tpu_custom_call" | custom-call | tf_op jit(solution)/shard_map/partial_tractions/pallas_call | solution.py:661
  13.4 1.9 %collective-permute-start.6 = (f32[120,128]{1,0:T(8,128)S(1)}, f32[120,128]{1,0:T(8,128)S(1)}, u32[]{:S(2)}, u32[]{:S(2)}) collective-permute-start(f32[120,128]{1,0:T(8,128)S(1)} %get-tuple-element.49), channel_id=1, source_target_pairs={{0,6},{2,4},{4,2},{6,0},{8,14},{10,12},{12,10},{14,8},{16,22},{18,... | collective-permute-start | bytes 184328 | tf_op jit(solution)/shard_map/ppermute | solution.py:675
  15.3 0.5 %collective-permute-start.7 = (f32[120,128]{1,0:T(8,128)S(1)}, f32[120,128]{1,0:T(8,128)S(1)}, u32[]{:S(2)}, u32[]{:S(2)}) collective-permute-start(f32[120,128]{1,0:T(8,128)S(1)} %get-tuple-element.50), channel_id=1, source_target_pairs={{0,2},{2,6},{4,0},{6,4},{8,10},{10,14},{12,8},{14,12},{16,18},{18,... | collective-permute-start | bytes 184328 | tf_op jit(solution)/shard_map/ppermute | solution.py:675
  15.8 1.5 %collective-permute-start.8 = (f32[120,128]{1,0:T(8,128)S(1)}, f32[120,128]{1,0:T(8,128)S(1)}, u32[]{:S(2)}, u32[]{:S(2)}) collective-permute-start(f32[120,128]{1,0:T(8,128)S(1)} %get-tuple-element.51), channel_id=1, source_target_pairs={{0,4},{2,0},{4,6},{6,2},{8,12},{10,8},{12,14},{14,10},{16,20},{18,... | collective-permute-start | bytes 184328 | tf_op jit(solution)/shard_map/ppermute | solution.py:675
  17.3 1.0 %unloaded_substeps.1 = (f32[768,128]{1,0:T(8,128)S(1)}, f32[768,128]{1,0:T(8,128)S(1)}) custom-call(f32[768,128]{1,0:T(8,128)S(1)} %bitcast.8, f32[768,128]{1,0:T(8,128)S(1)} %bitcast.11, f32[256,128]{1,0:T(8,128)S(1)} %get-tuple-element.30.m_ref, f32[17,32,128]{2,1,0:T(8,128)S(1)} %collective-permute-done.rest_0_), custom_call_target="tpu_custom_call" | custom-call | tf_op jit(solution)/shard_map/unloaded_substeps/pallas_call | solution.py:677
  18.3 0.0 collective-permute-done.4.refs_0_
  18.3 0.0 collective-permute-done.5.refs_1_
  18.3 0.8 %end_strips.1 = (f32[3,8,16,128]{3,2,1,0:T(8,128)S(1)}, f32[3,8,16,128]{3,2,1,0:T(8,128)S(1)}, f32[3,40,128]{2,1,0:T(8,128)S(1)}, f32[40,128]{1,0:T(8,128)S(1)}) custom-call(f32[768,128]{1,0:T(8,128)S(1)} %bitcast.9, f32[768,128]{1,0:T(8,128)S(1)} %bitcast.12, f32[256,128]{1,0:T(8,128)S(1)} %get-tuple-element.30.m_ref, s32[2,32,128]{2,1,0:T(8,128)S(1)} %copy-done.2, ...), custom_call_target="tpu_custom_call" | custom-call | tf_op jit(solution)/shard_map/end_strips/pallas_call | solution.py:698
  19.1 0.2 collective-permute-done.6.rest_0_
  19.3 0.5 %collective-permute-done.7.rest_1_ = f32[120,128]{1,0:T(8,128)S(1)} collective-permute-done((f32[120,128]{1,0:T(8,128)S(1)}, f32[120,128]{1,0:T(8,128)S(1)}, u32[]{:S(2)}, u32[]{:S(2)}) %collective-permute-start.7) | collective-permute-done | bytes 61472 | tf_op jit(solution)/shard_map/ppermute | solution.py:675
  19.8 0.3 %collective-permute-done.8.rest_2_ = f32[120,128]{1,0:T(8,128)S(1)} collective-permute-done((f32[120,128]{1,0:T(8,128)S(1)}, f32[120,128]{1,0:T(8,128)S(1)}, u32[]{:S(2)}, u32[]{:S(2)}) %collective-permute-start.8) | collective-permute-done | bytes 61472 | tf_op jit(solution)/shard_map/ppermute | solution.py:675
  20.1 1.1 %add_force_response.1 = (f32[768,128]{1,0:T(8,128)}, f32[768,128]{1,0:T(8,128)}) custom-call(f32[120,128]{1,0:T(8,128)S(1)} %get-tuple-element.38.mine_ref, f32[40,128]{1,0:T(8,128)S(1)} %get-tuple-element.43.contact_ref, f32[3,40,128]{2,1,0:T(8,128)S(1)} %get-tuple-element.44.m_ref, f32[768,128]{1,0:T(8,128)S(1)} %get-tuple-element.45.base_u, ...), custom_call_target="tpu_custom_call" | custom-call | tf_op jit(solution)/shard_map/add_force_response/pallas_call | solution.py:719
  (1 shorter events, 0.0 us)
Async XLA Ops:
  0.6 8.9 %copy-start = (f32[3,32,8,128]{3,2,1,0:T(8,128)S(1)}, f32[3,32,8,128]{3,2,1,0:T(8,128)}, u32[]{:S(2)}) copy-start(f32[3,32,8,128]{3,2,1,0:T(8,128)} %u_ref.1) | copy-start | bytes 1179652
  0.6 8.9 %copy-start.1 = (f32[3,32,8,128]{3,2,1,0:T(8,128)S(1)}, f32[3,32,8,128]{3,2,1,0:T(8,128)}, u32[]{:S(2)}) copy-start(f32[3,32,8,128]{3,2,1,0:T(8,128)} %v_ref.1) | copy-start | bytes 1179652
  0.7 8.8 %copy-start.2 = (s32[2,32,128]{2,1,0:T(8,128)S(1)}, s32[2,32,128]{2,1,0:T(8,128)}, u32[]{:S(2)}) copy-start(s32[2,32,128]{2,1,0:T(8,128)} %c_ref.3) | copy-start | bytes 98308
  2.4 7.1 %collective-permute-start = (f32[17,32,128]{2,1,0:T(8,128)S(1)}, f32[17,32,128]{2,1,0:T(8,128)S(1)}, u32[]{:S(2)}, u32[]{:S(2)}) collective-permute-start(f32[17,32,128]{2,1,0:T(8,128)S(1)} %get-tuple-element.32), channel_id=1, source_target_pairs={{0,1},{1,0},{2,3},{3,2},{4,5},{5,4},{6,7},{7,6},{8,9},{9,8},{10,11... | collective-permute-start | bytes 835592 | tf_op jit(solution)/shard_map/ppermute | solution.py:644
  2.9 10.0 %collective-permute-start.1 = (bf16[176,128]{1,0:T(8,128)(2,1)S(1)}, bf16[176,128]{1,0:T(8,128)(2,1)S(1)}, u32[]{:S(2)}, u32[]{:S(2)}) collective-permute-start(bf16[176,128]{1,0:T(8,128)(2,1)S(1)} %get-tuple-element.34), channel_id=1, source_target_pairs={{0,8},{2,10},{4,12},{6,14},{8,16},{10,18},{12,20},{14,22},{16,24},... | collective-permute-start | bytes 135176 | tf_op jit(solution)/shard_map/ppermute | solution.py:628
  5.5 7.4 %collective-permute-start.2 = (bf16[176,128]{1,0:T(8,128)(2,1)S(1)}, bf16[176,128]{1,0:T(8,128)(2,1)S(1)}, u32[]{:S(2)}, u32[]{:S(2)}) collective-permute-start(bf16[176,128]{1,0:T(8,128)(2,1)S(1)} %get-tuple-element.35), channel_id=1, source_target_pairs={{0,16},{2,18},{4,20},{6,22},{8,24},{10,26},{12,28},{14,30},{16,0},... | collective-permute-start | bytes 135176 | tf_op jit(solution)/shard_map/ppermute | solution.py:628
  8.1 4.8 %collective-permute-start.3 = (bf16[176,128]{1,0:T(8,128)(2,1)S(1)}, bf16[176,128]{1,0:T(8,128)(2,1)S(1)}, u32[]{:S(2)}, u32[]{:S(2)}) collective-permute-start(bf16[176,128]{1,0:T(8,128)(2,1)S(1)} %get-tuple-element.36), channel_id=1, source_target_pairs={{0,24},{2,26},{4,28},{6,30},{8,0},{10,2},{12,4},{14,6},{16,8},{18,... | collective-permute-start | bytes 135176 | tf_op jit(solution)/shard_map/ppermute | solution.py:628
  9.9 8.4 %collective-permute-start.4 = (bf16[192,128]{1,0:T(8,128)(2,1)S(1)}, bf16[192,128]{1,0:T(8,128)(2,1)S(1)}, u32[]{:S(2)}, u32[]{:S(2)}) collective-permute-start(bf16[192,128]{1,0:T(8,128)(2,1)S(1)} %get-tuple-element.39), channel_id=1, source_target_pairs={{0,30},{2,4},{4,2},{6,8},{8,6},{10,12},{12,10},{14,16},{16,14},{18... | collective-permute-start | bytes 147464 | tf_op jit(solution)/shard_map/ppermute | solution.py:656
  12.3 6.0 %collective-permute-start.5 = (bf16[192,128]{1,0:T(8,128)(2,1)S(1)}, bf16[192,128]{1,0:T(8,128)(2,1)S(1)}, u32[]{:S(2)}, u32[]{:S(2)}) collective-permute-start(bf16[192,128]{1,0:T(8,128)(2,1)S(1)} %get-tuple-element.40), channel_id=1, source_target_pairs={{0,2},{2,0},{4,6},{6,4},{8,10},{10,8},{12,14},{14,12},{16,18},{18,... | collective-permute-start | bytes 147464 | tf_op jit(solution)/shard_map/ppermute | solution.py:655
  13.4 5.9 %collective-permute-start.6 = (f32[120,128]{1,0:T(8,128)S(1)}, f32[120,128]{1,0:T(8,128)S(1)}, u32[]{:S(2)}, u32[]{:S(2)}) collective-permute-start(f32[120,128]{1,0:T(8,128)S(1)} %get-tuple-element.49), channel_id=1, source_target_pairs={{0,6},{2,4},{4,2},{6,0},{8,14},{10,12},{12,10},{14,8},{16,22},{18,... | collective-permute-start | bytes 184328 | tf_op jit(solution)/shard_map/ppermute | solution.py:675
  15.3 4.5 %collective-permute-start.7 = (f32[120,128]{1,0:T(8,128)S(1)}, f32[120,128]{1,0:T(8,128)S(1)}, u32[]{:S(2)}, u32[]{:S(2)}) collective-permute-start(f32[120,128]{1,0:T(8,128)S(1)} %get-tuple-element.50), channel_id=1, source_target_pairs={{0,2},{2,6},{4,0},{6,4},{8,10},{10,14},{12,8},{14,12},{16,18},{18,... | collective-permute-start | bytes 184328 | tf_op jit(solution)/shard_map/ppermute | solution.py:675
  15.8 4.2 %collective-permute-start.8 = (f32[120,128]{1,0:T(8,128)S(1)}, f32[120,128]{1,0:T(8,128)S(1)}, u32[]{:S(2)}, u32[]{:S(2)}) collective-permute-start(f32[120,128]{1,0:T(8,128)S(1)} %get-tuple-element.51), channel_id=1, source_target_pairs={{0,4},{2,0},{4,6},{6,2},{8,12},{10,8},{12,14},{14,10},{16,20},{18,... | collective-permute-start | bytes 184328 | tf_op jit(solution)/shard_map/ppermute | solution.py:675
